TPU v7x, 32 devices: a whole 2x2x4 slice. The times are simulated.
32 devices in a mesh: grp: 8 (over z, x), band: 4 (over y, core).
Axes of the slice: x: 2, y: 2, z: 4, core: 2. Of those that a mesh axis runs over, the one named last changes fastest.
Arguments:
- patches: bfloat16 [16, 32, 32, 1152], P('grp', 'band'), may hold values from -6 to 6
- grad_out: bfloat16 [16, 32, 32, 1152], P('grp', 'band'), may hold values from -6 to 6
- cond_table: float32 [8, 1152], replicated, may hold values from -6 to 6
- group_ids: int32 [16], P('grp'), may hold values from 0 to 7
- live_count: int32 [8], P('grp'), may hold values from 1 to 2, as said below
- band_order: int32 [4], P('band'), may hold values from 0 to 3, each once
- w_ada: bfloat16 [1152, 6912], P('grp'), may hold values from -0.1875 to 0.1875
- b_ada: bfloat16 [6912], P('grp'), may hold values from -2 to 2
- w_qkv: bfloat16 [1152, 3456], P('grp'), may hold values from -0.1875 to 0.1875
- q_gain: float32 [72], replicated, may hold values from 0.25 to 1.75
- k_gain: float32 [72], replicated, may hold values from 0.25 to 1.75
- w_proj: bfloat16 [1152, 1152], P('grp'), may hold values from -0.75 to 0.75
- w_gate: bfloat16 [1152, 3072], P('grp'), may hold values from -0.1875 to 0.1875
- w_up: bfloat16 [1152, 3072], P('grp'), may hold values from -0.1875 to 0.1875
- w_down: bfloat16 [3072, 1152], P('grp'), may hold values from -0.109375 to 0.109375
Outputs:
- patches_out: bfloat16 [16, 32, 32, 1152], P('grp', 'band')
- d_patches: float32 [16, 32, 32, 1152], P('grp', 'band')
- d_cond_table: float32 [8, 1152], replicated
- d_w_ada: float32 [1152, 6912], P('grp')
- d_b_ada: float32 [6912], P('grp')
- d_w_qkv: float32 [1152, 3456], P('grp')
- d_q_gain: float32 [72], replicated
- d_k_gain: float32 [72], replicated
- d_w_proj: float32 [1152, 1152], P('grp')
- d_w_gate: float32 [1152, 3072], P('grp')
- d_w_up: float32 [1152, 3072], P('grp')
- d_w_down: float32 [3072, 1152], P('grp')
Inputs may be any that keep to these rules, and one draw needn't show every extreme that they name: `live_count`: live slots come first on each grp index; slots at or above the count are empty; at least one index has all 2 slots live.
All inputs are finite; a program needn't handle non-finite values.
Results may differ from a plain program's by a relative error of at most 0.017.
Values may be sent and summed in bfloat16 or wider, within the bound.
A program may use at most 320 MiB of HBM per device.

v0:
```python
import jax
import jax.numpy as jnp
from jax import lax
from jax.sharding import PartitionSpec as P

HEADS = 16
HDIM = 72
GROUPS = 8


EPS = 1e-06


def rms_norm(values):
    return values * lax.rsqrt(jnp.mean(values * values, axis=-1, keepdims=True) + EPS)


def rope_tables(row_index, col_index):
    quarter = HDIM // 4
    frequency = 10000.0 ** (-jnp.arange(quarter, dtype=jnp.float32) / quarter)
    row_angle = (row_index[:, None] * frequency[None, :])[:, None, :]
    col_angle = (col_index[:, None] * frequency[None, :])[:, None, :]
    return (jnp.cos(row_angle), jnp.sin(row_angle), jnp.cos(col_angle), jnp.sin(col_angle))


def rotate(tensor, tables):
    quarter = tensor.shape[-1] // 4
    cos_row, sin_row, cos_col, sin_col = tables
    part_a = tensor[..., :quarter]
    part_b = tensor[..., quarter : 2 * quarter]
    part_c = tensor[..., 2 * quarter : 3 * quarter]
    part_d = tensor[..., 3 * quarter :]
    return jnp.concatenate(
        [
            part_a * cos_row - part_b * sin_row,
            part_a * sin_row + part_b * cos_row,
            part_c * cos_col - part_d * sin_col,
            part_c * sin_col + part_d * cos_col,
        ],
        axis=-1,
    )


def modulate(values, shift_in, scale_in):
    return rms_norm(values) * (1.0 + scale_in[:, None, :]) + shift_in[:, None, :]


def swiglu(gate_in, up_in):
    return jax.nn.silu(gate_in) * up_in


def split_heads(tensor, per_block):
    count, span, heads_all, size = tensor.shape
    groups = heads_all // per_block
    shaped = tensor.reshape(count, span, groups, per_block, size)
    return jnp.transpose(shaped, (0, 2, 1, 3, 4)).reshape(count * groups, span, per_block, size)


def join_heads(tensor, count):
    blocks, span, per_block, size = tensor.shape
    groups = blocks // count
    shaped = tensor.reshape(count, groups, span, per_block, size)
    return jnp.transpose(shaped, (0, 2, 1, 3, 4)).reshape(count, span, groups * per_block, size)


def body(
    patches,
    grad_out,
    cond_table,
    group_ids,
    live_count,
    band_order,
    w_ada,
    b_ada,
    w_qkv,
    q_gain,
    k_gain,
    w_proj,
    w_gate,
    w_up,
    w_down,
):
    images, rows, cols, width = patches.shape
    length = rows * cols
    score_scale = HDIM ** (-0.5)
    per_block = 4
    gathered = (
        lax.all_gather(w_ada, "grp", axis=0, tiled=True),
        lax.all_gather(b_ada, "grp", axis=0, tiled=True),
        lax.all_gather(w_qkv, "grp", axis=0, tiled=True),
        lax.all_gather(w_proj, "grp", axis=0, tiled=True),
        lax.all_gather(w_gate, "grp", axis=0, tiled=True),
        lax.all_gather(w_up, "grp", axis=0, tiled=True),
        lax.all_gather(w_down, "grp", axis=0, tiled=True),
    )
    ada_all, bias_all, qkv_all, proj_all, gate_all, up_all, down_all = gathered
    onehot = (group_ids[:, None] == jnp.arange(GROUPS, dtype=jnp.int32)[None, :]).astype(
        jnp.float32
    )
    cond_vec = jnp.dot(
        onehot, cond_table, precision=lax.Precision.HIGHEST, preferred_element_type=jnp.float32
    )
    silu_cond, silu_pull = jax.vjp(jax.nn.silu, cond_vec)
    silu_low = silu_cond.astype(jnp.bfloat16)
    modulation = jnp.dot(silu_low, ada_all, preferred_element_type=jnp.float32) + bias_all.astype(
        jnp.float32
    )
    shift_one, scale_one, gate_one, shift_two, scale_two, gate_two = jnp.split(
        modulation, 6, axis=-1
    )
    live_mask = (jnp.arange(images, dtype=jnp.int32) < live_count[0]).astype(jnp.float32)
    row_index = jnp.repeat(band_order[0] * rows + jnp.arange(rows, dtype=jnp.int32), cols).astype(
        jnp.float32
    )
    col_index = jnp.tile(jnp.arange(cols, dtype=jnp.int32), rows).astype(jnp.float32)
    tables = rope_tables(row_index, col_index)
    x_flat = patches.reshape(images, length, width).astype(jnp.float32)
    normed_one, norm_one_pull = jax.vjp(modulate, x_flat, shift_one, scale_one)
    normed_one_low = normed_one.astype(jnp.bfloat16).reshape(images * length, width)
    qkv = jnp.dot(normed_one_low, qkv_all, preferred_element_type=jnp.float32).reshape(
        images, length, 3, HEADS, HDIM
    )

    def query_key(query_raw, key_raw, query_gain, key_gain):
        return (
            rotate(rms_norm(query_raw) * query_gain, tables),
            rotate(rms_norm(key_raw) * key_gain, tables),
        )

    (query_rot, key_rot), qk_pull = jax.vjp(query_key, qkv[:, :, 0], qkv[:, :, 1], q_gain, k_gain)
    query_low = query_rot.astype(jnp.bfloat16)
    key_low = key_rot.astype(jnp.bfloat16).reshape(images, length, width)
    value_low = qkv[:, :, 2].astype(jnp.bfloat16).reshape(images, length, width)
    kv_local = jnp.concatenate([key_low, value_low], axis=-1)
    kv_rows = lax.all_gather(kv_local, "band", axis=1, tiled=True)
    query_blocks = split_heads(query_low, per_block)
    keys_all = kv_rows[..., :width].reshape(images, -1, HEADS, HDIM)
    values_all = kv_rows[..., width:].reshape(images, -1, HEADS, HDIM)
    key_blocks = split_heads(keys_all, per_block)
    value_blocks = split_heads(values_all, per_block)

    def forward_block(item):
        query_part, key_part, value_part = item
        scores = (
            jnp.einsum("qhd,khd->hqk", query_part, key_part, preferred_element_type=jnp.float32)
            * score_scale
        )
        top_score = jnp.max(scores, axis=-1, keepdims=True)
        expo_scores = jnp.exp(scores - top_score)
        total_weight = jnp.sum(expo_scores, axis=-1, keepdims=True)
        probs_low = (expo_scores / total_weight).astype(jnp.bfloat16)
        attended_part = jnp.einsum(
            "hqk,khd->qhd", probs_low, value_part, preferred_element_type=jnp.float32
        )
        return (attended_part.astype(jnp.bfloat16), top_score + jnp.log(total_weight))

    attended_blocks, log_blocks = lax.map(forward_block, (query_blocks, key_blocks, value_blocks))
    attended_low = join_heads(attended_blocks, images).reshape(images * length, width)
    proj = jnp.dot(attended_low, proj_all, preferred_element_type=jnp.float32).reshape(
        images, length, width
    )
    middle = x_flat + gate_one[:, None, :] * proj
    normed_two, norm_two_pull = jax.vjp(modulate, middle, shift_two, scale_two)
    normed_two_low = normed_two.astype(jnp.bfloat16).reshape(images * length, width)
    gate_pre = jnp.dot(normed_two_low, gate_all, preferred_element_type=jnp.float32)
    up_pre = jnp.dot(normed_two_low, up_all, preferred_element_type=jnp.float32)
    hidden, swiglu_pull = jax.vjp(swiglu, gate_pre, up_pre)
    hidden_low = hidden.astype(jnp.bfloat16)
    mlp = jnp.dot(hidden_low, down_all, preferred_element_type=jnp.float32).reshape(
        images, length, width
    )
    output = (middle + gate_two[:, None, :] * mlp) * live_mask[:, None, None]
    patches_out = output.astype(jnp.bfloat16).reshape(images, rows, cols, width)
    gathered = (
        lax.all_gather(w_ada, "grp", axis=0, tiled=True),
        lax.all_gather(b_ada, "grp", axis=0, tiled=True),
        lax.all_gather(w_qkv, "grp", axis=0, tiled=True),
        lax.all_gather(w_proj, "grp", axis=0, tiled=True),
        lax.all_gather(w_gate, "grp", axis=0, tiled=True),
        lax.all_gather(w_up, "grp", axis=0, tiled=True),
        lax.all_gather(w_down, "grp", axis=0, tiled=True),
    )
    ada_all, bias_all, qkv_all, proj_all, gate_all, up_all, down_all = gathered
    grad_y = grad_out.reshape(images, length, width).astype(jnp.float32) * live_mask[:, None, None]
    d_gate_two = jnp.sum(grad_y * mlp, axis=1)
    d_mlp = (grad_y * gate_two[:, None, :]).astype(jnp.bfloat16).reshape(images * length, width)
    d_w_down = jnp.einsum("tf,td->fd", hidden_low, d_mlp, preferred_element_type=jnp.float32)
    d_hidden = jnp.einsum("td,fd->tf", d_mlp, down_all, preferred_element_type=jnp.float32)
    d_gate_pre, d_up_pre = swiglu_pull(d_hidden)
    d_gate_low = d_gate_pre.astype(jnp.bfloat16)
    d_up_low = d_up_pre.astype(jnp.bfloat16)
    d_w_gate = jnp.einsum(
        "td,tf->df", normed_two_low, d_gate_low, preferred_element_type=jnp.float32
    )
    d_w_up = jnp.einsum("td,tf->df", normed_two_low, d_up_low, preferred_element_type=jnp.float32)
    d_normed_two = jnp.einsum("tf,df->td", d_gate_low, gate_all, preferred_element_type=jnp.float32)
    d_normed_two = d_normed_two + jnp.einsum(
        "tf,df->td", d_up_low, up_all, preferred_element_type=jnp.float32
    )
    d_middle_norm, d_shift_two, d_scale_two = norm_two_pull(
        d_normed_two.reshape(images, length, width)
    )
    d_middle = grad_y + d_middle_norm
    d_gate_one = jnp.sum(d_middle * proj, axis=1)
    d_proj = (d_middle * gate_one[:, None, :]).astype(jnp.bfloat16).reshape(images * length, width)
    d_w_proj = jnp.einsum("td,te->de", attended_low, d_proj, preferred_element_type=jnp.float32)
    d_attended = jnp.einsum("te,de->td", d_proj, proj_all, preferred_element_type=jnp.float32)
    d_attended = d_attended.astype(jnp.bfloat16).reshape(images, length, HEADS, HDIM)
    d_att_blocks = split_heads(d_attended, per_block)

    def backward_block(item):
        query_part, key_part, value_part, d_att_part, log_part = item
        scores = (
            jnp.einsum("qhd,khd->hqk", query_part, key_part, preferred_element_type=jnp.float32)
            * score_scale
        )
        probs = jnp.exp(scores - log_part)
        probs_low = probs.astype(jnp.bfloat16)
        d_probs = jnp.einsum(
            "qhd,khd->hqk", d_att_part, value_part, preferred_element_type=jnp.float32
        )
        row_delta = jnp.sum(probs * d_probs, axis=-1, keepdims=True)
        d_scores = (probs * (d_probs - row_delta)).astype(jnp.bfloat16)
        d_query_part = (
            jnp.einsum("hqk,khd->qhd", d_scores, key_part, preferred_element_type=jnp.float32)
            * score_scale
        )
        key_grad = (
            jnp.einsum("hqk,qhd->khd", d_scores, query_part, preferred_element_type=jnp.float32)
            * score_scale
        )
        value_grad = jnp.einsum(
            "hqk,qhd->khd", probs_low, d_att_part, preferred_element_type=jnp.float32
        )
        return (d_query_part, key_grad, value_grad)

    query_grads, key_grads, value_grads = lax.map(
        backward_block, (query_blocks, key_blocks, value_blocks, d_att_blocks, log_blocks)
    )
    d_query = join_heads(query_grads, images)
    key_terms = join_heads(key_grads, images).reshape(images, -1, width)
    value_terms = join_heads(value_grads, images).reshape(images, -1, width)
    kv_terms = jnp.concatenate([key_terms, value_terms], axis=-1)
    kv_grad = lax.psum_scatter(
        kv_terms.astype(jnp.bfloat16), "band", scatter_dimension=1, tiled=True
    ).astype(jnp.float32)
    d_key = kv_grad[..., :width].reshape(images, length, HEADS, HDIM)
    d_value = kv_grad[..., width:]
    d_query_raw, d_key_raw, d_q_gain, d_k_gain = qk_pull((d_query, d_key))
    d_qkv = jnp.concatenate(
        [
            d_query_raw.reshape(images, length, width),
            d_key_raw.reshape(images, length, width),
            d_value,
        ],
        axis=-1,
    )
    d_qkv = d_qkv.astype(jnp.bfloat16).reshape(images * length, 3 * width)
    d_w_qkv = jnp.einsum("td,te->de", normed_one_low, d_qkv, preferred_element_type=jnp.float32)
    d_normed_one = jnp.einsum("te,de->td", d_qkv, qkv_all, preferred_element_type=jnp.float32)
    d_x_norm, d_shift_one, d_scale_one = norm_one_pull(d_normed_one.reshape(images, length, width))
    d_patches = (d_middle + d_x_norm).reshape(images, rows, cols, width)
    d_mod_part = jnp.concatenate(
        [d_shift_one, d_scale_one, d_gate_one, d_shift_two, d_scale_two, d_gate_two], axis=-1
    )
    d_modulation = lax.psum(d_mod_part, "band").astype(jnp.bfloat16)
    d_w_ada = jnp.einsum("bd,be->de", silu_low, d_modulation, preferred_element_type=jnp.float32)
    d_b_ada = jnp.sum(d_modulation.astype(jnp.float32), axis=0)
    d_silu = jnp.einsum("be,de->bd", d_modulation, ada_all, preferred_element_type=jnp.float32)
    d_cond_vec = silu_pull(d_silu)[0]
    d_cond_part = jnp.dot(
        onehot.T, d_cond_vec, precision=lax.Precision.HIGHEST, preferred_element_type=jnp.float32
    )
    shards = (
        lax.psum_scatter(d_w_ada, "grp", scatter_dimension=0, tiled=True),
        lax.psum_scatter(d_b_ada, "grp", scatter_dimension=0, tiled=True),
        lax.psum_scatter(d_w_qkv, "grp", scatter_dimension=0, tiled=True),
        lax.psum_scatter(d_w_proj, "grp", scatter_dimension=0, tiled=True),
        lax.psum_scatter(d_w_gate, "grp", scatter_dimension=0, tiled=True),
        lax.psum_scatter(d_w_up, "grp", scatter_dimension=0, tiled=True),
        lax.psum_scatter(d_w_down, "grp", scatter_dimension=0, tiled=True),
    )
    banded = (
        lax.psum(shards[2].astype(jnp.bfloat16), "band").astype(jnp.float32),
        lax.psum(shards[3].astype(jnp.bfloat16), "band").astype(jnp.float32),
        lax.psum(shards[4].astype(jnp.bfloat16), "band").astype(jnp.float32),
        lax.psum(shards[5].astype(jnp.bfloat16), "band").astype(jnp.float32),
        lax.psum(shards[6].astype(jnp.bfloat16), "band").astype(jnp.float32),
        lax.psum(d_q_gain.astype(jnp.bfloat16), "band").astype(jnp.float32),
        lax.psum(d_k_gain.astype(jnp.bfloat16), "band").astype(jnp.float32),
    )
    group_total = lax.psum((d_cond_part, banded[5], banded[6]), "grp")
    return (
        patches_out,
        d_patches,
        group_total[0],
        shards[0],
        shards[1],
        banded[0],
        group_total[1],
        group_total[2],
        banded[1],
        banded[2],
        banded[3],
        banded[4],
    )


def solution(mesh):
    in_specs = (
        P("grp", "band", None, None),
        P("grp", "band", None, None),
        P(),
        P("grp"),
        P("grp"),
        P("band"),
        P("grp", None),
        P("grp"),
        P("grp", None),
        P(),
        P(),
        P("grp", None),
        P("grp", None),
        P("grp", None),
        P("grp", None),
    )
    out_specs = (
        P("grp", "band", None, None),
        P("grp", "band", None, None),
        P(),
        P("grp", None),
        P("grp"),
        P("grp", None),
        P(),
        P(),
        P("grp", None),
        P("grp", None),
        P("grp", None),
        P("grp", None),
    )
    return jax.shard_map(body, mesh=mesh, in_specs=in_specs, out_specs=out_specs, check_vma=False)
```

profile of v0, /device:TPU:0, one launch (start us, length us, event | category | flops | bytes accessed | tf_op | source)
XLA Modules:
  0.0 2747.7 jit_solution(16294332230577527738)
XLA Ops:
  10.3 39.6 %all-reduce.8 = bf16[6912]{0:T(1024)(128)(2,1)S(1)} all-reduce(bf16[6912]{0:T(1024)(128)(2,1)S(1)} %dynamic-update-slice), channel_id=1, replica_groups=mesh['grp'=8,'band'=4] {'grp'}, use_global_device_ids=true, to_apply=%add.8 | all-reduce | flops 6912 | bytes 27648
  52.2 81.0 %all-gather.10.cloned.1.call-done = bf16[1152,3456]{1,0:T(8,128)(2,1)} async-done(((bf16[144,3456]{1,0:T(8,128)(2,1)}), bf16[1152,3456]{1,0:T(8,128)(2,1)}) %all-gather.10.cloned.1.call-update) | async-done | bytes 7962640 | tf_op jit(solution)/shard_map/all_gather | solution.py:90
  133.2 11.7 copy.81
  145.0 205.9 %all-gather.8.cloned.1.call-done = bf16[1152,6912]{1,0:T(8,128)(2,1)} async-done(((bf16[144,6912]{1,0:T(8,128)(2,1)}), bf16[1152,6912]{1,0:T(8,128)(2,1)}) %all-gather.8.cloned.1.call-update) | async-done | bytes 15925264 | tf_op jit(solution)/shard_map/all_gather | solution.py:88
  350.8 7.8 convolution_add_fusion
  359.2 4.8 fusion.102
  379.6 54.5 %all-gather.12.cloned.1.call-done = bf16[2,1024,2304]{1,2,0:T(8,128)(2,1)} async-done(((bf16[2,256,2304]{1,2,0:T(8,128)(2,1)}), bf16[2,1024,2304]{1,2,0:T(8,128)(2,1)}) %all-gather.12.cloned.1.call-update) | async-done | bytes 9437200 | tf_op jit(solution)/shard_map/all_gather | solution.py:135
  434.1 8.5 fusion.98
  442.6 41.0 %while.26 = (s32[]{:T(128)}, bf16[8,256,4,72]{1,3,2,0:T(8,128)(2,1)S(1)}, f32[8,4,256,1]{2,1,3,0:T(4,128)S(1)}, bf16[8,1024,4,72]{1,3,2,0:T(8,128)(2,1)}, bf16[8...) while((s32[]{:T(128)}, bf16[8,256,4,72]{1,3,2,0:T(8,128)(2,1)S(1)}, ...), condition=%wide.region_6.7_spmd, body=%wide.region_3.6_spmd.sunk | while | flops 311499776 | bytes 14092377 | solution.py:157
  483.6 7.5 all-gather.14.cloned.1.call-done
  491.1 6.0 multiply_reduce_fusion.9
  498.5 102.1 %all-gather.16.cloned.1.call-done = bf16[1152,3072]{1,0:T(8,128)(2,1)} async-done(((bf16[144,3072]{1,0:T(8,128)(2,1)}), bf16[1152,3072]{1,0:T(8,128)(2,1)}) %all-gather.16.cloned.1.call-update) | async-done | bytes 7077904 | tf_op jit(solution)/shard_map/all_gather | solution.py:92
  600.6 10.3 fusion.103
  610.9 98.8 %all-gather.18.cloned.1.call-done = bf16[1152,3072]{1,0:T(8,128)(2,1)} async-done(((bf16[144,3072]{1,0:T(8,128)(2,1)}), bf16[1152,3072]{1,0:T(8,128)(2,1)}) %all-gather.18.cloned.1.call-update) | async-done | bytes 7077904 | tf_op jit(solution)/shard_map/all_gather | solution.py:93
  709.7 10.3 fusion.104
  720.0 98.9 %all-gather.20.cloned.1.call-done = bf16[3072,1152]{1,0:T(8,128)(2,1)} async-done(((bf16[384,1152]{1,0:T(8,128)(2,1)}), bf16[3072,1152]{1,0:T(8,128)(2,1)}) %all-gather.20.cloned.1.call-update) | async-done | bytes 7077904 | tf_op jit(solution)/shard_map/all_gather | solution.py:94
  818.9 12.7 multiply_convert_fusion.1
  831.5 10.6 fusion.106
  842.2 6.2 convolution_add_fusion.1
  850.3 4.3 fusion.105
  862.7 97.0 %while.27 = (s32[]{:T(128)}, f32[8,256,4,72]{1,3,2,0:T(8,128)}, bf16[8,1024,4,72]{1,3,2,0:T(8,128)(2,1)}, bf16[8,1024,4,72]{1,3,2,0:T(8,128)(2,1)}, bf16[8,1024,...) while((s32[]{:T(128)}, f32[8,256,4,72]{1,3,2,0:T(8,128)}, ...), condition=%wide.region_11.12_spmd, body=%wide.region_9.11_spmd.sunk | while | flops 767925248 | bytes 36504688 | solution.py:237
  959.7 6.7 copy.90
  966.5 6.7 copy.89
  973.2 9.0 pad_maximum_fusion
  984.9 4.4 fusion.107
  990.9 9.9 fusion.108
  1000.9 9.0 fusion.109
  1011.2 10.1 fusion.110
  1024.8 34.2 %reduce-scatter.8.cloned.1.call-done = bf16[2,256,2304]{2,1,0:T(8,128)(2,1)} async-done(((bf16[2,1024,2304]{2,1,0:T(8,128)(2,1)}), bf16[2,256,2304]{2,1,0:T(8,128)(2,1)}) %reduce-scatter.8.cloned.1.call-update) | async-done | bytes 2359312 | tf_op jit(solution)/shard_map/reduce_scatter | solution.py:244
  1059.0 3.7 slice_convert_fusion.1
  1066.1 4.4 multiply_reduce_fusion.3
  1070.6 3.2 fusion.61
  1078.0 10.7 fusion.68
  1088.8 8.2 convolution_bitcast_fusion
  1097.1 69.7 %reduce-scatter.14.cloned.1.call-done = f32[144,1152]{1,0:T(8,128)} async-done(((f32[1152,1152]{1,0:T(8,128)}), f32[144,1152]{1,0:T(8,128)}) %reduce-scatter.14.cloned.1.call-update) | async-done | bytes 663568 | tf_op jit(solution)/shard_map/reduce_scatter | solution.py:278
  1168.6 231.0 %reduce-scatter.16.cloned.1.call-done = f32[144,3072]{1,0:T(8,128)} async-done(((f32[1152,3072]{1,0:T(8,128)}), f32[144,3072]{1,0:T(8,128)}) %reduce-scatter.16.cloned.1.call-update) | async-done | bytes 1769488 | tf_op jit(solution)/shard_map/reduce_scatter | solution.py:279
  1402.1 229.9 %reduce-scatter.18.cloned.1.call-done = f32[144,3072]{1,0:T(8,128)} async-done(((f32[1152,3072]{1,0:T(8,128)}), f32[144,3072]{1,0:T(8,128)}) %reduce-scatter.18.cloned.1.call-update) | async-done | bytes 1769488 | tf_op jit(solution)/shard_map/reduce_scatter | solution.py:280
  1634.6 229.8 %reduce-scatter.20.cloned.1.call-done = f32[384,1152]{1,0:T(8,128)} async-done(((f32[3072,1152]{1,0:T(8,128)}), f32[384,1152]{1,0:T(8,128)}) %reduce-scatter.20.cloned.1.call-update) | async-done | bytes 1769488 | tf_op jit(solution)/shard_map/reduce_scatter | solution.py:281
  1866.8 270.3 %reduce-scatter.12.cloned.1.call-done = f32[144,3456]{1,0:T(8,128)} async-done(((f32[1152,3456]{1,0:T(8,128)}), f32[144,3456]{1,0:T(8,128)}) %reduce-scatter.12.cloned.1.call-update) | async-done | bytes 1990672 | tf_op jit(solution)/shard_map/reduce_scatter | solution.py:277
  2137.2 2.6 convert_element_type.270
  2140.5 13.0 psum.77
  2153.5 12.8 fusion.91
  2167.0 6.5 all-reduce.11
  2173.5 10.0 fusion.111
  2183.9 36.3 %all-reduce.10 = (f32[8,1152]{1,0:T(8,128)}, f32[6912]{0:T(1024)S(1)}, f32[72]{0:T(128)}, f32[72]{0:T(128)}) all-reduce(f32[8,1152]{1,0:T(8,128)S(1)} %fusion.80, f32[6912]{0:T(1024)S(1)} %convert_reduce_fusion, bf16[72]{0:T(256)(128)(2,1)S(1)} %get-tuple-element.205, ...), channel_id=1, replica_groups=mesh['grp'=8,'band'=4] {'grp'}, use_global_device_ids=true, to_apply=%region_23.24 | all-reduce | flops 16272 | bytes 129888 | tf_op jit(solution)/shard_map/psum | solution.py:292
  2220.8 4.1 fusion.63
  2224.9 2.7 convert_element_type.271
  2232.6 508.1 %reduce-scatter.10.cloned.1.call-done = f32[144,6912]{1,0:T(8,128)} async-done(((f32[1152,6912]{1,0:T(8,128)}), f32[144,6912]{1,0:T(8,128)}) %reduce-scatter.10.cloned.1.call-update) | async-done | bytes 3981328 | tf_op jit(solution)/shard_map/reduce_scatter | solution.py:275
  (341 shorter events, 200.5 us)
Async XLA Ops:
  7.2 44.5 %copy-start = (f32[8,1152]{1,0:T(8,128)S(1)}, f32[8,1152]{1,0:T(8,128)}, u32[]{:S(2)}) copy-start(f32[8,1152]{1,0:T(8,128)} %param.21) | copy-start | bytes 110596
  7.2 43.6 %copy-start.5 = (bf16[2,8,32,1152]{3,2,1,0:T(8,128)(2,1)S(1)}, bf16[2,8,32,1152]{3,2,1,0:T(8,128)(2,1)}, u32[]{:S(2)}) copy-start(bf16[2,8,32,1152]{3,2,1,0:T(8,128)(2,1)} %param.19) | copy-start | bytes 3538948
  7.2 44.5 %copy-start.62 = (s32[2]{0:T(128)S(1)}, s32[2]{0:T(128)}, u32[]{:S(2)}) copy-start(s32[2]{0:T(128)} %param.22) | copy-start | bytes 28
  7.2 126.0 %all-gather.10.cloned.1.call-start = ((), (), s32[]{:S(2)}) async-start(), calls=%async_computation.8 | async-start | bytes 8957952 | tf_op jit(solution)/shard_map/all_gather | solution.py:90
  8.0 342.9 %all-gather.8.cloned.1.call-start = ((), (), s32[]{:S(2)}) async-start(), calls=%async_computation.7 | async-start | bytes 17915904 | tf_op jit(solution)/shard_map/all_gather | solution.py:88
  8.7 425.3 %all-gather.12.cloned.1.call-start = ((), (), s32[]{:S(2)}) async-start(), calls=%async_computation.9 | async-start | bytes 11796480 | tf_op jit(solution)/shard_map/all_gather | solution.py:135
  51.9 299.0 %copy-start.48 = (f32[2,1152]{1,0:T(2,128)}, f32[2,1152]{1,0:T(2,128)S(1)}, u32[]{:S(2)}) copy-start(f32[2,1152]{1,0:T(2,128)S(1)} %fusion.86) | copy-start | bytes 27652
  52.2 321.4 %copy-start.29 = (f32[256,18]{0,1:T(8,128)}, f32[256,18]{0,1:T(8,128)S(1)}, u32[]{:S(2)}) copy-start(f32[256,18]{0,1:T(8,128)S(1)} %get-tuple-element.272) | copy-start | bytes 55300
  52.2 321.4 %copy-start.31 = (f32[256,18]{0,1:T(8,128)}, f32[256,18]{0,1:T(8,128)S(1)}, u32[]{:S(2)}) copy-start(f32[256,18]{0,1:T(8,128)S(1)} %get-tuple-element.273) | copy-start | bytes 55300
  52.2 321.4 %copy-start.33 = (f32[256,18]{0,1:T(8,128)}, f32[256,18]{0,1:T(8,128)S(1)}, u32[]{:S(2)}) copy-start(f32[256,18]{0,1:T(8,128)S(1)} %get-tuple-element.278) | copy-start | bytes 55300
  52.2 321.3 %copy-start.35 = (f32[256,18]{0,1:T(8,128)}, f32[256,18]{0,1:T(8,128)S(1)}, u32[]{:S(2)}) copy-start(f32[256,18]{0,1:T(8,128)S(1)} %get-tuple-element.279) | copy-start | bytes 55300
  350.8 8.3 copy-start.9
  358.7 5.3 copy-start.46
  358.7 5.3 copy-start.50
  370.2 120.9 %all-gather.14.cloned.1.call-start = ((), (), s32[]{:S(2)}) async-start(), calls=%async_computation.10 | async-start | bytes 2985984 | tf_op jit(solution)/shard_map/all_gather | solution.py:91
  370.8 229.8 %all-gather.16.cloned.1.call-start = ((), (), s32[]{:S(2)}) async-start(), calls=%async_computation.11 | async-start | bytes 7962624 | tf_op jit(solution)/shard_map/all_gather | solution.py:92
  371.4 338.3 %all-gather.18.cloned.1.call-start = ((), (), s32[]{:S(2)}) async-start(), calls=%async_computation.12 | async-start | bytes 7962624 | tf_op jit(solution)/shard_map/all_gather | solution.py:93
  372.0 446.9 %all-gather.20.cloned.1.call-start = ((), (), s32[]{:S(2)}) async-start(), calls=%async_computation.13 | async-start | bytes 7962624 | tf_op jit(solution)/shard_map/all_gather | solution.py:94
  372.7 686.3 %reduce-scatter.8.cloned.1.call-start = ((), (), s32[]{:S(2)}) async-start(), calls=%async_computation.14 | async-start | bytes 11796480 | tf_op jit(solution)/shard_map/reduce_scatter | solution.py:244
  379.6 63.0 %copy-start.13 = (bf16[8,256,4,72]{1,3,2,0:T(8,128)(2,1)S(1)}, bf16[8,256,4,72]{1,3,2,0:T(8,128)(2,1)}, u32[]{:S(2)}) copy-start(bf16[8,256,4,72]{1,3,2,0:T(8,128)(2,1)} %custom-call.1) | copy-start | bytes 3538948
  483.6 7.5 copy-start.7
  483.6 7.5 copy-start.14
  831.5 10.7 copy-start.65
  831.5 10.7 copy-start.64
  831.5 10.7 copy-start.61
  831.5 18.2 slice-start.2
  842.2 7.5 slice-start.3
  850.3 4.3 copy-start.8
  850.3 4.3 copy-start.19
  982.2 184.5 %reduce-scatter.14.cloned.1.call-start = ((), (), s32[]{:S(2)}) async-start(), calls=%async_computation.17 | async-start | bytes 5971968 | tf_op jit(solution)/shard_map/reduce_scatter | solution.py:278
  989.4 410.3 %reduce-scatter.16.cloned.1.call-start = ((), (), s32[]{:S(2)}) async-start(), calls=%async_computation.18 | async-start | bytes 15925248 | tf_op jit(solution)/shard_map/reduce_scatter | solution.py:279
  1000.9 631.2 %reduce-scatter.18.cloned.1.call-start = ((), (), s32[]{:S(2)}) async-start(), calls=%async_computation.19 | async-start | bytes 15925248 | tf_op jit(solution)/shard_map/reduce_scatter | solution.py:280
  1010.0 854.4 %reduce-scatter.20.cloned.1.call-start = ((), (), s32[]{:S(2)}) async-start(), calls=%async_computation.20 | async-start | bytes 15925248 | tf_op jit(solution)/shard_map/reduce_scatter | solution.py:281
  1021.4 1115.8 %reduce-scatter.12.cloned.1.call-start = ((), (), s32[]{:S(2)}) async-start(), calls=%async_computation.16 | async-start | bytes 17915904 | tf_op jit(solution)/shard_map/reduce_scatter | solution.py:277
  1064.7 5.9 slice-start
  1066.0 4.5 copy-start.43
  1066.1 4.5 copy-start.45
  1066.1 4.5 slice-start.1
  1066.1 4.5 copy-start.12
  1078.0 10.8 copy-start.16
  1078.0 10.8 copy-start.17
  1097.0 71.6 %copy-start.53 = (f32[2,1152]{1,0:T(2,128)S(1)}, f32[2,1152]{1,0:T(2,128)}, u32[]{:S(2)}) copy-start(f32[2,1152]{1,0:T(2,128)} %get-tuple-element.169) | copy-start | bytes 27652
  1097.0 1127.9 %all-reduce.15.cloned.1.call-start = ((), (), s32[]{:S(2)}) async-start(), calls=%async_computation.21 | async-start | bytes 7962624 | tf_op jit(solution)/shard_map/psum | solution.py:284
  2139.8 13.7 copy-start.49
  2139.8 600.9 %reduce-scatter.10.cloned.1.call-start = ((), (), s32[]{:S(2)}) async-start(), calls=%async_computation.15 | async-start | bytes 35831808 | tf_op jit(solution)/shard_map/reduce_scatter | solution.py:275
  2173.5 10.0 copy-start.63
  2173.5 47.3 %copy-start.4 = (f32[2,256,1152]{2,1,0:T(8,128)S(1)}, f32[2,256,1152]{2,1,0:T(8,128)}, u32[]{:S(2)}) copy-start(f32[2,256,1152]{2,1,0:T(8,128)} %copy-done.3) | copy-start | bytes 7077892
  2229.9 510.8 %copy-start.1 = (f32[8,1152]{1,0:T(8,128)S(1)}, f32[8,1152]{1,0:T(8,128)}, u32[]{:S(2)}) copy-start(f32[8,1152]{1,0:T(8,128)} %param.21) | copy-start | bytes 110596
  (38 other events, 74.4 us)
Sparse Core Ops, SparseCore 0:
  10.3 122.9 all-gather.9
  135.4 215.3 all-gather.7
  370.3 63.6 all-gather.11
  436.1 55.0 all-gather.13
  493.2 107.3 all-gather.15
  602.6 106.9 all-gather.17
  711.8 106.9 all-gather.19
  982.3 76.5 reduce-scatter.7
  1062.6 104.1 reduce-scatter.13
  1170.7 228.9 reduce-scatter.15
  1403.7 228.2 reduce-scatter.17
  1636.0 228.2 reduce-scatter.19
  1868.7 268.3 reduce-scatter.11
  2141.1 82.5 all-reduce.14
  2228.0 512.6 reduce-scatter.9
where the time goes:
time: 2760 us; the launch traced here: 2750 us
  waiting for transfers between devices  2230 us (81%)
  matrix products  271 us (10%)
  blocking collectives  95.4 us (3%)
  other arithmetic  76.5 us (3%)
  local copies, waits for them, and re-layouts  60.1 us (2%)
    reduce_scatter x1, waiting for transfers between devices, body(): lax.psum_scatter(d_w_ada, 'grp', scatter_dimension=0, tiled=True)  508 us
    reduce_scatter x1, waiting for transfers between devices, body(): lax.psum_scatter(d_w_qkv, 'grp', scatter_dimension=0, tiled=True)  270 us
    reduce_scatter x1, waiting for transfers between devices, body(): lax.psum_scatter(d_w_gate, 'grp', scatter_dimension=0, tiled=True)  231 us
    reduce_scatter x1, waiting for transfers between devices, body(): lax.psum_scatter(d_w_up, 'grp', scatter_dimension=0, tiled=True)  230 us
    reduce_scatter x1, waiting for transfers between devices, body(): lax.psum_scatter(d_w_down, 'grp', scatter_dimension=0, tiled=True)  230 us
    all_gather x1, waiting for transfers between devices, body(): lax.all_gather(w_ada, 'grp', axis=0, tiled=True)  206 us
    all_gather x1, waiting for transfers between devices, body(): lax.all_gather(w_gate, 'grp', axis=0, tiled=True)  102 us
    all_gather x1, waiting for transfers between devices, body(): lax.all_gather(w_down, 'grp', axis=0, tiled=True)  98.9 us
  transfers between devices with their start and end apart: 15, of which 14 were waited for; matrix products, arithmetic and copies ran while one was open for 8% of the time, Pallas kernels for 0%

commit v1 on v0

--- a/solution.py
+++ b/solution.py
@@ -84,27 +84,29 @@
     length = rows * cols
     score_scale = HDIM ** (-0.5)
     per_block = 4
-    gathered = (
-        lax.all_gather(w_ada, "grp", axis=0, tiled=True),
-        lax.all_gather(b_ada, "grp", axis=0, tiled=True),
-        lax.all_gather(w_qkv, "grp", axis=0, tiled=True),
-        lax.all_gather(w_proj, "grp", axis=0, tiled=True),
-        lax.all_gather(w_gate, "grp", axis=0, tiled=True),
-        lax.all_gather(w_up, "grp", axis=0, tiled=True),
-        lax.all_gather(w_down, "grp", axis=0, tiled=True),
-    )
-    ada_all, bias_all, qkv_all, proj_all, gate_all, up_all, down_all = gathered
+    grp = lax.axis_index("grp")
+    ada_rows = w_ada.shape[0]
+    bias_cols = b_ada.shape[0]
+    qkv_all = lax.all_gather(w_qkv, "grp", axis=0, tiled=True)
+    proj_all = lax.all_gather(w_proj, "grp", axis=0, tiled=True)
+    gate_all = lax.all_gather(w_gate, "grp", axis=0, tiled=True)
+    up_all = lax.all_gather(w_up, "grp", axis=0, tiled=True)
+    down_all = lax.all_gather(w_down, "grp", axis=0, tiled=True)
     onehot = (group_ids[:, None] == jnp.arange(GROUPS, dtype=jnp.int32)[None, :]).astype(
         jnp.float32
     )
-    cond_vec = jnp.dot(
-        onehot, cond_table, precision=lax.Precision.HIGHEST, preferred_element_type=jnp.float32
-    )
-    silu_cond, silu_pull = jax.vjp(jax.nn.silu, cond_vec)
-    silu_low = silu_cond.astype(jnp.bfloat16)
-    modulation = jnp.dot(silu_low, ada_all, preferred_element_type=jnp.float32) + bias_all.astype(
-        jnp.float32
-    )
+    cond_rows = lax.dynamic_slice_in_dim(cond_table, grp * ada_rows, ada_rows, axis=1)
+    silu_rows, silu_pull = jax.vjp(jax.nn.silu, cond_rows)
+    silu_rows = silu_rows.astype(jnp.bfloat16)
+    mod_part = jnp.dot(silu_rows, w_ada, preferred_element_type=jnp.float32)
+    bias_part = lax.dynamic_update_slice_in_dim(
+        jnp.zeros((mod_part.shape[1],), jnp.float32),
+        b_ada.astype(jnp.float32),
+        grp * bias_cols,
+        axis=0,
+    )
+    mod_table = lax.psum(mod_part + bias_part[None, :], "grp")
+    modulation = jnp.take(mod_table, group_ids, axis=0)
     shift_one, scale_one, gate_one, shift_two, scale_two, gate_two = jnp.split(
         modulation, 6, axis=-1
     )
@@ -171,16 +173,6 @@
     )
     output = (middle + gate_two[:, None, :] * mlp) * live_mask[:, None, None]
     patches_out = output.astype(jnp.bfloat16).reshape(images, rows, cols, width)
-    gathered = (
-        lax.all_gather(w_ada, "grp", axis=0, tiled=True),
-        lax.all_gather(b_ada, "grp", axis=0, tiled=True),
-        lax.all_gather(w_qkv, "grp", axis=0, tiled=True),
-        lax.all_gather(w_proj, "grp", axis=0, tiled=True),
-        lax.all_gather(w_gate, "grp", axis=0, tiled=True),
-        lax.all_gather(w_up, "grp", axis=0, tiled=True),
-        lax.all_gather(w_down, "grp", axis=0, tiled=True),
-    )
-    ada_all, bias_all, qkv_all, proj_all, gate_all, up_all, down_all = gathered
     grad_y = grad_out.reshape(images, length, width).astype(jnp.float32) * live_mask[:, None, None]
     d_gate_two = jnp.sum(grad_y * mlp, axis=1)
     d_mlp = (grad_y * gate_two[:, None, :]).astype(jnp.bfloat16).reshape(images * length, width)
@@ -264,45 +256,47 @@
         [d_shift_one, d_scale_one, d_gate_one, d_shift_two, d_scale_two, d_gate_two], axis=-1
     )
     d_modulation = lax.psum(d_mod_part, "band").astype(jnp.bfloat16)
-    d_w_ada = jnp.einsum("bd,be->de", silu_low, d_modulation, preferred_element_type=jnp.float32)
-    d_b_ada = jnp.sum(d_modulation.astype(jnp.float32), axis=0)
-    d_silu = jnp.einsum("be,de->bd", d_modulation, ada_all, preferred_element_type=jnp.float32)
-    d_cond_vec = silu_pull(d_silu)[0]
-    d_cond_part = jnp.dot(
-        onehot.T, d_cond_vec, precision=lax.Precision.HIGHEST, preferred_element_type=jnp.float32
-    )
-    shards = (
-        lax.psum_scatter(d_w_ada, "grp", scatter_dimension=0, tiled=True),
-        lax.psum_scatter(d_b_ada, "grp", scatter_dimension=0, tiled=True),
-        lax.psum_scatter(d_w_qkv, "grp", scatter_dimension=0, tiled=True),
-        lax.psum_scatter(d_w_proj, "grp", scatter_dimension=0, tiled=True),
-        lax.psum_scatter(d_w_gate, "grp", scatter_dimension=0, tiled=True),
-        lax.psum_scatter(d_w_up, "grp", scatter_dimension=0, tiled=True),
-        lax.psum_scatter(d_w_down, "grp", scatter_dimension=0, tiled=True),
-    )
-    banded = (
-        lax.psum(shards[2].astype(jnp.bfloat16), "band").astype(jnp.float32),
-        lax.psum(shards[3].astype(jnp.bfloat16), "band").astype(jnp.float32),
-        lax.psum(shards[4].astype(jnp.bfloat16), "band").astype(jnp.float32),
-        lax.psum(shards[5].astype(jnp.bfloat16), "band").astype(jnp.float32),
-        lax.psum(shards[6].astype(jnp.bfloat16), "band").astype(jnp.float32),
-        lax.psum(d_q_gain.astype(jnp.bfloat16), "band").astype(jnp.float32),
-        lax.psum(d_k_gain.astype(jnp.bfloat16), "band").astype(jnp.float32),
-    )
-    group_total = lax.psum((d_cond_part, banded[5], banded[6]), "grp")
+    payload = jnp.concatenate([d_modulation, onehot.astype(jnp.bfloat16)], axis=-1)
+    payload = lax.all_gather(payload, "grp", axis=0, tiled=True)
+    d_mod_all = payload[:, : d_modulation.shape[1]]
+    onehot_all = payload[:, d_modulation.shape[1] :]
+    silu_all = jnp.dot(onehot_all, silu_rows, preferred_element_type=jnp.float32).astype(
+        jnp.bfloat16
+    )
+    d_w_ada = jnp.einsum("bd,be->de", silu_all, d_mod_all, preferred_element_type=jnp.float32)
+    d_b_ada = lax.dynamic_slice_in_dim(
+        jnp.sum(d_mod_all.astype(jnp.float32), axis=0), grp * bias_cols, bias_cols, axis=0
+    )
+    d_silu = jnp.einsum("be,de->bd", d_mod_all, w_ada, preferred_element_type=jnp.float32)
+    d_silu = jnp.dot(
+        onehot_all.astype(jnp.float32).T,
+        d_silu,
+        precision=lax.Precision.HIGHEST,
+        preferred_element_type=jnp.float32,
+    )
+    d_cond_rows = silu_pull(d_silu)[0]
+    d_cond = lax.all_gather(d_cond_rows, "grp", axis=1, tiled=True)
+    d_q_gain, d_k_gain = lax.psum((d_q_gain, d_k_gain), ("grp", "band"))
+
+    def spread(grad):
+        shard = lax.psum_scatter(
+            grad.astype(jnp.bfloat16), "grp", scatter_dimension=0, tiled=True
+        )
+        return lax.psum(shard, "band").astype(jnp.float32)
+
     return (
         patches_out,
         d_patches,
-        group_total[0],
-        shards[0],
-        shards[1],
-        banded[0],
-        group_total[1],
-        group_total[2],
-        banded[1],
-        banded[2],
-        banded[3],
-        banded[4],
+        d_cond,
+        d_w_ada,
+        d_b_ada,
+        spread(d_w_qkv),
+        d_q_gain,
+        d_k_gain,
+        spread(d_w_proj),
+        spread(d_w_gate),
+        spread(d_w_up),
+        spread(d_w_down),
     )
 
 

time: 2760 us -> 1680 us (0.61)
  waiting for transfers between devices: 2230 us -> 1140 us
    reduce_scatter x6 -> x5, waiting for transfers between devices: 1540 us -> 564 us  [spread(): lax.psum_scatter(grad.astype(jnp.bfloat16), 'grp', scatter_dimension=0, t...]
    all_gather x6 -> x5, waiting for transfers between devices: 594 us -> 421 us  [the longest x1 118 us: body(): qkv_all = lax.all_gather(w_qkv, 'grp', axis=0, tiled=True)]
    psum x1 -> x2, waiting for transfers between devices: 0.01 us -> 71.5 us  [the longest x1 71.5 us: body(): mod_table = lax.psum(mod_part + bias_part[None, :], 'grp')]
    all_gather x0 -> x2, blocking collectives: none -> 63.2 us  [the longest x1 32.7 us: body(): payload = lax.all_gather(payload, 'grp', axis=0, tiled=True)]
    unnamed x1 -> x0, blocking collectives: 39.6 us -> none
  transfers between devices with their start and end apart: 15 -> 14, of which waited for: 14 -> 13; matrix products, arithmetic and copies ran while one was open for 8% -> 11% of each run, Pallas kernels for 0% -> 0%
where the time goes in v1:
time: 1680 us
  waiting for transfers between devices  1140 us (68%)
  matrix products  258 us (15%)
  blocking collectives  112 us (7%)
  local copies, waits for them, and re-layouts  73.6 us (4%)
  other arithmetic  72.4 us (4%)
    reduce_scatter x5, waiting for transfers between devices, spread(): lax.psum_scatter(grad.astype(jnp.bfloat16), 'grp', scatter_dimension=0, t...  564 us
    all_gather x1, waiting for transfers between devices, body(): qkv_all = lax.all_gather(w_qkv, 'grp', axis=0, tiled=True)  118 us
    all_gather x1, waiting for transfers between devices, body(): gate_all = lax.all_gather(w_gate, 'grp', axis=0, tiled=True)  102 us
    all_gather x1, waiting for transfers between devices, body(): up_all = lax.all_gather(w_up, 'grp', axis=0, tiled=True)  100 us
    all_gather x1, waiting for transfers between devices, body(): down_all = lax.all_gather(w_down, 'grp', axis=0, tiled=True)  99.1 us
    psum x1, waiting for transfers between devices, body(): mod_table = lax.psum(mod_part + bias_part[None, :], 'grp')  71.5 us
    all_gather x1, waiting for transfers between devices, body(): kv_rows = lax.all_gather(kv_local, 'band', axis=1, tiled=True)  47.2 us
    reduce_scatter x1, waiting for transfers between devices, body(): lax.psum_scatter(kv_terms.astype(jnp.bfloat16), 'band', scatter_dimension...  38.5 us
  transfers between devices with their start and end apart: 14, of which 13 were waited for; matrix products, arithmetic and copies ran while one was open for 11% of the time, Pallas kernels for 0%

profile of v1, /device:TPU:0, one launch (start us, length us, event | category | flops | bytes accessed | tf_op | source)
XLA Modules:
  0.0 1678.6 jit_solution(6766691968802740562)
XLA Ops:
  13.6 71.5 %all-reduce.13.cloned.1.call-done = f32[8,6912]{1,0:T(8,128)} async-done(((f32[8,6912]{1,0:T(8,128)}), f32[8,6912]{1,0:T(8,128)}) %all-reduce.13.cloned.1.call-update) | async-done | bytes 221200 | tf_op jit(solution)/shard_map/psum | solution.py:108
  88.8 117.6 %all-gather.9.cloned.1.call-done = bf16[1152,3456]{1,0:T(8,128)(2,1)} async-done(((bf16[144,3456]{1,0:T(8,128)(2,1)}), bf16[1152,3456]{1,0:T(8,128)(2,1)}) %all-gather.9.cloned.1.call-update) | async-done | bytes 7962640 | tf_op jit(solution)/shard_map/all_gather | solution.py:90
  206.4 11.5 copy.68
  218.0 7.6 fusion.101
  243.2 4.2 reshape.420
  250.0 47.2 %all-gather.11.cloned.1.call-done = bf16[2,1024,2304]{1,2,0:T(8,128)(2,1)} async-done(((bf16[2,256,2304]{1,2,0:T(8,128)(2,1)}), bf16[2,1024,2304]{1,2,0:T(8,128)(2,1)}) %all-gather.11.cloned.1.call-update) | async-done | bytes 9437200 | tf_op jit(solution)/shard_map/all_gather | solution.py:137
  297.1 8.5 fusion.98
  305.6 46.7 %while.26 = (s32[]{:T(128)}, bf16[8,256,4,72]{1,3,2,0:T(8,128)(2,1)}, f32[8,4,256,1]{2,1,3,0:T(4,128)S(1)}, bf16[8,1024,4,72]{1,3,2,0:T(8,128)(2,1)}, bf16[8,256...) while((s32[]{:T(128)}, bf16[8,256,4,72]{1,3,2,0:T(8,128)(2,1)}, ...), condition=%wide.region_7.8_spmd, body=%wide.region_4.7_spmd.sunk | while | flops 311499776 | bytes 14092377 | solution.py:159
  314.4 2.9 fusion.154
  320.2 2.9 fusion.154
  337.7 2.9 fusion.154
  354.4 5.6 multiply_reduce_fusion.9
  361.9 102.2 %all-gather.15.cloned.1.call-done = bf16[1152,3072]{1,0:T(8,128)(2,1)} async-done(((bf16[144,3072]{1,0:T(8,128)(2,1)}), bf16[1152,3072]{1,0:T(8,128)(2,1)}) %all-gather.15.cloned.1.call-update) | async-done | bytes 7077904 | tf_op jit(solution)/shard_map/all_gather | solution.py:92
  464.1 9.3 fusion.102
  473.4 100.0 %all-gather.17.cloned.1.call-done = bf16[1152,3072]{1,0:T(8,128)(2,1)} async-done(((bf16[144,3072]{1,0:T(8,128)(2,1)}), bf16[1152,3072]{1,0:T(8,128)(2,1)}) %all-gather.17.cloned.1.call-update) | async-done | bytes 7077904 | tf_op jit(solution)/shard_map/all_gather | solution.py:93
  573.4 10.4 fusion.103
  583.8 99.1 %all-gather.19.cloned.1.call-done = bf16[3072,1152]{1,0:T(8,128)(2,1)} async-done(((bf16[384,1152]{1,0:T(8,128)(2,1)}), bf16[3072,1152]{1,0:T(8,128)(2,1)}) %all-gather.19.cloned.1.call-update) | async-done | bytes 7077904 | tf_op jit(solution)/shard_map/all_gather | solution.py:94
  682.8 22.6 %multiply_convert_fusion.1 = (bf16[512,3072]{1,0:T(8,128)(2,1)}, bf16[512,3072]{1,0:T(8,128)(2,1)}, bf16[512,3072]{1,0:T(8,128)(2,1)S(1)}) fusion(f32[512,3072]{1,0:T(8,128)} %fusion.102, f32[512,3072]{1,0:T(8,128)} %fusion.103, bf16[512,1152]{1,0:T(8,128)(2,1)S(1)} %copy-done.15, bf16[3072,1152]{1,0:T(8,128)(2,1)} %all-gather.19.cloned.1.call-done), kind=kOutput, calls=%fused_computation.72 | convolution fusion | flops 3649044480 | bytes 30277632 | tf_op jit(solution)/shard_map/td,fd->tf/dot_general | solution.py:180
  705.4 9.4 fusion.105
  714.9 6.4 convolution_add_fusion.1
  722.1 4.2 fusion.104
  739.0 96.7 %while.27 = (s32[]{:T(128)}, f32[8,256,4,72]{1,3,2,0:T(8,128)}, bf16[8,1024,4,72]{1,3,2,0:T(8,128)(2,1)}, bf16[8,1024,4,72]{1,3,2,0:T(8,128)(2,1)}, bf16[8,1024,...) while((s32[]{:T(128)}, f32[8,256,4,72]{1,3,2,0:T(8,128)}, ...), condition=%wide.region_12.13_spmd, body=%wide.region_10.12_spmd.sunk | while | flops 767925248 | bytes 36504688 | solution.py:229
  835.6 6.8 copy.77
  842.4 6.7 copy.76
  849.1 9.0 pad_maximum_fusion
  860.9 3.2 convolution_convert_fusion.3
  865.7 8.3 convolution_convert_fusion.2
  874.1 7.6 convolution_convert_fusion.1
  883.0 8.9 convolution_convert_fusion
  892.7 3.8 multiply_add_fusion.7
  896.4 38.5 %reduce-scatter.7.cloned.1.call-done = bf16[2,256,2304]{2,1,0:T(8,128)(2,1)} async-done(((bf16[2,1024,2304]{2,1,0:T(8,128)(2,1)}), bf16[2,256,2304]{2,1,0:T(8,128)(2,1)}) %reduce-scatter.7.cloned.1.call-update) | async-done | bytes 2359312 | tf_op jit(solution)/shard_map/reduce_scatter | solution.py:236
  934.9 3.7 slice_convert_fusion.1
  938.6 3.2 copy.78
  944.7 4.3 multiply_reduce_fusion.3
  949.1 3.1 fusion.62
  957.0 11.2 fusion.69
  968.2 7.0 fusion.52
  976.0 11.1 psum.64
  987.2 22.4 %reduce-scatter.11.cloned.1.call-done = bf16[144,1152]{1,0:T(8,128)(2,1)} async-done(((bf16[1152,1152]{1,0:T(8,128)(2,1)}), bf16[144,1152]{1,0:T(8,128)(2,1)}) %reduce-scatter.11.cloned.1.call-update) | async-done | bytes 331792 | tf_op jit(solution)/shard_map/reduce_scatter | solution.py:282
  1009.6 131.6 %reduce-scatter.13.cloned.1.call-done = bf16[144,3072]{1,0:T(8,128)(2,1)} async-done(((bf16[1152,3072]{1,0:T(8,128)(2,1)}), bf16[144,3072]{1,0:T(8,128)(2,1)}) %reduce-scatter.13.cloned.1.call-update) | async-done | bytes 884752 | tf_op jit(solution)/shard_map/reduce_scatter | solution.py:282
  1141.2 132.2 %reduce-scatter.15.cloned.1.call-done = bf16[144,3072]{1,0:T(8,128)(2,1)} async-done(((bf16[1152,3072]{1,0:T(8,128)(2,1)}), bf16[144,3072]{1,0:T(8,128)(2,1)}) %reduce-scatter.15.cloned.1.call-update) | async-done | bytes 884752 | tf_op jit(solution)/shard_map/reduce_scatter | solution.py:282
  1273.4 131.7 %reduce-scatter.17.cloned.1.call-done = bf16[384,1152]{1,0:T(8,128)(2,1)} async-done(((bf16[3072,1152]{1,0:T(8,128)(2,1)}), bf16[384,1152]{1,0:T(8,128)(2,1)}) %reduce-scatter.17.cloned.1.call-update) | async-done | bytes 884752 | tf_op jit(solution)/shard_map/reduce_scatter | solution.py:282
  1405.1 145.6 %reduce-scatter.9.cloned.1.call-done = bf16[144,3456]{1,0:T(8,128)(2,1)} async-done(((bf16[1152,3456]{1,0:T(8,128)(2,1)}), bf16[144,3456]{1,0:T(8,128)(2,1)}) %reduce-scatter.9.cloned.1.call-update) | async-done | bytes 995344 | tf_op jit(solution)/shard_map/reduce_scatter | solution.py:282
  1550.7 32.7 %all-gather = bf16[8,2,6920]{2,1,0:T(2,128)(2,1)} all-gather(bf16[1,2,6920]{2,1,0:T(2,128)(2,1)S(1)} %maximum_bitcast_fusion), channel_id=1, replica_groups=mesh['grp'=8,'band'=4] {'grp'}, dimensions={0}, use_global_device_ids=true | all-gather | bytes 249120 | tf_op jit(solution)/shard_map/all_gather | solution.py:260
  1586.0 30.5 %all-gather.1 = f32[8,144,8]{1,2,0:T(8,128)S(1)} all-gather(f32[1,144,8]{1,2,0:T(8,128)S(1)} %fusion.85), channel_id=1, replica_groups=mesh['grp'=8,'band'=4] {'grp'}, dimensions={0}, use_global_device_ids=true | all-gather | bytes 41472 | tf_op jit(solution)/shard_map/all_gather | solution.py:278
  1618.0 38.1 %all-reduce.8 = (f32[72]{0:T(128)}, f32[72]{0:T(128)}) all-reduce(f32[72]{0:T(128)S(1)} %get-tuple-element.146, f32[72]{0:T(128)S(1)} %get-tuple-element.209), channel_id=1, replica_groups=mesh['grp'=8,'band'=4] {'grp','band'}, use_global_device_ids=true, to_apply=%region_28.29 | all-reduce | flops 144 | bytes 1152 | tf_op jit(solution)/shard_map/psum | solution.py:279
  1656.2 3.6 fusion.77
  1659.8 4.4 fusion.64
  (320 shorter events, 206.8 us)
Async XLA Ops:
  7.2 5.1 copy-start.54
  7.2 5.2 copy-start.5
  7.2 77.9 %all-reduce.13.cloned.1.call-start = ((), (), s32[]{:S(2)}) async-start(), calls=%async_computation.6 | async-start | bytes 442368 | tf_op jit(solution)/shard_map/psum | solution.py:108
  10.6 195.8 %all-gather.9.cloned.1.call-start = ((), (), s32[]{:S(2)}) async-start(), calls=%async_computation.7 | async-start | bytes 8957952 | tf_op jit(solution)/shard_map/all_gather | solution.py:90
  11.4 285.8 %all-gather.11.cloned.1.call-start = ((), (), s32[]{:S(2)}) async-start(), calls=%async_computation.8 | async-start | bytes 11796480 | tf_op jit(solution)/shard_map/all_gather | solution.py:137
  13.5 226.0 %copy-start.27 = (f32[256,18]{0,1:T(8,128)}, f32[256,18]{0,1:T(8,128)S(1)}, u32[]{:S(2)}) copy-start(f32[256,18]{0,1:T(8,128)S(1)} %get-tuple-element.253) | copy-start | bytes 55300
  13.5 226.0 %copy-start.29 = (f32[256,18]{0,1:T(8,128)}, f32[256,18]{0,1:T(8,128)S(1)}, u32[]{:S(2)}) copy-start(f32[256,18]{0,1:T(8,128)S(1)} %get-tuple-element.254) | copy-start | bytes 55300
  13.6 226.0 %copy-start.31 = (f32[256,18]{0,1:T(8,128)}, f32[256,18]{0,1:T(8,128)S(1)}, u32[]{:S(2)}) copy-start(f32[256,18]{0,1:T(8,128)S(1)} %get-tuple-element.257) | copy-start | bytes 55300
  13.6 226.0 %copy-start.33 = (f32[256,18]{0,1:T(8,128)}, f32[256,18]{0,1:T(8,128)S(1)}, u32[]{:S(2)}) copy-start(f32[256,18]{0,1:T(8,128)S(1)} %get-tuple-element.258) | copy-start | bytes 55300
  225.6 2.9 copy-start.1
  226.3 4.2 copy-start.35
  233.3 121.1 %all-gather.13.cloned.1.call-start = ((), (), s32[]{:S(2)}) async-start(), calls=%async_computation.9 | async-start | bytes 2985984 | tf_op jit(solution)/shard_map/all_gather | solution.py:91
  233.9 230.2 %all-gather.15.cloned.1.call-start = ((), (), s32[]{:S(2)}) async-start(), calls=%async_computation.10 | async-start | bytes 7962624 | tf_op jit(solution)/shard_map/all_gather | solution.py:92
  234.4 339.0 %all-gather.17.cloned.1.call-start = ((), (), s32[]{:S(2)}) async-start(), calls=%async_computation.11 | async-start | bytes 7962624 | tf_op jit(solution)/shard_map/all_gather | solution.py:93
  235.0 447.8 %all-gather.19.cloned.1.call-start = ((), (), s32[]{:S(2)}) async-start(), calls=%async_computation.12 | async-start | bytes 7962624 | tf_op jit(solution)/shard_map/all_gather | solution.py:94
  235.8 699.2 %reduce-scatter.7.cloned.1.call-start = ((), (), s32[]{:S(2)}) async-start(), calls=%async_computation.13 | async-start | bytes 11796480 | tf_op jit(solution)/shard_map/reduce_scatter | solution.py:236
  235.9 3.7 copy-start.7
  361.9 102.2 %copy-start.19 = (bf16[2,256,1152]{2,1,0:T(8,128)(2,1)}, bf16[2,256,1152]{2,1,0:T(8,128)(2,1)S(1)}, u32[]{:S(2)}) copy-start(bf16[2,256,1152]{2,1,0:T(8,128)(2,1)S(1)} %add_convert_fusion) | copy-start | bytes 3538948
  473.4 209.5 %copy-start.15 = (bf16[512,1152]{1,0:T(8,128)(2,1)S(1)}, bf16[512,1152]{1,0:T(8,128)(2,1)}, u32[]{:S(2)}) copy-start(bf16[512,1152]{1,0:T(8,128)(2,1)} %fusion.65) | copy-start | bytes 3538948
  705.4 16.6 copy-start.56
  705.4 9.4 copy-start.53
  705.4 16.6 slice-start.2
  714.8 6.4 copy-start.3
  714.9 7.2 slice-start.3
  722.0 4.3 copy-start.8
  722.1 4.3 copy-start.13
  858.1 151.4 %reduce-scatter.11.cloned.1.call-start = ((), (), s32[]{:S(2)}) async-start(), calls=%async_computation.15 | async-start | bytes 2985984 | tf_op jit(solution)/shard_map/reduce_scatter | solution.py:282
  864.1 277.1 %reduce-scatter.13.cloned.1.call-start = ((), (), s32[]{:S(2)}) async-start(), calls=%async_computation.16 | async-start | bytes 7962624 | tf_op jit(solution)/shard_map/reduce_scatter | solution.py:282
  874.0 399.4 %reduce-scatter.15.cloned.1.call-start = ((), (), s32[]{:S(2)}) async-start(), calls=%async_computation.17 | async-start | bytes 7962624 | tf_op jit(solution)/shard_map/reduce_scatter | solution.py:282
  881.7 523.4 %reduce-scatter.17.cloned.1.call-start = ((), (), s32[]{:S(2)}) async-start(), calls=%async_computation.18 | async-start | bytes 7962624 | tf_op jit(solution)/shard_map/reduce_scatter | solution.py:282
  891.9 658.8 %reduce-scatter.9.cloned.1.call-start = ((), (), s32[]{:S(2)}) async-start(), calls=%async_computation.14 | async-start | bytes 8957952 | tf_op jit(solution)/shard_map/reduce_scatter | solution.py:282
  941.8 2.8 copy-start.36
  941.8 2.8 copy-start.38
  941.8 2.8 copy-start.50
  941.9 2.8 copy-start.52
  941.9 7.2 slice-start
  944.7 4.3 copy-start.41
  944.7 4.3 copy-start.43
  944.7 4.4 slice-start.1
  944.7 4.4 copy-start.11
  952.1 4.9 copy-start.6
  952.1 4.9 copy-start.45
  952.1 4.9 copy-start.47
  957.0 11.2 copy-start.17
  957.0 11.2 copy-start.18
  957.0 11.2 copy-start.23
  975.3 688.9 %all-reduce.15.cloned.1.call-start = ((), (), s32[]{:S(2)}) async-start(), calls=%async_computation.19 | async-start | bytes 7962624 | tf_op jit(solution)/shard_map/psum | solution.py:285
  1664.2 3.6 copy-start.26
  (27 other events, 42.6 us)
Sparse Core Ops, SparseCore 0:
  12.0 73.0 all-reduce.12
  87.5 118.8 all-gather.8
  233.4 63.6 all-gather.10
  299.4 55.0 all-gather.12
  356.7 107.3 all-gather.14
  466.4 106.9 all-gather.16
  575.8 106.9 all-gather.18
  858.3 76.6 reduce-scatter.6
  939.0 70.4 reduce-scatter.10
  1013.1 128.0 reduce-scatter.12
  1145.3 128.0 reduce-scatter.14
  1276.9 128.0 reduce-scatter.16
  1409.1 141.5 reduce-scatter.8
  1553.5 82.7 all-reduce.14

commit v2 on v1

--- a/solution.py
+++ b/solution.py
@@ -1,7 +1,112 @@
+import functools
+
 import jax
 import jax.numpy as jnp
 from jax import lax
+from jax.experimental import pallas as pl
+from jax.experimental.pallas import tpu as pltpu
 from jax.sharding import PartitionSpec as P
+
+MESH = pl.DeviceIdType.MESH
+
+def gather_kernel(cuts, when_own, *refs):
+    n = len(cuts)
+    ins, outs = refs[:n], refs[n:2*n]
+    lsem, zs, zr, xs, xr, ys, yr, cs, cr, ds, dr = refs[2*n:]
+    g = lax.axis_index("grp"); band = lax.axis_index("band")
+    z = g // 2; x = g % 2; y = band // 2; c = band % 2
+    far = [z, z + 1 - 2 * (z % 2), 2 - z // 2, 3 - 3 * (z // 2)]
+    ypeer = (g, (1 - y) * 2 + c); cpeer = (g, y * 2 + 1 - c); xpeer = (z * 2 + 1 - x, band)
+    bar = pltpu.get_barrier_semaphore()
+    for d in [xpeer, ypeer, cpeer] + [(zz * 2 + x, band) for zz in far[1:]]:
+        pl.semaphore_signal(bar, inc=1, device_id=d, device_id_type=MESH)
+    pl.semaphore_wait(bar, 6)
+    def at(ref, shard, axis, start, size):
+        ref = ref if shard is None else ref.at[shard]
+        if axis == 0:
+            return ref.at[pl.ds(pl.multiple_of(start, 16), size), :]
+        return ref.at[:, pl.ds(pl.multiple_of(start, 128), size)]
+    def piece(i, ref, shard, yy, cc):
+        axis, half, a, b = cuts[i]
+        return at(ref, shard, axis, cc * half + yy * b, a + b)
+    def bpart(i, ref, shard, yy, cc):
+        axis, half, a, b = cuts[i]
+        return at(ref, shard, axis, cc * half + yy * (a + b), b)
+    tail = []
+    def send(src, dst, ssem, rsem, dev, cond=None):
+        d = pltpu.make_async_remote_copy(src_ref=src, dst_ref=dst, send_sem=ssem, recv_sem=rsem, device_id=dev, device_id_type=MESH)
+        if cond is None:
+            d.start(); tail.append(d.wait_send)
+        else:
+            pl.when(cond)(d.start); tail.append(lambda: pl.when(cond)(d.wait_send))
+    def arrived(ref, rsem):
+        pltpu.make_async_remote_copy(src_ref=ref, dst_ref=ref, send_sem=lsem.at[0], recv_sem=rsem, device_id=xpeer, device_id_type=MESH).wait_recv()
+    def own(i):
+        src, dst = piece(i, ins[i], None, y, c), piece(i, outs[i], g, y, c)
+        send(src, dst, zs.at[i, 0], zr.at[i, z], (g + 2, band), z < 3)
+        send(src, dst, ds.at[i], zr.at[i, z], (g - 2, band), z > 0)
+        send(src, dst, xs.at[i, 0], xr.at[i, 0], xpeer)
+        d = pltpu.make_async_copy(ins[i], outs[i].at[g], lsem.at[i]); d.start(); tail.append(d.wait)
+    def down(i, slot, shard):
+        p = bpart(i, outs[i], shard, y, c)
+        send(p, p, ys.at[i, slot], yr.at[i, slot], ypeer)
+        p = piece(i, outs[i], shard, y, c)
+        send(p, p, cs.at[i, slot], cr.at[i, slot], cpeer)
+    def zarr(i, t):
+        zz = far[t]
+        s = zz * 2 + x
+        p = piece(i, outs[i], s, y, c)
+        arrived(p, zr.at[i, zz])
+        nxt = jnp.where(zz < z, z + 1, z - 1)
+        send(p, p, zs.at[i, t], zr.at[i, zz], (jnp.clip(nxt, 0, 3) * 2 + x, band), (nxt >= 0) & (nxt <= 3))
+        send(p, p, xs.at[i, t], xr.at[i, t], xpeer)
+        down(i, t - 1, s)
+    def xarr(i, t):
+        s = far[t] * 2 + 1 - x
+        arrived(piece(i, outs[i], s, y, c), xr.at[i, t])
+        down(i, 3 + t, s)
+    def slots():
+        return [(t - 1, far[t] * 2 + x) for t in (1, 2, 3)] + [(3 + t, far[t] * 2 + 1 - x) for t in range(4)]
+    def yarr(i, slot, s):
+        p = bpart(i, outs[i], s, 1 - y, c)
+        arrived(p, yr.at[i, slot])
+        send(p, p, cs.at[i, 7 + slot], cr.at[i, 7 + slot], cpeer)
+    acts = []
+    order = [3, 0, 4, 1, 5, 2, 6]
+    for i in range(n):
+        if i == 0:
+            acts.append(lambda: own(0))
+        seq = [lambda i=i: zarr(i, 1), lambda i=i: xarr(i, 0), lambda i=i: zarr(i, 2), lambda i=i: xarr(i, 1), lambda i=i: zarr(i, 3), lambda i=i: xarr(i, 2), lambda i=i: xarr(i, 3)]
+        if i + 1 < n:
+            seq.insert(when_own, lambda i=i: own(i + 1))
+        sl = slots()
+        if i > 0:
+            for q in range(7):
+                seq.insert(2 * q + 1, lambda i=i, q=q: yarr(i - 1, *sl[order[q]]))
+        acts += seq
+    sl = slots()
+    acts += [lambda q=q: yarr(n - 1, *sl[order[q]]) for q in range(7)]
+    for a in acts:
+        a()
+    for i in range(n):
+        for slot, s in sl:
+            arrived(piece(i, outs[i], s, y, 1 - c), cr.at[i, slot])
+            arrived(bpart(i, outs[i], s, 1 - y, 1 - c), cr.at[i, 7 + slot])
+    for w in tail:
+        w()
+
+def gather(ws, cuts, cid=0, when_own=3):
+    n = len(ws)
+    S = pltpu.SemaphoreType.DMA
+    return pl.pallas_call(
+        functools.partial(gather_kernel, cuts, when_own),
+        out_shape=[jax.ShapeDtypeStruct((8,) + w.shape, w.dtype) for w in ws],
+        in_specs=[pl.BlockSpec(memory_space=pl.ANY)] * n,
+        out_specs=[pl.BlockSpec(memory_space=pl.ANY)] * n,
+        scratch_shapes=[S((n,)), S((n, 4)), S((n, 4)), S((n, 4)), S((n, 4)), S((n, 7)), S((n, 7)), S((n, 14)), S((n, 14)), S((n,)), S((n,))],
+        compiler_params=pltpu.CompilerParams(collective_id=cid, has_side_effects=True),
+        name="weight_gather",
+    )(*ws)
 
 HEADS = 16
 HDIM = 72
@@ -61,6 +166,32 @@
     groups = blocks // count
     shaped = tensor.reshape(count, groups, span, per_block, size)
     return jnp.transpose(shaped, (0, 2, 1, 3, 4)).reshape(count, span, groups * per_block, size)
+
+
+def half_cuts(axis, size, own_parts, shared_parts):
+    unit = size // 2 // (own_parts + 2 * shared_parts)
+    return (axis, size // 2, own_parts * unit, shared_parts * unit)
+
+
+def gather_weights(shards):
+    rows, wide = shards[0].shape
+    fits = (
+        lax.axis_size("grp") == 8
+        and lax.axis_size("band") == 4
+        and rows % 16 == 0
+        and shards[2].shape[0] % 96 == 0
+        and wide % 768 == 0
+        and shards[1].shape[1] % 768 == 0
+    )
+    if not fits:
+        return [lax.all_gather(w, "grp", axis=0, tiled=True) for w in shards]
+    cuts = (
+        half_cuts(1, wide, 1, 1),
+        half_cuts(1, shards[1].shape[1], 1, 1),
+        half_cuts(0, shards[2].shape[0], 1, 1),
+    )
+    full = gather(shards, cuts)
+    return [w.reshape(-1, w.shape[-1]) for w in full]
 
 
 def body(
@@ -87,11 +218,14 @@
     grp = lax.axis_index("grp")
     ada_rows = w_ada.shape[0]
     bias_cols = b_ada.shape[0]
-    qkv_all = lax.all_gather(w_qkv, "grp", axis=0, tiled=True)
-    proj_all = lax.all_gather(w_proj, "grp", axis=0, tiled=True)
-    gate_all = lax.all_gather(w_gate, "grp", axis=0, tiled=True)
-    up_all = lax.all_gather(w_up, "grp", axis=0, tiled=True)
-    down_all = lax.all_gather(w_down, "grp", axis=0, tiled=True)
+    shards = (
+        jnp.concatenate([w_qkv, w_proj], axis=1),
+        jnp.concatenate([w_gate, w_up], axis=1),
+        w_down,
+    )
+    qp_all, gu_all, down_all = gather_weights(shards)
+    qkv_all, proj_all = qp_all[:, : w_qkv.shape[1]], qp_all[:, w_qkv.shape[1] :]
+    gate_all, up_all = gu_all[:, : w_gate.shape[1]], gu_all[:, w_gate.shape[1] :]
     onehot = (group_ids[:, None] == jnp.arange(GROUPS, dtype=jnp.int32)[None, :]).astype(
         jnp.float32
     )

time: 1680 us -> 1350 us (0.80)
  waiting for transfers between devices: 1140 us -> 656 us
  Pallas kernels: 0 us -> 141 us
    all_gather x5 -> x0, waiting for transfers between devices: 421 us -> none  [the longest x1 118 us: body(): qkv_all = lax.all_gather(w_qkv, 'grp', axis=0, tiled=True)]
    pallas_call x0 -> x1, Pallas kernels: none -> 141 us  [gather(): pl.pallas_call(functools.partial(gather_kernel, cuts, when_own), out_shap...]
    psum x1, waiting for transfers between devices: 71.5 us -> 0.02 us  [body(): mod_table = lax.psum(mod_part + bias_part[None, :], 'grp')]
  transfers between devices with their start and end apart: 14 -> 9, of which waited for: 13 -> 7; matrix products, arithmetic and copies ran while one was open for 11% -> 9% of each run, Pallas kernels for 0% -> 11%
where the time goes in v2:
time: 1350 us; the launch traced here: 1340 us
  waiting for transfers between devices  656 us (49%)
  matrix products  264 us (20%)
  Pallas kernels  141 us (10%)
  blocking collectives  113 us (8%)
  local copies, waits for them, and re-layouts  78.8 us (6%)
  other arithmetic  72.4 us (5%)
  between operations  16.3 us (1%)
    reduce_scatter x5, waiting for transfers between devices, spread(): lax.psum_scatter(grad.astype(jnp.bfloat16), 'grp', scatter_dimension=0, t...  564 us
    pallas_call x1, Pallas kernels, gather(): pl.pallas_call(functools.partial(gather_kernel, cuts, when_own), out_shap...  141 us
    all_gather x1, waiting for transfers between devices, body(): kv_rows = lax.all_gather(kv_local, 'band', axis=1, tiled=True)  52.7 us
    reduce_scatter x1, waiting for transfers between devices, body(): lax.psum_scatter(kv_terms.astype(jnp.bfloat16), 'band', scatter_dimension...  39.3 us
    psum x1, blocking collectives, body(): d_q_gain, d_k_gain = lax.psum((d_q_gain, d_k_gain), ('grp', 'band'))  38 us
    all_gather x1, blocking collectives, body(): payload = lax.all_gather(payload, 'grp', axis=0, tiled=True)  32.7 us
    all_gather x1, blocking collectives, body(): d_cond = lax.all_gather(d_cond_rows, 'grp', axis=1, tiled=True)  30.7 us
  transfers between devices with their start and end apart: 9, of which 7 were waited for; matrix products, arithmetic and copies ran while one was open for 9% of the time, Pallas kernels for 11%

profile of v2, /device:TPU:0, one launch (start us, length us, event | category | flops | bytes accessed | tf_op | source)
XLA Modules:
  0.0 1342.3 jit_solution(5673033545035342892)
XLA Ops:
  15.4 141.1 %weight_gather.1 = (bf16[8,144,4608]{2,1,0:T(8,128)(2,1)}, bf16[8,144,6144]{2,1,0:T(8,128)(2,1)}, bf16[8,384,1152]{2,1,0:T(8,128)(2,1)}) custom-call(bf16[144,4608]{1,0:T(8,128)(2,1)} %pad_maximum_fusion.6.refs_0_, bf16[144,6144]{1,0:T(8,128)(2,1)} %pad_maximum_fusion.3.refs_1_, bf16[384,1152]{1,0:T(8,128)(2,1)} %refs_2_.1), custom_call_target="tpu_custom_call" | custom-call | tf_op jit(solution)/shard_map/weight_gather/pallas_call | solution.py:101
  156.5 6.9 slice_bitcast_fusion
  163.4 11.5 copy.68
  178.4 7.3 fusion.115
  200.0 4.0 reshape.466
  206.8 52.7 %all-gather.4.cloned.1.call-done = bf16[2,1024,2304]{1,2,0:T(8,128)(2,1)} async-done(((bf16[2,256,2304]{1,2,0:T(8,128)(2,1)}), bf16[2,1024,2304]{1,2,0:T(8,128)(2,1)}) %all-gather.4.cloned.1.call-update) | async-done | bytes 9437200 | tf_op jit(solution)/shard_map/all_gather | solution.py:271
  259.5 8.5 fusion.112
  268.0 46.7 %while.26 = (s32[]{:T(128)}, bf16[8,256,4,72]{1,3,2,0:T(8,128)(2,1)}, f32[8,4,256,1]{2,1,3,0:T(4,128)S(1)}, bf16[8,1024,4,72]{1,3,2,0:T(8,128)(2,1)}, bf16[8,256...) while((s32[]{:T(128)}, bf16[8,256,4,72]{1,3,2,0:T(8,128)(2,1)}, ...), condition=%wide.region_7.8_spmd, body=%wide.region_4.7_spmd.sunk | while | flops 311499776 | bytes 14092377 | solution.py:293
  276.7 2.9 fusion.160
  282.6 2.9 fusion.160
  288.4 2.9 fusion.160
  294.2 2.9 fusion.160
  300.1 2.9 fusion.160
  314.7 5.7 multiply_reduce_fusion.9
  321.1 9.7 fusion.116
  330.7 9.1 fusion.62
  339.8 23.5 %fusion.58 = (bf16[512,3072]{1,0:T(8,128)(2,1)S(1)}, bf16[512,3072]{1,0:T(8,128)(2,1)}, bf16[512,3072]{1,0:T(8,128)(2,1)S(1)}) fusion(f32[512,3072]{1,0:T(8,128)} %fusion.116, f32[512,3072]{1,0:T(8,128)} %fusion.62, bf16[512,1152]{1,0:T(8,128)(2,1)S(1)} %bitcast.318, bf16[1152,6144]{1,0:T(8,128)(2,1)} %bitcast.327), kind=kOutput, calls=%fused_computation.73 | convolution fusion | flops 3649044480 | bytes 30277632 | tf_op jit(solution)/shard_map/dot_general | solution.py:301
  363.3 10.5 fusion.60
  373.9 7.5 fusion.68
  383.0 5.9 multiply_reduce_fusion.4
  391.5 5.1 convolution_convert_fusion.4
  400.7 96.5 %while.27 = (s32[]{:T(128)}, f32[8,256,4,72]{1,3,2,0:T(8,128)}, bf16[8,1024,4,72]{1,3,2,0:T(8,128)(2,1)}, bf16[8,1024,4,72]{1,3,2,0:T(8,128)(2,1)}, bf16[8,1024,...) while((s32[]{:T(128)}, f32[8,256,4,72]{1,3,2,0:T(8,128)}, ...), condition=%wide.region_12.13_spmd, body=%wide.region_10.12_spmd.sunk | while | flops 767925248 | bytes 36504688 | solution.py:363
  497.3 6.7 copy.77
  504.0 6.8 copy.76
  510.8 9.1 pad_maximum_fusion
  522.7 3.4 convolution_convert_fusion.3
  527.3 8.5 convolution_convert_fusion.2
  535.9 7.8 convolution_convert_fusion.1
  545.7 9.0 convolution_convert_fusion
  555.5 3.8 multiply_add_fusion.7
  559.2 39.3 %reduce-scatter.7.cloned.1.call-done = bf16[2,256,2304]{2,1,0:T(8,128)(2,1)} async-done(((bf16[2,1024,2304]{2,1,0:T(8,128)(2,1)}), bf16[2,256,2304]{2,1,0:T(8,128)(2,1)}) %reduce-scatter.7.cloned.1.call-update) | async-done | bytes 2359312 | tf_op jit(solution)/shard_map/reduce_scatter | solution.py:370
  598.5 3.7 slice_convert_fusion.1
  602.2 3.0 copy.78
  608.1 4.3 multiply_reduce_fusion.3
  612.5 3.1 fusion.74
  620.4 11.1 fusion.81
  631.6 6.9 fusion.52
  639.3 11.1 psum.64
  650.4 22.6 %reduce-scatter.11.cloned.1.call-done = bf16[144,1152]{1,0:T(8,128)(2,1)} async-done(((bf16[1152,1152]{1,0:T(8,128)(2,1)}), bf16[144,1152]{1,0:T(8,128)(2,1)}) %reduce-scatter.11.cloned.1.call-update) | async-done | bytes 331792 | tf_op jit(solution)/shard_map/reduce_scatter | solution.py:416
  673.1 131.6 %reduce-scatter.13.cloned.1.call-done = bf16[144,3072]{1,0:T(8,128)(2,1)} async-done(((bf16[1152,3072]{1,0:T(8,128)(2,1)}), bf16[144,3072]{1,0:T(8,128)(2,1)}) %reduce-scatter.13.cloned.1.call-update) | async-done | bytes 884752 | tf_op jit(solution)/shard_map/reduce_scatter | solution.py:416
  804.7 132.1 %reduce-scatter.15.cloned.1.call-done = bf16[144,3072]{1,0:T(8,128)(2,1)} async-done(((bf16[1152,3072]{1,0:T(8,128)(2,1)}), bf16[144,3072]{1,0:T(8,128)(2,1)}) %reduce-scatter.15.cloned.1.call-update) | async-done | bytes 884752 | tf_op jit(solution)/shard_map/reduce_scatter | solution.py:416
  936.7 131.8 %reduce-scatter.17.cloned.1.call-done = bf16[384,1152]{1,0:T(8,128)(2,1)} async-done(((bf16[3072,1152]{1,0:T(8,128)(2,1)}), bf16[384,1152]{1,0:T(8,128)(2,1)}) %reduce-scatter.17.cloned.1.call-update) | async-done | bytes 884752 | tf_op jit(solution)/shard_map/reduce_scatter | solution.py:416
  1068.5 145.8 %reduce-scatter.9.cloned.1.call-done = bf16[144,3456]{1,0:T(8,128)(2,1)} async-done(((bf16[1152,3456]{1,0:T(8,128)(2,1)}), bf16[144,3456]{1,0:T(8,128)(2,1)}) %reduce-scatter.9.cloned.1.call-update) | async-done | bytes 995344 | tf_op jit(solution)/shard_map/reduce_scatter | solution.py:416
  1214.3 32.7 %all-gather = bf16[8,2,6920]{2,1,0:T(2,128)(2,1)} all-gather(bf16[1,2,6920]{2,1,0:T(2,128)(2,1)S(1)} %maximum_bitcast_fusion), channel_id=1, replica_groups=mesh['grp'=8,'band'=4] {'grp'}, dimensions={0}, use_global_device_ids=true | all-gather | bytes 249120 | tf_op jit(solution)/shard_map/all_gather | solution.py:394
  1249.6 30.7 %all-gather.1 = f32[8,144,8]{1,2,0:T(8,128)S(1)} all-gather(f32[1,144,8]{1,2,0:T(8,128)S(1)} %fusion.99), channel_id=1, replica_groups=mesh['grp'=8,'band'=4] {'grp'}, dimensions={0}, use_global_device_ids=true | all-gather | bytes 41472 | tf_op jit(solution)/shard_map/all_gather | solution.py:412
  1281.9 38.0 %all-reduce.8 = (f32[72]{0:T(128)}, f32[72]{0:T(128)}) all-reduce(f32[72]{0:T(128)S(1)} %get-tuple-element.152, f32[72]{0:T(128)S(1)} %get-tuple-element.215), channel_id=1, replica_groups=mesh['grp'=8,'band'=4] {'grp','band'}, use_global_device_ids=true, to_apply=%region_28.29 | all-reduce | flops 144 | bytes 1152 | tf_op jit(solution)/shard_map/psum | solution.py:413
  1319.8 3.6 fusion.91
  1323.4 4.4 fusion.76
  (305 shorter events, 191.6 us)
Async XLA Ops:
  7.2 3.5 copy-start.50
  7.2 3.6 copy-start.2
  7.2 4.5 copy-start.36
  7.2 168.9 %all-reduce.13.cloned.1.call-start = ((), (), s32[]{:S(2)}) async-start(), calls=%async_computation.6 | async-start | bytes 442368 | tf_op jit(solution)/shard_map/psum | solution.py:242
  10.6 248.8 %all-gather.4.cloned.1.call-start = ((), (), s32[]{:S(2)}) async-start(), calls=%async_computation.7 | async-start | bytes 11796480 | tf_op jit(solution)/shard_map/all_gather | solution.py:271
  10.7 3.4 copy-start.18
  10.7 3.4 copy-start.19
  176.0 18.3 %copy-start.23 = (f32[256,18]{0,1:T(8,128)}, f32[256,18]{0,1:T(8,128)S(1)}, u32[]{:S(2)}) copy-start(f32[256,18]{0,1:T(8,128)S(1)} %get-tuple-element.261) | copy-start | bytes 55300
  176.0 18.3 %copy-start.25 = (f32[256,18]{0,1:T(8,128)}, f32[256,18]{0,1:T(8,128)S(1)}, u32[]{:S(2)}) copy-start(f32[256,18]{0,1:T(8,128)S(1)} %get-tuple-element.262) | copy-start | bytes 55300
  176.0 18.3 %copy-start.27 = (f32[256,18]{0,1:T(8,128)}, f32[256,18]{0,1:T(8,128)S(1)}, u32[]{:S(2)}) copy-start(f32[256,18]{0,1:T(8,128)S(1)} %get-tuple-element.265) | copy-start | bytes 55300
  176.1 18.3 %copy-start.29 = (f32[256,18]{0,1:T(8,128)}, f32[256,18]{0,1:T(8,128)S(1)}, u32[]{:S(2)}) copy-start(f32[256,18]{0,1:T(8,128)S(1)} %get-tuple-element.266) | copy-start | bytes 55300
  185.7 2.8 copy-start.1
  185.8 2.7 copy-start.46
  185.8 2.7 copy-start.48
  186.4 4.1 copy-start.31
  193.3 405.2 %reduce-scatter.7.cloned.1.call-start = ((), (), s32[]{:S(2)}) async-start(), calls=%async_computation.8 | async-start | bytes 11796480 | tf_op jit(solution)/shard_map/reduce_scatter | solution.py:370
  314.7 5.7 copy-start.8
  321.1 18.8 %copy-start.13 = (bf16[2,256,1152]{2,1,0:T(8,128)(2,1)}, bf16[2,256,1152]{2,1,0:T(8,128)(2,1)S(1)}, u32[]{:S(2)}) copy-start(bf16[2,256,1152]{2,1,0:T(8,128)(2,1)S(1)} %get-tuple-element.270) | copy-start | bytes 3538948
  363.3 10.5 copy-start.54
  363.3 18.9 %copy-start.52 = (bf16[512,3072]{1,0:T(8,128)(2,1)}, bf16[512,3072]{1,0:T(8,128)(2,1)S(1)}, u32[]{:S(2)}) copy-start(bf16[512,3072]{1,0:T(8,128)(2,1)S(1)} %get-tuple-element.209) | copy-start | bytes 9437188
  363.3 18.9 %slice-start.2 = ((s8[7077888]{0:T(1024)(128)(4,1)}), s8[4194304]{0:T(1024)(128)(4,1)S(1)}, s32[]{:S(2)}) async-start(s8[7077888]{0:T(1024)(128)(4,1)} %bitcast.331), calls=%async_computation.17 | async-start | bytes 8388608
  373.8 8.4 slice-start.3
  519.9 153.1 %reduce-scatter.11.cloned.1.call-start = ((), (), s32[]{:S(2)}) async-start(), calls=%async_computation.10 | async-start | bytes 2985984 | tf_op jit(solution)/shard_map/reduce_scatter | solution.py:416
  526.1 278.6 %reduce-scatter.13.cloned.1.call-start = ((), (), s32[]{:S(2)}) async-start(), calls=%async_computation.11 | async-start | bytes 7962624 | tf_op jit(solution)/shard_map/reduce_scatter | solution.py:416
  535.9 400.9 %reduce-scatter.15.cloned.1.call-start = ((), (), s32[]{:S(2)}) async-start(), calls=%async_computation.12 | async-start | bytes 7962624 | tf_op jit(solution)/shard_map/reduce_scatter | solution.py:416
  543.8 524.7 %reduce-scatter.17.cloned.1.call-start = ((), (), s32[]{:S(2)}) async-start(), calls=%async_computation.13 | async-start | bytes 7962624 | tf_op jit(solution)/shard_map/reduce_scatter | solution.py:416
  554.7 659.5 %reduce-scatter.9.cloned.1.call-start = ((), (), s32[]{:S(2)}) async-start(), calls=%async_computation.9 | async-start | bytes 8957952 | tf_op jit(solution)/shard_map/reduce_scatter | solution.py:416
  605.2 2.8 copy-start.5
  605.2 2.8 copy-start.6
  605.2 2.8 copy-start.32
  605.2 2.8 copy-start.34
  605.2 2.8 copy-start.47
  605.3 2.8 copy-start.49
  605.3 7.2 slice-start
  608.1 4.3 copy-start.40
  608.1 4.3 copy-start.38
  608.1 4.4 slice-start.1
  608.1 4.4 copy-start.7
  615.5 4.9 copy-start.3
  615.5 4.9 copy-start.42
  615.5 4.9 copy-start.44
  620.4 11.1 copy-start.11
  620.4 11.1 copy-start.12
  620.4 11.1 copy-start.17
  638.5 689.3 %all-reduce.15.cloned.1.call-start = ((), (), s32[]{:S(2)}) async-start(), calls=%async_computation.14 | async-start | bytes 7962624 | tf_op jit(solution)/shard_map/psum | solution.py:419
  1327.8 2.7 copy-start.35
  1327.8 3.6 copy-start.22
  1331.4 2.8 copy-start.20
  (20 other events, 23.8 us)
Sparse Core Ops, SparseCore 0:
  12.0 74.6 all-reduce.12
  193.5 65.9 all-gather.3
  520.1 78.4 reduce-scatter.6
  602.5 70.5 reduce-scatter.10
  676.6 128.0 reduce-scatter.12
  808.6 128.0 reduce-scatter.14
  940.4 128.0 reduce-scatter.16
  1072.5 141.6 reduce-scatter.8
  1217.2 82.7 all-reduce.14

commit v3 on v2

--- a/solution.py
+++ b/solution.py
@@ -168,30 +168,203 @@
     return jnp.transpose(shaped, (0, 2, 1, 3, 4)).reshape(count, span, groups * per_block, size)
 
 
+def scatter_kernel(cuts, lags, *refs):
+    n = len(cuts)
+    ins, outs = refs[:n], refs[n:2*n]
+    O, C, Y, X, Z, F = (refs[2*n + k*n: 2*n + (k+1)*n] for k in range(6))
+    ls, cs, cr, ys, yr, xs, xr, zs, zr, fs, fr, es, er, ws = refs[8*n:]
+    g = lax.axis_index("grp"); band = lax.axis_index("band")
+    z = g // 2; x = g % 2; y = band // 2; c = band % 2
+    far = [z, z + 1 - 2 * (z % 2), 2 - z // 2, 3 - 3 * (z // 2)]
+    ypeer = (g, (1 - y) * 2 + c); cpeer = (g, y * 2 + 1 - c); xpeer = (z * 2 + 1 - x, band)
+    bar = pltpu.get_barrier_semaphore()
+    for d in [xpeer, ypeer, cpeer] + [(zz * 2 + x, band) for zz in far[1:]]:
+        pl.semaphore_signal(bar, inc=1, device_id=d, device_id_type=MESH)
+    pl.semaphore_wait(bar, 6)
+    def at(ref, axis, start, size):
+        if axis == 0:
+            return ref.at[pl.ds(pl.multiple_of(start, 16), size), :]
+        return ref.at[:, pl.ds(pl.multiple_of(start, 128), size)]
+    def piece(i, ref):
+        axis, half, a, b = cuts[i]
+        return at(ref, axis, y * b, a + b)
+    def bpart(i, ref, yy):
+        axis, half, a, b = cuts[i]
+        return at(ref, axis, yy * (a + b), b)
+    tail = []
+    def send(src, dst, ssem, rsem, dev, cond=None):
+        d = pltpu.make_async_remote_copy(src_ref=src, dst_ref=dst, send_sem=ssem, recv_sem=rsem, device_id=dev, device_id_type=MESH)
+        if cond is None:
+            d.start(); tail.append(d.wait_send)
+            return d.wait_send
+        else:
+            pl.when(cond)(d.start); tail.append(lambda: pl.when(cond)(d.wait_send))
+    def arrived(ref, rsem):
+        pltpu.make_async_remote_copy(src_ref=ref, dst_ref=ref, send_sem=ls.at[0, 0], recv_sem=rsem, device_id=xpeer, device_id_type=MESH).wait_recv()
+    def add(dst, src):
+        rows = src.shape[0]
+        def step(r, _):
+            w = pl.ds(pl.multiple_of(r * 16, 16), 16)
+            dst[w, :] = dst[w, :] + src[w, :]
+            return 0
+        lax.fori_loop(0, rows // 16, step, 0)
+    order = [(t, j) for t in (3, 2, 1, 0) for j in (1, 0)]
+    def shard(t, j):
+        return far[t] * 2 + (1 - x if j else x)
+    seq = [(i, t, j) for i in range(n) for (t, j) in order]
+    loads, sent = {}, {}
+    for i, t, j in seq:
+        axis, half, a, b = cuts[i]
+        s = shard(t, j)
+        q = order.index((t, j))
+        send(at(ins[i].at[s], axis, (1 - c) * half, half), C[i].at[s], cs.at[i, q], cr.at[i, s], cpeer)
+        d = pltpu.make_async_copy(at(ins[i].at[s], axis, c * half, half), O[i].at[s], ls.at[i, q])
+        d.start(); loads[(i, t, j)] = d
+    def cadd(i, t, j):
+        s = shard(t, j)
+        loads[(i, t, j)].wait()
+        arrived(C[i].at[s], cr.at[i, s])
+        add(O[i].at[s], C[i].at[s])
+        sent[i, t, j] = send(bpart(i, O[i].at[s], 1 - y), Y[i].at[s], ys.at[i, order.index((t, j))], yr.at[i, s], ypeer)
+    def yadd(i, t, j):
+        s = shard(t, j)
+        arrived(Y[i].at[s], yr.at[i, s])
+        add(bpart(i, O[i].at[s], y), Y[i].at[s])
+        if j:
+            send(piece(i, O[i].at[s]), X[i].at[far[t]], xs.at[i, t], xr.at[i, far[t]], xpeer)
+    def xadd(i, t):
+        zz = far[t]
+        arrived(X[i].at[zz], xr.at[i, zz])
+        add(piece(i, O[i].at[shard(t, 0)]), X[i].at[zz])
+    def zadd(i, t):
+        zz = far[t]
+        p = piece(i, O[i].at[shard(t, 0)])
+        if t > 0:
+            inc = jnp.where(zz < z, z + 1, z - 1)
+            @pl.when((inc >= 0) & (inc <= 3))
+            def _():
+                arrived(Z[i].at[zz], zr.at[i, zz])
+                add(p, Z[i].at[zz])
+            nxt = jnp.where(zz < z, z - 1, z + 1)
+            slot = jnp.where((zz < z) & (nxt == zz), 4, zz)
+            send(p, Z[i].at[slot], zs.at[i, t - 1], zr.at[i, slot], (nxt * 2 + x, band))
+        else:
+            @pl.when(z > 0)
+            def _():
+                arrived(Z[i].at[z], zr.at[i, z])
+                add(p, Z[i].at[z])
+            @pl.when(z < 3)
+            def _():
+                arrived(Z[i].at[4], zr.at[i, 4])
+                add(p, Z[i].at[4])
+            sent[i] = send(p, F[i], fs.at[i], fr.at[i], ypeer)
+    def fin2(i):
+        axis, half, a, b = cuts[i]
+        own = O[i].at[g]
+        arrived(F[i], fr.at[i])
+        for done in (sent[i], sent[i, 0, 0]):
+            done(); tail.remove(done)
+        for yy in (0, 1):
+            @pl.when(y == 1 - yy)
+            def _():
+                add(at(own, axis, b, a), at(F[i], axis, b if yy == 0 else 0, a))
+                dst = at(own, axis, yy * (a + b), b); src = at(F[i], axis, 0 if yy == 0 else a, b)
+                def step(r, _):
+                    w = pl.ds(pl.multiple_of(r * 16, 16), 16)
+                    dst[w, :] = src[w, :]
+                    return 0
+                lax.fori_loop(0, src.shape[0] // 16, step, 0)
+        o = at(outs[i], axis, c * half, half)
+        send(own, o, es.at[i], er.at[i], cpeer)
+        d = pltpu.make_async_copy(own, o, ws.at[i]); d.start(); tail.append(d.wait)
+    ly, lx, lz, lf = lags
+    N = len(seq)
+    todo = {}
+    for q, (i, t, j) in enumerate(seq):
+        todo.setdefault(q, []).append((0, lambda a=(i, t, j): cadd(*a)))
+        todo.setdefault(q + ly, []).append((1, lambda a=(i, t, j): yadd(*a)))
+        if j == 0:
+            todo.setdefault(q + ly + lx, []).append((2, lambda a=(i, t): xadd(*a)))
+            todo.setdefault(q + ly + lx + lz, []).append((3, lambda a=(i, t): zadd(*a)))
+            if t == 0:
+                todo.setdefault(q + ly + lx + lz + lf, []).append((4, lambda i=i: fin2(i)))
+    for q in sorted(todo):
+        for _, f in sorted(todo[q], key=lambda p: p[0]):
+            f()
+    for i in range(n):
+        axis, half, a, b = cuts[i]
+        arrived(at(outs[i], axis, (1 - c) * half, half), er.at[i])
+    for w in tail:
+        w()
+
+def scatter(gs, cuts, cid=1, lags=(2, 2, 1, 2)):
+    n = len(gs)
+    S = pltpu.SemaphoreType.DMA
+    bf = jnp.bfloat16
+    def buf(lead, cut, w, size):
+        shape = (w.shape[1], size) if cut[0] == 1 else (size, w.shape[2])
+        return pltpu.VMEM(lead + shape, bf)
+    scr = [buf((8,), c, w, c[1]) for c, w in zip(cuts, gs)]
+    scr += [buf((8,), c, w, c[1]) for c, w in zip(cuts, gs)]
+    scr += [buf((8,), c, w, c[3]) for c, w in zip(cuts, gs)]
+    scr += [buf((4,), c, w, c[2] + c[3]) for c, w in zip(cuts, gs)]
+    scr += [buf((5,), c, w, c[2] + c[3]) for c, w in zip(cuts, gs)]
+    scr += [buf((), c, w, c[2] + c[3]) for c, w in zip(cuts, gs)]
+    return pl.pallas_call(
+        functools.partial(scatter_kernel, cuts, lags),
+        out_shape=[jax.ShapeDtypeStruct(w.shape[1:], bf) for w in gs],
+        in_specs=[pl.BlockSpec(memory_space=pl.ANY)] * n,
+        out_specs=[pl.BlockSpec(memory_space=pl.ANY)] * n,
+        scratch_shapes=scr + [S((n, 8)), S((n, 8)), S((n, 8)), S((n, 8)), S((n, 8)), S((n, 4)), S((n, 4)), S((n, 3)), S((n, 5)), S((n,)), S((n,)), S((n,)), S((n,)), S((n,))],
+        compiler_params=pltpu.CompilerParams(collective_id=cid, has_side_effects=True, vmem_limit_bytes=60 * 2**20),
+        name="gradient_scatter",
+    )(*gs)
+
+
 def half_cuts(axis, size, own_parts, shared_parts):
     unit = size // 2 // (own_parts + 2 * shared_parts)
     return (axis, size // 2, own_parts * unit, shared_parts * unit)
 
 
-def gather_weights(shards):
-    rows, wide = shards[0].shape
-    fits = (
+def fits(rows, wide, widest, deep):
+    return (
         lax.axis_size("grp") == 8
         and lax.axis_size("band") == 4
         and rows % 16 == 0
-        and shards[2].shape[0] % 96 == 0
-        and wide % 768 == 0
-        and shards[1].shape[1] % 768 == 0
-    )
-    if not fits:
+        and wide % 4608 == 0
+        and widest % 1024 == 0
+        and deep % 384 == 0
+    )
+
+
+def gather_weights(shards):
+    rows, wide = shards[0].shape
+    widest, deep = shards[1].shape[1], shards[2].shape[0]
+    if not fits(rows, wide, widest, deep):
         return [lax.all_gather(w, "grp", axis=0, tiled=True) for w in shards]
     cuts = (
         half_cuts(1, wide, 1, 1),
-        half_cuts(1, shards[1].shape[1], 1, 1),
-        half_cuts(0, shards[2].shape[0], 1, 1),
+        half_cuts(1, widest, 1, 1),
+        half_cuts(0, deep, 1, 1),
     )
     full = gather(shards, cuts)
     return [w.reshape(-1, w.shape[-1]) for w in full]
+
+
+def scatter_grads(grads):
+    parts = lax.axis_size("grp")
+    split = [w.reshape(parts, w.shape[0] // parts, w.shape[1]) for w in grads]
+    rows, wide = split[0].shape[1:]
+    widest, deep = split[1].shape[2], split[2].shape[1]
+    if not fits(rows, wide, widest, deep):
+        shards = [lax.psum_scatter(w, "grp", scatter_dimension=0, tiled=True) for w in grads]
+        return [lax.psum(w, "band") for w in shards]
+    cuts = (
+        half_cuts(1, wide, 8, 5),
+        half_cuts(1, widest, 2, 1),
+        half_cuts(0, deep, 2, 1),
+    )
+    return scatter([split[k] for k in (2, 1, 0)], [cuts[k] for k in (2, 1, 0)])[::-1]
 
 
 def body(
@@ -225,7 +398,7 @@
     )
     qp_all, gu_all, down_all = gather_weights(shards)
     qkv_all, proj_all = qp_all[:, : w_qkv.shape[1]], qp_all[:, w_qkv.shape[1] :]
-    gate_all, up_all = gu_all[:, : w_gate.shape[1]], gu_all[:, w_gate.shape[1] :]
+    ff = w_gate.shape[1]
     onehot = (group_ids[:, None] == jnp.arange(GROUPS, dtype=jnp.int32)[None, :]).astype(
         jnp.float32
     )
@@ -298,8 +471,8 @@
     middle = x_flat + gate_one[:, None, :] * proj
     normed_two, norm_two_pull = jax.vjp(modulate, middle, shift_two, scale_two)
     normed_two_low = normed_two.astype(jnp.bfloat16).reshape(images * length, width)
-    gate_pre = jnp.dot(normed_two_low, gate_all, preferred_element_type=jnp.float32)
-    up_pre = jnp.dot(normed_two_low, up_all, preferred_element_type=jnp.float32)
+    pre = jnp.dot(normed_two_low, gu_all, preferred_element_type=jnp.float32)
+    gate_pre, up_pre = pre[:, :ff], pre[:, ff:]
     hidden, swiglu_pull = jax.vjp(swiglu, gate_pre, up_pre)
     hidden_low = hidden.astype(jnp.bfloat16)
     mlp = jnp.dot(hidden_low, down_all, preferred_element_type=jnp.float32).reshape(
@@ -313,16 +486,11 @@
     d_w_down = jnp.einsum("tf,td->fd", hidden_low, d_mlp, preferred_element_type=jnp.float32)
     d_hidden = jnp.einsum("td,fd->tf", d_mlp, down_all, preferred_element_type=jnp.float32)
     d_gate_pre, d_up_pre = swiglu_pull(d_hidden)
-    d_gate_low = d_gate_pre.astype(jnp.bfloat16)
-    d_up_low = d_up_pre.astype(jnp.bfloat16)
-    d_w_gate = jnp.einsum(
-        "td,tf->df", normed_two_low, d_gate_low, preferred_element_type=jnp.float32
-    )
-    d_w_up = jnp.einsum("td,tf->df", normed_two_low, d_up_low, preferred_element_type=jnp.float32)
-    d_normed_two = jnp.einsum("tf,df->td", d_gate_low, gate_all, preferred_element_type=jnp.float32)
-    d_normed_two = d_normed_two + jnp.einsum(
-        "tf,df->td", d_up_low, up_all, preferred_element_type=jnp.float32
-    )
+    d_pre_low = jnp.concatenate(
+        [d_gate_pre.astype(jnp.bfloat16), d_up_pre.astype(jnp.bfloat16)], axis=1
+    )
+    d_w_gu = jnp.einsum("td,tf->df", normed_two_low, d_pre_low, preferred_element_type=jnp.float32)
+    d_normed_two = jnp.einsum("tf,df->td", d_pre_low, gu_all, preferred_element_type=jnp.float32)
     d_middle_norm, d_shift_two, d_scale_two = norm_two_pull(
         d_normed_two.reshape(images, length, width)
     )
@@ -412,25 +580,28 @@
     d_cond = lax.all_gather(d_cond_rows, "grp", axis=1, tiled=True)
     d_q_gain, d_k_gain = lax.psum((d_q_gain, d_k_gain), ("grp", "band"))
 
-    def spread(grad):
-        shard = lax.psum_scatter(
-            grad.astype(jnp.bfloat16), "grp", scatter_dimension=0, tiled=True
-        )
-        return lax.psum(shard, "band").astype(jnp.float32)
-
+    d_w_qp = jnp.concatenate(
+        [d_w_qkv.astype(jnp.bfloat16), d_w_proj.astype(jnp.bfloat16)], axis=1
+    )
+    d_qp, d_gu, d_down = (
+        w.astype(jnp.float32)
+        for w in scatter_grads(
+            (d_w_qp, d_w_gu.astype(jnp.bfloat16), d_w_down.astype(jnp.bfloat16))
+        )
+    )
     return (
         patches_out,
         d_patches,
         d_cond,
         d_w_ada,
         d_b_ada,
-        spread(d_w_qkv),
+        d_qp[:, : w_qkv.shape[1]],
         d_q_gain,
         d_k_gain,
-        spread(d_w_proj),
-        spread(d_w_gate),
-        spread(d_w_up),
-        spread(d_w_down),
+        d_qp[:, w_qkv.shape[1] :],
+        d_gu[:, :ff],
+        d_gu[:, ff:],
+        d_down,
     )
 
 

time: 1350 us -> 945 us (0.70)
  waiting for transfers between devices: 656 us -> 104 us
  Pallas kernels: 141 us -> 301 us
  matrix products: 264 us -> 247 us
    reduce_scatter x5 -> x0, waiting for transfers between devices: 564 us -> none  [spread(): lax.psum_scatter(grad.astype(jnp.bfloat16), 'grp', scatter_dimension=0, t...]
    pallas_call x0 -> x1, Pallas kernels: none -> 160 us  [scatter(): pl.pallas_call(functools.partial(scatter_kernel, cuts, lags), out_shape=[...]
    dot_general x6 -> x3, matrix products: 66.9 us -> 43.3 us  [the longest x1 16.5 us: body(): jnp.einsum('tf,df->td', d_pre_low, gu_all, preferred_element_type=jnp.flo...]
  transfers between devices with their start and end apart: 9 -> 3, of which waited for: 7 -> 2; matrix products, arithmetic and copies ran while one was open for 9% -> 7% of each run, Pallas kernels for 11% -> 15%
where the time goes in v3:
time: 945 us; the launch traced here: 934 us
  Pallas kernels  301 us (32%)
  matrix products  247 us (26%)
  blocking collectives  111 us (12%)
  waiting for transfers between devices  104 us (11%)
  local copies, waits for them, and re-layouts  84.8 us (9%)
  other arithmetic  69.2 us (7%)
  between operations  16.1 us (2%)
    pallas_call x1, Pallas kernels, scatter(): pl.pallas_call(functools.partial(scatter_kernel, cuts, lags), out_shape=[...  160 us
    pallas_call x1, Pallas kernels, gather(): pl.pallas_call(functools.partial(gather_kernel, cuts, when_own), out_shap...  141 us
    all_gather x1, waiting for transfers between devices, body(): kv_rows = lax.all_gather(kv_local, 'band', axis=1, tiled=True)  52.6 us
    reduce_scatter x1, waiting for transfers between devices, body(): lax.psum_scatter(kv_terms.astype(jnp.bfloat16), 'band', scatter_dimension...  51.3 us
    psum x1, blocking collectives, body(): d_q_gain, d_k_gain = lax.psum((d_q_gain, d_k_gain), ('grp', 'band'))  36.8 us
    all_gather x1, blocking collectives, body(): payload = lax.all_gather(payload, 'grp', axis=0, tiled=True)  33.1 us
    all_gather x1, blocking collectives, body(): d_cond = lax.all_gather(d_cond_rows, 'grp', axis=1, tiled=True)  30.5 us
    dot_general x8, matrix products, forward_block(): jnp.einsum('hqk,khd->qhd', probs_low, value_part, preferred_element_type=...  23.3 us
  transfers between devices with their start and end apart: 3, of which 2 were waited for; matrix products, arithmetic and copies ran while one was open for 7% of the time, Pallas kernels for 15%

profile of v3, /device:TPU:0, one launch (start us, length us, event | category | flops | bytes accessed | tf_op | source)
XLA Modules:
  0.0 933.9 jit_solution(3700596231602808980)
XLA Ops:
  15.4 141.1 %weight_gather.1 = (bf16[8,144,4608]{2,1,0:T(8,128)(2,1)}, bf16[8,144,6144]{2,1,0:T(8,128)(2,1)}, bf16[8,384,1152]{2,1,0:T(8,128)(2,1)}) custom-call(bf16[144,4608]{1,0:T(8,128)(2,1)} %pad_maximum_fusion.8.refs_0_, bf16[144,6144]{1,0:T(8,128)(2,1)} %pad_maximum_fusion.5.refs_1_, bf16[384,1152]{1,0:T(8,128)(2,1)} %refs_2_.1), custom_call_target="tpu_custom_call" | custom-call | tf_op jit(solution)/shard_map/weight_gather/pallas_call | solution.py:101
  156.5 6.9 slice_bitcast_fusion
  163.4 11.4 %copy.71 = bf16[3456,1152]{1,0:T(8,128)(2,1)} copy(bf16[3456,1152]{0,1:T(8,128)(2,1)} %slice_bitcast_fusion) | data formatting | bytes 15925248 | tf_op jit(solution)/shard_map/dot_general | solution.py:429
  178.3 7.3 fusion.104
  200.0 4.0 reshape.474
  204.0 2.8 copy.74
  206.8 52.6 %all-gather.4.cloned.1.call-done = bf16[2,1024,2304]{1,2,0:T(8,128)(2,1)} async-done(((bf16[2,256,2304]{1,2,0:T(8,128)(2,1)}), bf16[2,1024,2304]{1,2,0:T(8,128)(2,1)}) %all-gather.4.cloned.1.call-update) | async-done | bytes 9437200 | tf_op jit(solution)/shard_map/all_gather | solution.py:444
  259.4 8.5 fusion.100
  267.9 46.7 %while.26 = (s32[]{:T(128)}, bf16[8,256,4,72]{1,3,2,0:T(8,128)(2,1)}, f32[8,4,256,1]{2,1,3,0:T(4,128)S(1)}, bf16[8,1024,4,72]{1,3,2,0:T(8,128)(2,1)}, bf16[8,256...) while((s32[]{:T(128)}, bf16[8,256,4,72]{1,3,2,0:T(8,128)(2,1)}, ...), condition=%wide.region_7.8_spmd, body=%wide.region_4.7_spmd.sunk | while | flops 311499776 | bytes 14092377 | solution.py:466
  270.8 2.9 fusion.146
  276.6 2.9 fusion.146
  282.4 2.9 fusion.146
  288.3 2.9 fusion.146
  294.1 2.9 fusion.146
  300.0 2.9 fusion.146
  305.8 2.9 fusion.146
  311.6 2.9 fusion.146
  314.6 5.8 multiply_reduce_fusion.10
  321.7 15.0 %fusion.105 = f32[512,6144]{1,0:T(8,128)} fusion(bf16[512,1152]{1,0:T(8,128)(2,1)S(1)} %bitcast.316, bf16[1152,6144]{1,0:T(8,128)(2,1)} %bitcast.323), kind=kOutput, calls=%fused_computation.217 | convolution fusion | flops 7247757312 | bytes 27918336 | tf_op jit(solution)/shard_map/dot_general | solution.py:474
  336.7 12.9 %fusion.58 = (bf16[512,3072]{1,0:T(8,128)(2,1)S(1)}, bf16[512,3072]{1,0:T(8,128)(2,1)S(1)}, bf16[512,3072]{1,0:T(8,128)(2,1)}) fusion(f32[512,6144]{1,0:T(8,128)} %fusion.105, bf16[512,1152]{1,0:T(8,128)(2,1)S(1)} %bitcast.320, bf16[3072,1152]{1,0:T(8,128)(2,1)} %bitcast.325), kind=kOutput, calls=%fused_computation.73 | convolution fusion | flops 3649044480 | bytes 30277632 | tf_op jit(solution)/shard_map/td,fd->tf/dot_general | solution.py:487
  349.6 3.5 pad_maximum_fusion.2
  354.1 16.5 %multiply_reduce_fusion.5 = (f32[2,1152]{1,0:T(2,128)S(1)}, f32[2,256]{1,0:T(2,128)S(1)}, f32[2,1152]{1,0:T(2,128)S(1)}, f32[2,256,1152]{2,1,0:T(8,128)}) fusion(f32[2,256,1152]{2,1,0:T(8,128)} %copy-done.20, f32[2,256]{1,0:T(2,128)S(1)} %fusion.94, f32[2,1152]{1,0:T(2,128)S(1)} %get-tuple-element.258, bf16[2,256,6144]{2,1,0:T(8,128)(2,1)} %bitcast.296, ...), kind=kOutput, calls=%fused_computation.118 | convolution fusion | flops 7251880960 | bytes 25197568 | tf_op jit(solution)/shard_map/tf,df->td/dot_general | solution.py:493
  370.6 11.8 %multiply_reduce_fusion.4 = (f32[2,1152]{1,0:T(2,128)S(1)}, bf16[2,256,1152]{2,1,0:T(8,128)(2,1)}, f32[2,1152]{1,0:T(2,128)S(1)}, f32[2,256,1152]{2,1,0:T(8,128)S(1)}) fusion(bf16[2,8,32,1152]{3,2,1,0:T(8,128)(2,1)S(1)} %copy-done.11, f32[2]{0:T(128)S(1)} %compare_convert_fusion.1, f32[2,256,1152]{2,1,0:T(8,128)} %copy-done.20, ...), kind=kOutput, calls=%fused_computation.117 | convolution fusion | flops 3633311232 | bytes 22061064 | tf_op jit(solution)/shard_map/dot_general | solution.py:478
  385.0 4.7 convolution_convert_fusion.3
  393.9 96.7 %while.27 = (s32[]{:T(128)}, f32[8,256,4,72]{1,3,2,0:T(8,128)}, bf16[8,1024,4,72]{1,3,2,0:T(8,128)(2,1)}, bf16[8,1024,4,72]{1,3,2,0:T(8,128)(2,1)}, bf16[8,1024,...) while((s32[]{:T(128)}, f32[8,256,4,72]{1,3,2,0:T(8,128)}, ...), condition=%wide.region_12.13_spmd, body=%wide.region_10.12_spmd.sunk | while | flops 767925248 | bytes 36504688 | solution.py:531
  490.6 6.8 copy.80
  497.4 6.7 copy.79
  504.1 9.2 pad_maximum_fusion.1
  518.9 3.5 convolution_convert_fusion.2
  522.3 6.4 convolution_convert_fusion.1
  528.8 11.9 %convolution_convert_fusion = bf16[1152,6144]{1,0:T(8,128)(2,1)} fusion(bf16[512,1152]{1,0:T(8,128)(2,1)} %bitcast.317, bf16[512,3072]{1,0:T(8,128)(2,1)S(1)} %copy-done.17, bf16[512,3072]{1,0:T(8,128)(2,1)S(1)} %copy-done.15), kind=kOutput, calls=%fused_computation.58 | convolution fusion | flops 7267418112 | bytes 21626880 | tf_op jit(solution)/shard_map/td,tf->df/dot_general | solution.py:492
  540.7 51.3 %reduce-scatter.2.cloned.1.call-done = bf16[2,256,2304]{2,1,0:T(8,128)(2,1)} async-done(((bf16[2,1024,2304]{2,1,0:T(8,128)(2,1)}), bf16[2,256,2304]{2,1,0:T(8,128)(2,1)}) %reduce-scatter.2.cloned.1.call-update) | async-done | bytes 2359312 | tf_op jit(solution)/shard_map/reduce_scatter | solution.py:538
  591.9 3.7 slice_convert_fusion.1
  595.6 3.0 copy.81
  598.7 2.7 multiply_add_fusion.3
  601.5 4.1 multiply_reduce_fusion.3
  605.7 3.5 fusion.63
  614.0 11.2 %fusion.69 = (f32[2,1152]{1,0:T(2,128)S(1)}, f32[2,256]{1,0:T(2,128)S(1)}, f32[2,1152]{1,0:T(2,128)S(1)}, bf16[2,256,1152]{2,1,0:T(8,128)(2,1)}, f32[2,256,1152]{2,1,0:T(8,128)}) fusion(bf16[2,8,32,1152]{3,2,1,0:T(8,128)(2,1)S(1)} %copy-done.3, f32[2,256]{1,0:T(2,128)S(1)} %rsqrt.47, f32[2,1152]{1,0:T(2,128)S(1)} %copy-done.46, ...), kind=kOutput, calls=%fused_computation.107 | convolution fusion | flops 4093963264 | bytes 16261120 | tf_op jit(solution)/shard_map/te,de->td/dot_general | solution.py:554
  625.3 10.7 %psum.29 = bf16[2,6912]{1,0:T(2,128)(2,1)S(1)} all-reduce(f32[2,6912]{1,0:T(2,128)S(1)} %constant_dynamic-update-slice_fusion), channel_id=1, replica_groups=mesh['grp'=8,'band'=4] {'band'}, use_global_device_ids=true, to_apply=%region_23.24 | all-reduce | flops 13824 | bytes 82944 | tf_op jit(solution)/shard_map/psum | solution.py:560
  636.0 33.1 %all-gather = bf16[8,2,6920]{2,1,0:T(2,128)(2,1)} all-gather(bf16[1,2,6920]{2,1,0:T(2,128)(2,1)S(1)} %maximum_bitcast_fusion), channel_id=1, replica_groups=mesh['grp'=8,'band'=4] {'grp'}, dimensions={0}, use_global_device_ids=true | all-gather | bytes 249120 | tf_op jit(solution)/shard_map/all_gather | solution.py:562
  670.8 3.6 fusion.79
  674.6 7.0 fusion.52
  681.6 4.5 pad_maximum_fusion
  686.1 159.7 %gradient_scatter.1 = (bf16[384,1152]{1,0:T(8,128)(2,1)}, bf16[144,6144]{1,0:T(8,128)(2,1)}, bf16[144,4608]{1,0:T(8,128)(2,1)}) custom-call(bf16[8,384,1152]{2,1,0:T(8,128)(2,1)} %bitcast.295, bf16[8,144,6144]{2,1,0:T(8,128)(2,1)} %bitcast.291, bf16[8,144,4608]{2,1,0:T(8,128)(2,1)} %bitcast.289), custom_call_target="tpu_custom_call" | custom-call | tf_op jit(solution)/shard_map/gradient_scatter/pallas_call | solution.py:313
  845.9 2.7 slice.146
  850.4 30.5 %all-gather.1 = f32[8,144,8]{1,2,0:T(8,128)S(1)} all-gather(f32[1,144,8]{1,2,0:T(8,128)S(1)} %fusion.87), channel_id=1, replica_groups=mesh['grp'=8,'band'=4] {'grp'}, dimensions={0}, use_global_device_ids=true | all-gather | bytes 41472 | tf_op jit(solution)/shard_map/all_gather | solution.py:580
  882.3 3.8 fusion.101
  890.4 36.8 %all-reduce.8 = (f32[72]{0:T(128)}, f32[72]{0:T(128)}) all-reduce(f32[72]{0:T(128)S(1)} %get-tuple-element.158, f32[72]{0:T(128)S(1)} %get-tuple-element.216), channel_id=1, replica_groups=mesh['grp'=8,'band'=4] {'grp','band'}, use_global_device_ids=true, to_apply=%region_26.27 | all-reduce | flops 144 | bytes 1152 | tf_op jit(solution)/shard_map/psum | solution.py:581
  (284 shorter events, 173.2 us)
Async XLA Ops:
  7.2 3.5 copy-start.54
  7.2 3.6 copy-start.2
  7.2 4.5 copy-start.40
  7.2 168.8 %all-reduce.11.cloned.1.call-start = ((), (), s32[]{:S(2)}) async-start(), calls=%async_computation.1 | async-start | bytes 442368 | tf_op jit(solution)/shard_map/psum | solution.py:415
  10.6 248.8 %all-gather.4.cloned.1.call-start = ((), (), s32[]{:S(2)}) async-start(), calls=%async_computation.2 | async-start | bytes 11796480 | tf_op jit(solution)/shard_map/all_gather | solution.py:444
  10.7 3.4 copy-start.25
  10.7 3.4 copy-start.26
  175.9 18.4 %copy-start.28 = (f32[256,18]{0,1:T(8,128)}, f32[256,18]{0,1:T(8,128)S(1)}, u32[]{:S(2)}) copy-start(f32[256,18]{0,1:T(8,128)S(1)} %get-tuple-element.264) | copy-start | bytes 55300
  175.9 18.4 %copy-start.30 = (f32[256,18]{0,1:T(8,128)}, f32[256,18]{0,1:T(8,128)S(1)}, u32[]{:S(2)}) copy-start(f32[256,18]{0,1:T(8,128)S(1)} %get-tuple-element.265) | copy-start | bytes 55300
  175.9 18.4 %copy-start.32 = (f32[256,18]{0,1:T(8,128)}, f32[256,18]{0,1:T(8,128)S(1)}, u32[]{:S(2)}) copy-start(f32[256,18]{0,1:T(8,128)S(1)} %get-tuple-element.268) | copy-start | bytes 55300
  175.9 18.4 %copy-start.34 = (f32[256,18]{0,1:T(8,128)}, f32[256,18]{0,1:T(8,128)S(1)}, u32[]{:S(2)}) copy-start(f32[256,18]{0,1:T(8,128)S(1)} %get-tuple-element.269) | copy-start | bytes 55300
  185.6 2.9 copy-start.1
  185.7 2.8 copy-start.50
  185.8 2.7 copy-start.52
  186.3 4.2 copy-start.36
  188.5 2.0 copy-start.38
  193.3 398.6 %reduce-scatter.2.cloned.1.call-start = ((), (), s32[]{:S(2)}) async-start(), calls=%async_computation.3 | async-start | bytes 11796480 | tf_op jit(solution)/shard_map/reduce_scatter | solution.py:538
  314.5 5.8 copy-start.10
  321.7 15.0 %copy-start.22 = (bf16[2,256,1152]{2,1,0:T(8,128)(2,1)}, bf16[2,256,1152]{2,1,0:T(8,128)(2,1)S(1)}, u32[]{:S(2)}) copy-start(bf16[2,256,1152]{2,1,0:T(8,128)(2,1)S(1)} %get-tuple-element.274) | copy-start | bytes 3538948
  349.6 3.6 copy-start.14
  349.6 4.5 copy-start.16
  354.1 16.5 %copy-start.11 = (bf16[2,8,32,1152]{3,2,1,0:T(8,128)(2,1)S(1)}, bf16[2,8,32,1152]{3,2,1,0:T(8,128)(2,1)}, u32[]{:S(2)}) copy-start(bf16[2,8,32,1152]{3,2,1,0:T(8,128)(2,1)} %param.20) | copy-start | bytes 3538948
  515.4 1.7 copy-start.29
  515.4 1.7 copy-start.31
  515.4 1.7 copy-start.33
  517.1 1.8 copy-start.24
  518.9 3.5 copy-start.56
  522.3 6.4 copy-start.15
  522.3 6.4 copy-start.17
  598.6 2.8 copy-start.6
  598.6 2.8 copy-start.7
  598.6 2.8 copy-start.37
  598.6 2.8 copy-start.39
  598.6 2.8 copy-start.51
  598.6 2.8 copy-start.53
  598.7 7.0 slice-start
  601.5 4.1 copy-start.44
  601.5 4.1 copy-start.42
  601.5 4.2 slice-start.1
  601.5 4.2 copy-start.8
  609.1 4.8 copy-start.3
  609.1 4.8 copy-start.46
  609.1 4.8 copy-start.48
  674.6 7.0 copy-start.18
  845.9 2.7 copy-start.9
  882.3 3.8 copy-start.27
  882.3 5.1 copy-start.19
  886.1 2.3 copy-start.5
  (14 other events, 16.3 us)
Sparse Core Ops, SparseCore 0:
  12.0 74.6 all-reduce.10
  193.4 65.9 all-gather.3
  513.5 78.3 reduce-scatter.1

commit v4 on v1

v4 whole, which is shorter than its diff:
```python
import functools

import jax
import jax.numpy as jnp
from jax import lax
from jax.experimental import pallas as pl
from jax.experimental.pallas import tpu as pltpu
from jax.sharding import PartitionSpec as P

HEADS = 16
HDIM = 72
GROUPS = 8
LANES = 128
EPS = 1e-06
LOG2E = 1.4426950408889634

MESH = pl.DeviceIdType.MESH


class Place:
    def __init__(self):
        self.g, self.band = lax.axis_index("grp"), lax.axis_index("band")
        self.z, self.x = self.g // 2, self.g % 2
        self.y, self.c = self.band // 2, self.band % 2
        z = self.z
        self.far = [z, z + 1 - 2 * (z % 2), 2 - z // 2, 3 - 3 * (z // 2)]
        self.ypeer = (self.g, (1 - self.y) * 2 + self.c)
        self.cpeer = (self.g, self.y * 2 + 1 - self.c)
        self.xpeer = (z * 2 + 1 - self.x, self.band)
        self.draining = False

    def line(self, zz):
        return (zz * 2 + self.x, self.band)

    def greet(self, peers):
        bar = pltpu.get_barrier_semaphore()
        for d in peers:
            pl.semaphore_signal(bar, inc=1, device_id=d, device_id_type=MESH)
        pl.semaphore_wait(bar, len(peers))

    def greet_band(self):
        self.greet([self.ypeer, self.cpeer])

    def greet_all(self):
        self.greet([self.xpeer, self.ypeer, self.cpeer] + [self.line(zz) for zz in self.far[1:]])

    def copy(self, src, dst, ssem, rsem, dev):
        return pltpu.make_async_remote_copy(
            src_ref=src, dst_ref=dst, send_sem=ssem, recv_sem=rsem, device_id=dev, device_id_type=MESH
        )

    def send(self, src, dst, ssem, rsem, dev, cond=None):
        d = self.copy(src, dst, ssem, rsem, dev)
        act = d.wait_send if self.draining else d.start
        if cond is None:
            act()
        else:
            pl.when(cond)(act)

    def keep(self, src, dst, sem):
        d = pltpu.make_async_copy(src, dst, sem)
        d.wait() if self.draining else d.start()

    def arrived(self, ref, rsem):
        if not self.draining:
            self.copy(ref, ref, rsem, rsem, self.ypeer).wait_recv()

    def drain(self, steps):
        self.draining = True
        for step in steps:
            step()
        self.draining = False


def span(ref, axis, start, size):
    if axis == 0:
        return ref.at[pl.ds(pl.multiple_of(start, 16), size), :]
    return ref.at[:, pl.ds(pl.multiple_of(start, LANES), size)]


def gather_sems(n):
    s = pltpu.SemaphoreType.DMA
    return [s((n,)), s((n, 4)), s((n, 4)), s((n, 4)), s((n, 4)), s((n, 7)), s((n, 7)), s((n, 14)), s((n, 14)), s((n,))]


def gather_steps(at, cuts, ins, outs, sems):
    n = len(cuts)
    lsem, zs, zr, xs, xr, ys, yr, cs, cr, ds = sems
    x, y, z, c, far = at.x, at.y, at.z, at.c, at.far

    def piece(i, ref, yy, cc):
        axis, half, a, b = cuts[i]
        return span(ref, axis, cc * half + yy * b, a + b)

    def bpart(i, ref, yy, cc):
        axis, half, a, b = cuts[i]
        return span(ref, axis, cc * half + yy * (a + b), b)

    def own(i):
        src, dst = piece(i, ins[i], y, c), piece(i, outs[i].at[at.g], y, c)
        at.send(src, dst, zs.at[i, 0], zr.at[i, z], (at.g + 2, at.band), z < 3)
        at.send(src, dst, ds.at[i], zr.at[i, z], (at.g - 2, at.band), z > 0)
        at.send(src, dst, xs.at[i, 0], xr.at[i, 0], at.xpeer)
        at.keep(ins[i], outs[i].at[at.g], lsem.at[i])

    def down(i, slot, shard):
        p = bpart(i, outs[i].at[shard], y, c)
        at.send(p, p, ys.at[i, slot], yr.at[i, slot], at.ypeer)
        p = piece(i, outs[i].at[shard], y, c)
        at.send(p, p, cs.at[i, slot], cr.at[i, slot], at.cpeer)

    def zarr(i, t):
        zz = far[t]
        s = zz * 2 + x
        p = piece(i, outs[i].at[s], y, c)
        at.arrived(p, zr.at[i, zz])
        nxt = jnp.where(zz < z, z + 1, z - 1)
        at.send(p, p, zs.at[i, t], zr.at[i, zz], at.line(jnp.clip(nxt, 0, 3)), (nxt >= 0) & (nxt <= 3))
        at.send(p, p, xs.at[i, t], xr.at[i, t], at.xpeer)
        down(i, t - 1, s)

    def xarr(i, t):
        s = far[t] * 2 + 1 - x
        at.arrived(piece(i, outs[i].at[s], y, c), xr.at[i, t])
        down(i, 3 + t, s)

    def yarr(i, slot, s):
        p = bpart(i, outs[i].at[s], 1 - y, c)
        at.arrived(p, yr.at[i, slot])
        at.send(p, p, cs.at[i, 7 + slot], cr.at[i, 7 + slot], at.cpeer)

    slots = [(t - 1, far[t] * 2 + x) for t in (1, 2, 3)]
    slots += [(3 + t, far[t] * 2 + 1 - x) for t in range(4)]
    order = [slots[k] for k in (3, 0, 4, 1, 5, 2, 6)]
    steps = [lambda: own(0)]
    for i in range(n):
        steps.append(lambda i=i: zarr(i, 1))
        if i + 1 < n:
            steps.append(lambda i=i: own(i + 1))
        rest = [lambda i=i: xarr(i, 0)]
        for t in (2, 3):
            rest += [lambda i=i, t=t: zarr(i, t), lambda i=i, t=t: xarr(i, t - 1)]
        rest.append(lambda i=i: xarr(i, 3))
        for k, step in enumerate(rest):
            if i > 0:
                steps.append(lambda i=i, k=k: yarr(i - 1, *order[k]))
            steps.append(step)
        if i > 0:
            steps.append(lambda i=i: yarr(i - 1, *order[6]))
    steps += [lambda k=k: yarr(n - 1, *order[k]) for k in range(7)]

    def last():
        for i in range(n):
            for slot, s in slots:
                at.arrived(piece(i, outs[i].at[s], y, 1 - c), cr.at[i, slot])
                at.arrived(bpart(i, outs[i].at[s], 1 - y, 1 - c), cr.at[i, 7 + slot])

    return steps, last


def gather_kernel(cuts, *refs):
    n = len(cuts)
    at = Place()
    at.greet_all()
    steps, last = gather_steps(at, cuts, refs[:n], refs[n : 2 * n], refs[2 * n :])
    for step in steps:
        step()
    last()
    at.drain(steps)


def gather(ws, cuts):
    n = len(ws)
    return pl.pallas_call(
        functools.partial(gather_kernel, cuts),
        out_shape=[jax.ShapeDtypeStruct((8,) + w.shape, w.dtype) for w in ws],
        in_specs=[pl.BlockSpec(memory_space=pl.ANY)] * n,
        out_specs=[pl.BlockSpec(memory_space=pl.ANY)] * n,
        scratch_shapes=gather_sems(n),
        compiler_params=pltpu.CompilerParams(collective_id=0, has_side_effects=True),
        name="weight_gather",
    )(*ws)
def add_into(dst, src):
    def step(r, _):
        rows = pl.ds(pl.multiple_of(r * 16, 16), 16)
        dst[rows, :] = dst[rows, :] + src[rows, :]
        return 0

    lax.fori_loop(0, src.shape[0] // 16, step, 0)


def move_into(dst, src):
    def step(r, _):
        rows = pl.ds(pl.multiple_of(r * 16, 16), 16)
        dst[rows, :] = src[rows, :]
        return 0

    lax.fori_loop(0, src.shape[0] // 16, step, 0)


def scatter_scratch(grads, cuts):
    n = len(cuts)
    s = pltpu.SemaphoreType.DMA

    def buf(lead, k, size):
        shape = (grads[k].shape[1], size) if cuts[k][0] == 1 else (size, grads[k].shape[2])
        return pltpu.VMEM(lead + shape, jnp.bfloat16)

    out = []
    for lead, pick in (
        ((8,), lambda c: c[1]),
        ((8,), lambda c: c[1]),
        ((8,), lambda c: c[3]),
        ((4,), lambda c: c[2] + c[3]),
        ((5,), lambda c: c[2] + c[3]),
        ((), lambda c: c[2] + c[3]),
    ):
        out += [buf(lead, k, pick(cuts[k])) for k in range(n)]
    out += [s((n, 8))] * 5 + [s((n, 4))] * 2 + [s((n, 3)), s((n, 5))] + [s((n,))] * 5
    return out


def scatter_steps(at, cuts, ins, outs, scratch, lags):
    n = len(cuts)
    own_half, core_buf, y_buf, x_buf, z_buf, fin_buf = (scratch[k * n : (k + 1) * n] for k in range(6))
    ls, cs, cr, ys, yr, xs, xr, zs, zr, fs, fr, es, er, ws = scratch[6 * n :]
    x, y, z, c, far = at.x, at.y, at.z, at.c, at.far

    def piece(i, ref):
        _, _, a, b = cuts[i]
        return span(ref, cuts[i][0], y * b, a + b)

    def bpart(i, ref, yy):
        _, _, a, b = cuts[i]
        return span(ref, cuts[i][0], yy * (a + b), b)

    order = [(t, j) for t in (3, 2, 1, 0) for j in (1, 0)]

    def shard(t, j):
        return far[t] * 2 + (1 - x if j else x)

    def load(i, t, j):
        axis, half, _, _ = cuts[i]
        s, q = shard(t, j), order.index((t, j))
        return pltpu.make_async_copy(span(ins[i].at[s], axis, c * half, half), own_half[i].at[s], ls.at[i, q])

    def give(i, t, j):
        axis, half, _, _ = cuts[i]
        s, q = shard(t, j), order.index((t, j))
        src = span(ins[i].at[s], axis, (1 - c) * half, half)
        at.send(src, core_buf[i].at[s], cs.at[i, q], cr.at[i, s], at.cpeer)
        if not at.draining:
            load(i, t, j).start()

    def to_y(i, t, j):
        s = shard(t, j)
        src = bpart(i, own_half[i].at[s], 1 - y)
        return at.copy(src, y_buf[i].at[s], ys.at[i, order.index((t, j))], yr.at[i, s], at.ypeer)

    def to_fin(i):
        return at.copy(piece(i, own_half[i].at[at.g]), fin_buf[i], fs.at[i], fr.at[i], at.ypeer)

    def cadd(i, t, j):
        s = shard(t, j)
        if at.draining:
            if (t, j) != (0, 0):
                to_y(i, t, j).wait_send()
            return
        load(i, t, j).wait()
        at.arrived(core_buf[i].at[s], cr.at[i, s])
        add_into(own_half[i].at[s], core_buf[i].at[s])
        to_y(i, t, j).start()

    def yadd(i, t, j):
        s = shard(t, j)
        at.arrived(y_buf[i].at[s], yr.at[i, s])
        if not at.draining:
            add_into(bpart(i, own_half[i].at[s], y), y_buf[i].at[s])
        if j:
            at.send(piece(i, own_half[i].at[s]), x_buf[i].at[far[t]], xs.at[i, t], xr.at[i, far[t]], at.xpeer)

    def xadd(i, t):
        if at.draining:
            return
        at.arrived(x_buf[i].at[far[t]], xr.at[i, far[t]])
        add_into(piece(i, own_half[i].at[shard(t, 0)]), x_buf[i].at[far[t]])

    def zadd(i, t):
        zz = far[t]
        p = piece(i, own_half[i].at[shard(t, 0)])

        def join(cond, slot):
            def do():
                at.arrived(z_buf[i].at[slot], zr.at[i, slot])
                add_into(p, z_buf[i].at[slot])

            if not at.draining:
                pl.when(cond)(do)

        if t > 0:
            inc = jnp.where(zz < z, z + 1, z - 1)
            join((inc >= 0) & (inc <= 3), zz)
            nxt = jnp.where(zz < z, z - 1, z + 1)
            slot = jnp.where((zz < z) & (nxt == zz), 4, zz)
            at.send(p, z_buf[i].at[slot], zs.at[i, t - 1], zr.at[i, slot], at.line(nxt))
        else:
            join(z > 0, z)
            join(z < 3, 4)
            if not at.draining:
                to_fin(i).start()

    def fin(i):
        axis, half, a, b = cuts[i]
        own = own_half[i].at[at.g]
        if not at.draining:
            at.arrived(fin_buf[i], fr.at[i])
            to_fin(i).wait_send()
            to_y(i, 0, 0).wait_send()
            for yy in (0, 1):

                @pl.when(y == 1 - yy)
                def _():
                    add_into(span(own, axis, b, a), span(fin_buf[i], axis, b if yy == 0 else 0, a))
                    move_into(span(own, axis, yy * (a + b), b), span(fin_buf[i], axis, 0 if yy == 0 else a, b))

        o = span(outs[i], axis, c * half, half)
        at.send(own, o, es.at[i], er.at[i], at.cpeer)
        at.keep(own, o, ws.at[i])

    seq = [(i, t, j) for i in range(n) for (t, j) in order]
    opening = [functools.partial(give, *p) for p in seq]
    ly, lx, lz, lf = lags
    todo = []
    for q, (i, t, j) in enumerate(seq):
        todo.append((q, 0, functools.partial(cadd, i, t, j)))
        todo.append((q + ly, 1, functools.partial(yadd, i, t, j)))
        if j == 0:
            todo.append((q + ly + lx, 2, functools.partial(xadd, i, t)))
            todo.append((q + ly + lx + lz, 3, functools.partial(zadd, i, t)))
            if t == 0:
                todo.append((q + ly + lx + lz + lf, 4, functools.partial(fin, i)))
    todo.sort(key=lambda p: p[:2])

    def last():
        for i in range(n):
            axis, half, _, _ = cuts[i]
            at.arrived(span(outs[i], axis, (1 - c) * half, half), er.at[i])

    return opening, [f for _, _, f in todo], last


def scatter_kernel(cuts, lags, *refs):
    n = len(cuts)
    at = Place()
    at.greet_all()
    opening, steps, last = scatter_steps(at, cuts, refs[:n], refs[n : 2 * n], refs[2 * n :], lags)
    for step in opening + steps:
        step()
    last()
    at.drain(opening + steps)


def scatter(grads, cuts, lags):
    n = len(grads)
    return pl.pallas_call(
        functools.partial(scatter_kernel, cuts, lags),
        out_shape=[jax.ShapeDtypeStruct(w.shape[1:], jnp.bfloat16) for w in grads],
        in_specs=[pl.BlockSpec(memory_space=pl.ANY)] * n,
        out_specs=[pl.BlockSpec(memory_space=pl.ANY)] * n,
        scratch_shapes=scatter_scratch(grads, cuts),
        compiler_params=pltpu.CompilerParams(
            collective_id=1, has_side_effects=True, vmem_limit_bytes=60 * 2**20
        ),
        name="gradient_scatter",
    )(*grads)
def head_window(h):
    first = jnp.minimum(h * HDIM // LANES, HEADS * HDIM // LANES - 2) * LANES
    lane = lax.broadcasted_iota(jnp.int32, (1, 2 * LANES), 1) + first
    inside = (lane >= h * HDIM) & (lane < h * HDIM + HDIM)
    return pl.ds(pl.multiple_of(first, LANES), 2 * LANES), inside


def dot_t(left, right):
    return lax.dot_general(left, right, (((1,), (1,)), ((), ())), preferred_element_type=jnp.float32)


def first_dot(left, right):
    return lax.dot_general(left, right, (((0,), (0,)), ((), ())), preferred_element_type=jnp.float32)


def exact_dot(left, right):
    return jnp.dot(
        left, right, precision=lax.Precision.HIGHEST, preferred_element_type=jnp.float32
    )


def turn(values, cos, sin_next, sin_prev):
    width = values.shape[-1]
    after = pltpu.roll(values, width - HDIM // 4, 1)
    before = pltpu.roll(values, HDIM // 4, 1)
    return values * cos + after * sin_next + before * sin_prev


def turn_back(values, cos, sin_next, sin_prev):
    width = values.shape[-1]
    after = pltpu.roll(values, width - HDIM // 4, 1)
    before = pltpu.roll(values, HDIM // 4, 1)
    return values * cos - after * sin_next - before * sin_prev


def qkv_kernel(
    x_ref, mod_ref, w_ref, gains_ref, cos_ref, next_ref, prev_ref, pick_ref, spread_ref,
    normed_ref, q_ref, k_ref, v_ref, nq_ref, nk_ref, rq_ref, rk_ref,
):
    width = x_ref.shape[-1]
    x = x_ref[0].astype(jnp.float32)
    root = lax.rsqrt(jnp.mean(x * x, axis=-1, keepdims=True) + EPS)
    shift, scale = mod_ref[0, 0:1, :], mod_ref[0, 1:2, :]
    normed = (x * root * (1.0 + scale) + shift).astype(jnp.bfloat16)
    normed_ref[0] = normed
    tables = (cos_ref[...], next_ref[...], prev_ref[...])
    outs = ((q_ref, nq_ref, rq_ref), (k_ref, nk_ref, rk_ref))
    for part, (low_ref, n_ref, r_ref) in enumerate(outs):
        raw = jnp.dot(
            normed, w_ref[:, part * width : (part + 1) * width], preferred_element_type=jnp.float32
        )
        inv = lax.rsqrt(exact_dot(raw * raw, pick_ref[...]) * (1.0 / HDIM) + EPS)
        r_ref[0] = inv
        unit = raw * exact_dot(inv, spread_ref[...])
        n_ref[0] = unit
        low_ref[0] = turn(unit * gains_ref[part : part + 1, :], *tables).astype(jnp.bfloat16)
    v_ref[0] = jnp.dot(
        normed, w_ref[:, 2 * width : 3 * width], preferred_element_type=jnp.float32
    ).astype(jnp.bfloat16)


def qkv_forward(x, mod, qp_all, gains, tables, pick, spread):
    images, length, width = x.shape
    row = lambda w, d: (jax.ShapeDtypeStruct((images, length, w), d), pl.BlockSpec((1, length, w), lambda i: (i, 0, 0)))
    whole = lambda a: pl.BlockSpec(a.shape, lambda i: (0,) * a.ndim)
    outs = [row(width, jnp.bfloat16)] * 4 + [row(width, jnp.float32)] * 2 + [row(LANES, jnp.float32)] * 2
    return pl.pallas_call(
        qkv_kernel,
        grid=(images,),
        in_specs=[
            pl.BlockSpec((1, length, width), lambda i: (i, 0, 0)),
            pl.BlockSpec((1, 6, width), lambda i: (i, 0, 0)),
            pl.BlockSpec((width, 3 * width), lambda i: (0, 0)),
            whole(gains),
        ]
        + [whole(t) for t in tables]
        + [whole(pick), whole(spread)],
        out_shape=[s for s, _ in outs],
        out_specs=[b for _, b in outs],
        compiler_params=pltpu.CompilerParams(vmem_limit_bytes=60 * 2**20),
        name="qkv_forward",
    )(x, mod, qp_all, gains, *tables, pick, spread)


def qkv_back_kernel(
    x_ref, mod_ref, mid_ref, dq_ref, dk_ref, dv_ref, nq_ref, nk_ref, rq_ref, rk_ref, w_ref,
    gains_ref, cos_ref, next_ref, prev_ref, pick_ref, spread_ref,
    dqkv_ref, dx_ref, sums_ref,
):
    width = x_ref.shape[-1]
    tables = (cos_ref[...], next_ref[...], prev_ref[...])
    ins = ((dq_ref, nq_ref, rq_ref), (dk_ref, nk_ref, rk_ref))
    for part, (d_ref, n_ref, r_ref) in enumerate(ins):
        back = turn_back(d_ref[0].astype(jnp.float32) * HDIM ** (-0.5), *tables)
        unit = n_ref[0]
        sums_ref[0, 2 + part : 3 + part, :] = jnp.sum(back * unit, axis=0, keepdims=True)
        inner = back * gains_ref[part : part + 1, :]
        mean = exact_dot(inner * unit, pick_ref[...]) * (1.0 / HDIM)
        grad = (inner - unit * exact_dot(mean, spread_ref[...])) * exact_dot(r_ref[0], spread_ref[...])
        dqkv_ref[0, :, part * width : (part + 1) * width] = grad.astype(jnp.bfloat16)
    dqkv_ref[0, :, 2 * width : 3 * width] = dv_ref[0]
    d_normed = dot_t(dqkv_ref[0], w_ref[...])
    x = x_ref[0].astype(jnp.float32)
    root = lax.rsqrt(jnp.mean(x * x, axis=-1, keepdims=True) + EPS)
    unit = x * root
    sums_ref[0, 0:1, :] = jnp.sum(d_normed, axis=0, keepdims=True)
    sums_ref[0, 1:2, :] = jnp.sum(d_normed * unit, axis=0, keepdims=True)
    inner = d_normed * (1.0 + mod_ref[0, 1:2, :])
    dx_ref[0] = mid_ref[0] + root * (inner - unit * jnp.mean(inner * unit, axis=-1, keepdims=True))


def qkv_backward(x, mod, d_mid, dq, dk, dv, nq, nk, rq, rk, qp_all, gains, tables, pick, spread):
    images, length, width = x.shape
    row = lambda w: pl.BlockSpec((1, length, w), lambda i: (i, 0, 0))
    whole = lambda a: pl.BlockSpec(a.shape, lambda i: (0,) * a.ndim)
    return pl.pallas_call(
        qkv_back_kernel,
        grid=(images,),
        in_specs=[row(width), pl.BlockSpec((1, 6, width), lambda i: (i, 0, 0))]
        + [row(width)] * 6
        + [row(LANES)] * 2
        + [pl.BlockSpec((width, 3 * width), lambda i: (0, 0)), whole(gains)]
        + [whole(t) for t in tables]
        + [whole(pick), whole(spread)],
        out_shape=[
            jax.ShapeDtypeStruct((images, length, 3 * width), jnp.bfloat16),
            jax.ShapeDtypeStruct((images, length, width), jnp.float32),
            jax.ShapeDtypeStruct((images, 4, width), jnp.float32),
        ],
        out_specs=[row(3 * width), row(width), pl.BlockSpec((1, 4, width), lambda i: (i, 0, 0))],
        compiler_params=pltpu.CompilerParams(vmem_limit_bytes=60 * 2**20),
        name="qkv_backward",
    )(x, mod, d_mid, dq, dk, dv, nq, nk, rq, rk, qp_all, gains, *tables, pick, spread)
def attention_kernel(cuts, q_ref, k_ref, v_ref, *refs):
    n = len(cuts)
    ins, (o_ref, inv_ref, kv_out), outs = refs[:n], refs[n : n + 3], refs[n + 3 : 2 * n + 3]
    kv, own_sem, ks, kr, os = refs[2 * n + 3 : 2 * n + 8]
    images, length, width = q_ref.shape
    at = Place()
    at.greet_all() if n else at.greet_band()
    parts = [(i, s) for i in range(images) for s in (0, 1)]

    def rows(s, i, band):
        return kv.at[s, i, pl.ds(pl.multiple_of(band * length, 16), length), :]

    here, over = at.band, (1 - at.y) * 2 + at.c
    beside, across = at.y * 2 + 1 - at.c, (1 - at.y) * 2 + 1 - at.c
    def give(i, s):
        src, dst = (k_ref, v_ref)[s].at[i], rows(s, i, here)
        at.send(src, dst, ks.at[i, s, 0], kr.at[i, s, 0], at.ypeer)
        at.send(src, dst, ks.at[i, s, 1], kr.at[i, s, 1], at.cpeer)
        if not at.draining:
            at.keep(src, dst, own_sem.at[i, s])

    for i, s in parts:
        give(i, s)
    steps, last = gather_steps(at, cuts, ins, outs, refs[2 * n + 8 :]) if n else ([], lambda: None)

    def pass_on(i, s):
        p = rows(s, i, over)
        at.arrived(p, kr.at[i, s, 0])
        at.send(p, p, ks.at[i, s, 2], kr.at[i, s, 2], at.cpeer)

    def ready(i):
        for s in (0, 1):
            if not at.draining:
                src, dst = (k_ref, v_ref)[s].at[i], rows(s, i, here)
                pltpu.make_async_copy(src, dst, own_sem.at[i, s]).wait()
            at.arrived(rows(s, i, beside), kr.at[i, s, 1])
            at.arrived(rows(s, i, across), kr.at[i, s, 2])
            at.keep(kv.at[s, i], kv_out.at[s, i], os.at[i, s])

    def head(i, h):
        win, inside = head_window(h)
        query = q_ref[i, :, win]
        query = jnp.where(inside, query, jnp.zeros_like(query))
        power = jnp.exp2(dot_t(query, kv[0, i, :, win]) * (HDIM ** (-0.5) * LOG2E))
        inv = 1.0 / jnp.sum(power, axis=-1, keepdims=True)
        out = jnp.dot(
            (power * inv).astype(jnp.bfloat16), kv[1, i, :, win], preferred_element_type=jnp.float32
        )
        o_ref[i, :, win] = jnp.where(inside, out.astype(jnp.bfloat16), o_ref[i, :, win])
        lane = lax.broadcasted_iota(jnp.int32, (1, LANES), 1)
        inv_ref[i] = jnp.where(lane == h, inv, inv_ref[i])

    o_ref[...] = jnp.zeros_like(o_ref)
    inv_ref[...] = jnp.zeros_like(inv_ref)
    early = steps[:5]
    for step in early:
        step()
    pass_on(0, 0)
    pass_on(0, 1)
    ready(0)
    todo = steps[5:]
    for i in range(images):
        if i > 0:
            pass_on(i, 0)
            pass_on(i, 1)
            ready(i)
        mine, todo = (todo[:HEADS], todo[HEADS:])

        def body(h, _, i=i, mine=mine):
            for k, step in enumerate(mine):
                pl.when(h == k)(step)
            head(i, h)
            return 0

        lax.fori_loop(0, HEADS, body, 0)
    for step in todo:
        step()
    last()
    at.drain(steps)
    for i, s in parts:
        at.drain([functools.partial(give, i, s), functools.partial(pass_on, i, s)])
    for i in range(images):
        at.drain([functools.partial(ready, i)])


def attention_forward(q, k, v, shards, cuts):
    n = len(shards)
    images, length, width = q.shape
    bands = lax.axis_size("band")
    keys = (2, images, bands * length, width)
    s = pltpu.SemaphoreType.DMA
    any_ref = pl.BlockSpec(memory_space=pl.ANY)
    vmem = pl.BlockSpec(memory_space=pltpu.VMEM)
    return pl.pallas_call(
        functools.partial(attention_kernel, cuts),
        out_shape=[
            jax.ShapeDtypeStruct(q.shape, jnp.bfloat16),
            jax.ShapeDtypeStruct((images, length, LANES), jnp.float32),
            jax.ShapeDtypeStruct(keys, jnp.bfloat16),
        ]
        + [jax.ShapeDtypeStruct((8,) + w.shape, w.dtype) for w in shards],
        in_specs=[vmem, any_ref, any_ref] + [any_ref] * n,
        out_specs=[vmem, vmem, any_ref] + [any_ref] * n,
        scratch_shapes=[
            pltpu.VMEM(keys, jnp.bfloat16),
            s((images, 2)),
            s((images, 2, 3)),
            s((images, 2, 3)),
            s((images, 2)),
        ]
        + (gather_sems(n) if n else []),
        compiler_params=pltpu.CompilerParams(
            collective_id=2, has_side_effects=True, vmem_limit_bytes=60 * 2**20
        ),
        name="attention_forward",
    )(q, k, v, *shards)
def attention_back_kernel(cuts, lags, q_ref, do_ref, inv_ref, kv_ref, *refs):
    n = len(cuts)
    ins, (dq_ref, d_out), outs = refs[:n], refs[n : n + 2], refs[n + 2 : 2 * n + 2]
    kv, dkv, core_buf, y_buf, load_sem, ks, kr, ys, yr, ws = refs[2 * n + 2 : 2 * n + 12]
    images, length, width = q_ref.shape
    at = Place()
    loads = [pltpu.make_async_copy(kv_ref.at[:, i], kv.at[i], load_sem.at[i]) for i in range(images)]
    for d in loads:
        d.start()
    at.greet_all() if n else at.greet_band()
    opening, todo, last = [], [], lambda: None
    if n:
        opening, todo, last = scatter_steps(at, cuts, ins, outs, refs[2 * n + 12 :], lags)
    for step in opening:
        step()
    steps = opening + todo

    def rows(s, i, band):
        return dkv.at[s, i, pl.ds(pl.multiple_of(band * length, 16), length), :]

    def to_core(i):
        for s in (0, 1):
            for yy in (0, 1):
                at.send(rows(s, i, yy * 2 + 1 - at.c), core_buf.at[i, s, yy], ks.at[i, s, yy], kr.at[i, s, yy], at.cpeer)

    def core_add(i):
        for s in (0, 1):
            p = rows(s, i, (1 - at.y) * 2 + at.c)
            at.arrived(core_buf.at[i, s, 1 - at.y], kr.at[i, s, 1 - at.y])
            if not at.draining:
                add_into(p, core_buf.at[i, s, 1 - at.y])
            at.send(p, y_buf.at[i, s], ys.at[i, s], yr.at[i, s], at.ypeer)
        for s in (0, 1):
            at.arrived(core_buf.at[i, s, at.y], kr.at[i, s, at.y])
            if not at.draining:
                add_into(rows(s, i, at.band), core_buf.at[i, s, at.y])

    def y_add(i):
        for s in (0, 1):
            p = rows(s, i, at.band)
            at.arrived(y_buf.at[i, s], yr.at[i, s])
            if not at.draining:
                add_into(p, y_buf.at[i, s])
            at.keep(p, d_out.at[s, i], ws.at[i, s])

    def head(i, h):
        win, inside = head_window(h)
        query, grad = q_ref[i, :, win], do_ref[i, :, win]
        query = jnp.where(inside, query, jnp.zeros_like(query))
        grad = jnp.where(inside, grad, jnp.zeros_like(grad))
        keys, values = kv[i, 0, :, win], kv[i, 1, :, win]
        inv = inv_ref[i, pl.ds(h, 1), :]
        probs = jnp.exp2(dot_t(keys, query) * (HDIM ** (-0.5) * LOG2E)) * inv
        d_probs = dot_t(values, grad)
        delta = jnp.sum(probs * d_probs, axis=0, keepdims=True)
        d_scores = (probs * (d_probs - delta)).astype(jnp.bfloat16)
        d_key = jnp.dot(d_scores, query, preferred_element_type=jnp.float32).astype(jnp.bfloat16)
        d_value = jnp.dot(
            probs.astype(jnp.bfloat16), grad, preferred_element_type=jnp.float32
        ).astype(jnp.bfloat16)
        dkv[0, i, :, win] = jnp.where(inside, d_key, dkv[0, i, :, win])
        dkv[1, i, :, win] = jnp.where(inside, d_value, dkv[1, i, :, win])
        dq_ref[i, :, win] = jnp.where(inside, first_dot(d_scores, keys), dq_ref[i, :, win])

    dq_ref[...] = jnp.zeros_like(dq_ref)
    for s in (0, 1):
        for i in range(images):

            def clear(r, _, s=s, i=i):
                dkv[s, i, pl.ds(pl.multiple_of(r * 16, 16), 16), :] = jnp.zeros((16, width), jnp.bfloat16)
                return 0

            lax.fori_loop(0, kv.shape[2] // 16, clear, 0)
    exchange = []
    for i in range(images):
        loads[i].wait()
        mine, todo = (todo[:HEADS], todo[HEADS:])
        due = exchange
        exchange = [functools.partial(f, i) for f in (core_add, y_add)]

        def body(h, _, i=i, mine=mine, due=due):
            for k, step in enumerate(due):
                pl.when(h == 1 + 12 * k)(step)
            for k, step in enumerate(mine):
                pl.when(h == k)(step)
            head(i, h)
            return 0

        lax.fori_loop(0, HEADS, body, 0)
        to_core(i)
        steps += [functools.partial(to_core, i)] + exchange
    exchange[0]()
    part = min(6, len(todo))
    for step in todo[:part] + [exchange[1]] + todo[part:]:
        step()
    last()
    at.drain(steps)


def attention_backward(q, d_att, inv_rows, kv_all, grads, cuts, lags):
    n = len(grads)
    images, length, width = q.shape
    s = pltpu.SemaphoreType.DMA
    any_ref = pl.BlockSpec(memory_space=pl.ANY)
    vmem = pl.BlockSpec(memory_space=pltpu.VMEM)
    bf = jnp.bfloat16
    return pl.pallas_call(
        functools.partial(attention_back_kernel, cuts, lags),
        out_shape=[
            jax.ShapeDtypeStruct(q.shape, jnp.float32),
            jax.ShapeDtypeStruct((2, images, length, width), bf),
        ]
        + [jax.ShapeDtypeStruct(w.shape[1:], bf) for w in grads],
        in_specs=[vmem, vmem, vmem, any_ref] + [any_ref] * n,
        out_specs=[vmem, any_ref] + [any_ref] * n,
        scratch_shapes=[
            pltpu.VMEM((images, 2) + kv_all.shape[2:], bf),
            pltpu.VMEM(kv_all.shape, bf),
            pltpu.VMEM((images, 2, 2, length, width), bf),
            pltpu.VMEM((images, 2, length, width), bf),
            s((images,)),
            s((images, 2, 2)),
            s((images, 2, 2)),
            s((images, 2)),
            s((images, 2)),
            s((images, 2)),
        ]
        + (scatter_scratch(grads, cuts) if n else []),
        compiler_params=pltpu.CompilerParams(
            collective_id=3, has_side_effects=True, vmem_limit_bytes=63 * 2**20
        ),
        name="attention_backward",
    )(q, d_att, inv_rows, kv_all, *grads)
def modulate(values, shift_in, scale_in):
    root = lax.rsqrt(jnp.mean(values * values, axis=-1, keepdims=True) + EPS)
    return values * root * (1.0 + scale_in[:, None, :]) + shift_in[:, None, :]


def swiglu(gate_in, up_in):
    return jax.nn.silu(gate_in) * up_in


def rope_tables(band, rows, cols):
    quarter = HDIM // 4
    lane = jnp.arange(HDIM, dtype=jnp.int32)
    part = lane // quarter
    frequency = 10000.0 ** (-(lane % quarter).astype(jnp.float32) / quarter)
    row_index = jnp.repeat(band * rows + jnp.arange(rows, dtype=jnp.int32), cols)
    col_index = jnp.tile(jnp.arange(cols, dtype=jnp.int32), rows)
    index = jnp.where(part[None, :] < 2, row_index[:, None], col_index[:, None])
    angle = index.astype(jnp.float32) * frequency[None, :]
    sine = jnp.sin(angle)
    low = (part % 2 == 0)[None, :]
    tables = (jnp.cos(angle), jnp.where(low, -sine, 0.0), jnp.where(low, 0.0, sine))
    return [jnp.tile(t, (1, HEADS)) for t in tables]


def half_cuts(axis, size, own_parts, shared_parts):
    unit = size // 2 // (own_parts + 2 * shared_parts)
    return (axis, size // 2, own_parts * unit, shared_parts * unit)


def by_shard(grad):
    parts = lax.axis_size("grp")
    return grad.reshape(parts, grad.shape[0] // parts, grad.shape[1])


def body(
    patches,
    grad_out,
    cond_table,
    group_ids,
    live_count,
    band_order,
    w_ada,
    b_ada,
    w_qkv,
    q_gain,
    k_gain,
    w_proj,
    w_gate,
    w_up,
    w_down,
):
    images, rows, cols, width = patches.shape
    length = rows * cols
    ff = w_gate.shape[1]
    bf = jnp.bfloat16
    grp = lax.axis_index("grp")
    ada_rows, ada_cols, bias_cols = w_ada.shape[0], w_ada.shape[1], b_ada.shape[0]
    fits = (
        lax.axis_size("grp") == 8
        and w_qkv.shape[0] % 16 == 0
        and 4 * width % 4608 == 0
        and 2 * ff % 1024 == 0
        and w_down.shape[0] % 128 == 0
    )
    qp_cut = half_cuts(1, 4 * width, 8, 5)
    gu_cut = half_cuts(1, 2 * ff, 2, 1)
    down_cut = half_cuts(0, w_down.shape[0], 2, 1)

    w_qp = jnp.concatenate([w_qkv, w_proj], axis=1)
    w_gu = jnp.concatenate([w_gate, w_up], axis=1)
    full = lambda w: w.reshape(-1, w.shape[-1])
    if fits:
        qp_all = full(gather([w_qp], (qp_cut,))[0])
    else:
        qp_all, gu_all, down_all = (lax.all_gather(w, "grp", axis=0, tiled=True) for w in (w_qp, w_gu, w_down))

    onehot = (group_ids[:, None] == jnp.arange(GROUPS, dtype=jnp.int32)[None, :]).astype(jnp.float32)
    cond_rows = lax.dynamic_slice_in_dim(cond_table, grp * ada_rows, ada_rows, axis=1)
    silu_rows, silu_pull = jax.vjp(jax.nn.silu, cond_rows)
    silu_rows = silu_rows.astype(bf)
    mod_part = jnp.dot(silu_rows, w_ada, preferred_element_type=jnp.float32)
    bias_part = lax.dynamic_update_slice_in_dim(
        jnp.zeros((ada_cols,), jnp.float32), b_ada.astype(jnp.float32), grp * bias_cols, axis=0
    )
    mod_table = lax.psum(mod_part + bias_part[None, :], "grp")
    mod = jnp.take(mod_table, group_ids, axis=0).reshape(images, 6, width)
    gate_one, shift_two, scale_two, gate_two = (mod[:, k] for k in (2, 3, 4, 5))
    live_mask = (jnp.arange(images, dtype=jnp.int32) < live_count[0]).astype(jnp.float32)

    tables = rope_tables(band_order[0], rows, cols)
    gains = jnp.stack([jnp.tile(q_gain, HEADS), jnp.tile(k_gain, HEADS)])
    head_of = jnp.arange(width, dtype=jnp.int32) // HDIM
    pick = (head_of[:, None] == jnp.arange(LANES, dtype=jnp.int32)[None, :]).astype(jnp.float32)
    spread = pick.T
    x = patches.reshape(images, length, width)
    normed_one, query, key, value, nq, nk, rq, rk = qkv_forward(x, mod, qp_all, gains, tables, pick, spread)
    attended, inv, kv_all, *rest = attention_forward(
        query, key, value, [w_gu, w_down] if fits else [], (gu_cut, down_cut) if fits else ()
    )
    if fits:
        gu_all, down_all = full(rest[0]), full(rest[1])
    proj_all = qp_all[:, 3 * width :]
    flat = lambda a: a.reshape(images * length, a.shape[-1])
    attended_low = flat(attended)
    proj = jnp.dot(attended_low, proj_all, preferred_element_type=jnp.float32).reshape(images, length, width)
    middle = x.astype(jnp.float32) + gate_one[:, None, :] * proj
    normed_two, norm_two_pull = jax.vjp(modulate, middle, shift_two, scale_two)
    normed_two_low = flat(normed_two.astype(bf))
    pre = jnp.dot(normed_two_low, gu_all, preferred_element_type=jnp.float32)
    hidden, swiglu_pull = jax.vjp(swiglu, pre[:, :ff], pre[:, ff:])
    hidden_low = hidden.astype(bf)
    mlp = jnp.dot(hidden_low, down_all, preferred_element_type=jnp.float32).reshape(images, length, width)
    output = (middle + gate_two[:, None, :] * mlp) * live_mask[:, None, None]
    patches_out = output.astype(bf).reshape(images, rows, cols, width)

    grad_y = grad_out.reshape(images, length, width).astype(jnp.float32) * live_mask[:, None, None]
    d_gate_two = jnp.sum(grad_y * mlp, axis=1)
    d_mlp = flat((grad_y * gate_two[:, None, :]).astype(bf))
    d_w_down = jnp.einsum("tf,td->fd", hidden_low, d_mlp, preferred_element_type=jnp.float32).astype(bf)
    d_hidden = jnp.einsum("td,fd->tf", d_mlp, down_all, preferred_element_type=jnp.float32)
    d_pre = jnp.concatenate([d.astype(bf) for d in swiglu_pull(d_hidden)], axis=1)
    d_w_gu = jnp.einsum("td,tf->df", normed_two_low, d_pre, preferred_element_type=jnp.float32).astype(bf)
    d_normed_two = jnp.einsum("tf,df->td", d_pre, gu_all, preferred_element_type=jnp.float32)
    d_middle_norm, d_shift_two, d_scale_two = norm_two_pull(d_normed_two.reshape(images, length, width))
    d_middle = grad_y + d_middle_norm
    d_gate_one = jnp.sum(d_middle * proj, axis=1)
    d_proj = flat((d_middle * gate_one[:, None, :]).astype(bf))
    d_w_proj = jnp.einsum("td,te->de", attended_low, d_proj, preferred_element_type=jnp.float32).astype(bf)
    d_attended = jnp.einsum("te,de->td", d_proj, proj_all, preferred_element_type=jnp.float32).astype(bf)
    d_query, d_kv, *rest = attention_backward(
        query,
        d_attended.reshape(images, length, width),
        jnp.swapaxes(inv, 1, 2),
        kv_all,
        [by_shard(d_w_gu)] if fits else [],
        (gu_cut,) if fits else (),
        (2, 2, 1, 2),
    )
    d_qkv, d_x, sums = qkv_backward(
        x, mod, d_middle, d_query, d_kv[0], d_kv[1], nq, nk, rq, rk, qp_all, gains, tables, pick, spread
    )
    d_patches = d_x.reshape(images, rows, cols, width)
    d_w_qkv = jnp.einsum("td,te->de", flat(normed_one), flat(d_qkv), preferred_element_type=jnp.float32).astype(bf)
    d_w_qp = jnp.concatenate([d_w_qkv, d_w_proj], axis=1)

    d_mod_part = jnp.concatenate(
        [sums[:, 0], sums[:, 1], d_gate_one, d_shift_two, d_scale_two, d_gate_two], axis=-1
    )
    gain_part = jnp.sum(sums[:, 2:4].reshape(images, 2, HEADS, HDIM), axis=(0, 2))
    summed = lax.psum(jnp.concatenate([d_mod_part.reshape(-1), gain_part.reshape(-1)]), "band")
    d_modulation = summed[: images * ada_cols].reshape(images, ada_cols).astype(bf)
    gain_sum = summed[images * ada_cols :]
    high = lax.reduce_precision(gain_sum, 8, 7)
    middle_part = lax.reduce_precision(gain_sum - high, 8, 7)
    pieces = jnp.stack([high, middle_part, gain_sum - high - middle_part]).astype(bf)
    payload = jnp.concatenate([d_modulation.reshape(-1), onehot.astype(bf).reshape(-1), pieces.reshape(-1)])
    payload = lax.all_gather(payload, "grp", axis=0)
    parts = payload.shape[0]
    at_onehot = images * ada_cols
    at_gain = at_onehot + images * GROUPS
    d_mod_all = payload[:, :at_onehot].reshape(parts * images, ada_cols)
    onehot_all = payload[:, at_onehot:at_gain].reshape(parts * images, GROUPS)
    gain_all = jnp.sum(payload[:, at_gain:].astype(jnp.float32).reshape(parts * 3, 2, HDIM), axis=0)
    silu_all = jnp.dot(onehot_all, silu_rows, preferred_element_type=jnp.float32).astype(bf)
    d_w_ada = jnp.einsum("bd,be->de", silu_all, d_mod_all, preferred_element_type=jnp.float32)
    d_b_ada = lax.dynamic_slice_in_dim(
        jnp.sum(d_mod_all.astype(jnp.float32), axis=0), grp * bias_cols, bias_cols, axis=0
    )
    d_silu = jnp.einsum("be,de->bd", d_mod_all, w_ada, preferred_element_type=jnp.float32)
    d_silu = jnp.dot(
        onehot_all.astype(jnp.float32).T,
        d_silu,
        precision=lax.Precision.HIGHEST,
        preferred_element_type=jnp.float32,
    )
    d_cond = lax.all_gather(silu_pull(d_silu)[0], "grp", axis=1, tiled=True)

    if fits:
        d_gu = rest[0]
        d_down, d_qp = scatter([by_shard(d_w_down), by_shard(d_w_qp)], (down_cut, qp_cut), (2, 2, 1, 2))
    else:
        d_gu, d_down, d_qp = (
            lax.psum(lax.psum_scatter(w, "grp", scatter_dimension=0, tiled=True), "band")
            for w in (d_w_gu, d_w_down, d_w_qp)
        )
    wide = lambda a: a.astype(jnp.float32)
    return (
        patches_out,
        d_patches,
        d_cond,
        d_w_ada,
        d_b_ada,
        wide(d_qp[:, : 3 * width]),
        gain_all[0],
        gain_all[1],
        wide(d_qp[:, 3 * width :]),
        wide(d_gu[:, :ff]),
        wide(d_gu[:, ff:]),
        wide(d_down),
    )


def solution(mesh):
    in_specs = (
        P("grp", "band", None, None),
        P("grp", "band", None, None),
        P(),
        P("grp"),
        P("grp"),
        P("band"),
        P("grp", None),
        P("grp"),
        P("grp", None),
        P(),
        P(),
        P("grp", None),
        P("grp", None),
        P("grp", None),
        P("grp", None),
    )
    out_specs = (
        P("grp", "band", None, None),
        P("grp", "band", None, None),
        P(),
        P("grp", None),
        P("grp"),
        P("grp", None),
        P(),
        P(),
        P("grp", None),
        P("grp", None),
        P("grp", None),
        P("grp", None),
    )
    return jax.shard_map(body, mesh=mesh, in_specs=in_specs, out_specs=out_specs, check_vma=False)
```

time: 1680 us -> 690 us (0.41)
  waiting for transfers between devices: 1140 us -> 0.06 us
  Pallas kernels: 0 us -> 481 us
  matrix products: 258 us -> 99.2 us
  blocking collectives: 112 us -> 42.6 us
  local copies, waits for them, and re-layouts: 73.6 us -> 20.2 us
  other arithmetic: 72.4 us -> 25.5 us
    reduce_scatter x6 -> x0, waiting for transfers between devices: 602 us -> none  [the longest x5 564 us: spread(): lax.psum_scatter(grad.astype(jnp.bfloat16), 'grp', scatter_dimension=0, t...]
    pallas_call x0 -> x6, Pallas kernels: none -> 481 us  [the longest x1 139 us: attention_backward(): pl.pallas_call(functools.partial(attention_back_kernel, cuts, lags), out_...]
    all_gather x6 -> x0, waiting for transfers between devices: 468 us -> none  [the longest x1 118 us: body(): qkv_all = lax.all_gather(w_qkv, 'grp', axis=0, tiled=True)]
    dot_general x65 -> x4, matrix products: 204 us -> 42.5 us  [the longest x1 16.7 us: body(): jnp.einsum('tf,df->td', d_pre, gu_all, preferred_element_type=jnp.float32)]
    psum x1, waiting for transfers between devices: 71.5 us -> 0.02 us  [body(): mod_table = lax.psum(mod_part + bias_part[None, :], 'grp')]
    psum x2 -> x1, blocking collectives: 49.2 us -> 12.1 us  [body(): lax.psum(jnp.concatenate([d_mod_part.reshape(-1), gain_part.reshape(-1)])...]
    all_gather x2 -> x1, blocking collectives: 63.2 us -> 30.5 us  [body(): d_cond = lax.all_gather(silu_pull(d_silu)[0], 'grp', axis=1, tiled=True)]
  transfers between devices with their start and end apart: 14 -> 2, of which waited for: 13 -> 0; matrix products, arithmetic and copies ran while one was open for 11% -> 6% of each run, Pallas kernels for 0% -> 24%
where the time goes in v4:
time: 690 us; the launch traced here: 686 us
  Pallas kernels  481 us (70%)
  matrix products  99.2 us (14%)
  blocking collectives  42.6 us (6%)
  other arithmetic  25.5 us (4%)
  local copies, waits for them, and re-layouts  20.2 us (3%)
  between operations  17.1 us (2%)
    pallas_call x1, Pallas kernels, attention_backward(): pl.pallas_call(functools.partial(attention_back_kernel, cuts, lags), out_...  139 us
    pallas_call x1, Pallas kernels, attention_forward(): pl.pallas_call(functools.partial(attention_kernel, cuts), out_shape=[jax....  121 us
    pallas_call x1, Pallas kernels, scatter(): pl.pallas_call(functools.partial(scatter_kernel, cuts, lags), out_shape=[...  102 us
    pallas_call x1, Pallas kernels, gather(): pl.pallas_call(functools.partial(gather_kernel, cuts), out_shape=[jax.Sha...  62.7 us
    pallas_call x1, Pallas kernels, qkv_backward(): pl.pallas_call(qkv_back_kernel, grid=(images,), in_specs=[row(width), pl....  31 us
    all_gather x1, blocking collectives, body(): d_cond = lax.all_gather(silu_pull(d_silu)[0], 'grp', axis=1, tiled=True)  30.5 us
    pallas_call x1, Pallas kernels, qkv_forward(): pl.pallas_call(qkv_kernel, grid=(images,), in_specs=[pl.BlockSpec((1, len...  25.4 us
    dot_general x1, matrix products, body(): jnp.einsum('tf,df->td', d_pre, gu_all, preferred_element_type=jnp.float32)  16.7 us
  transfers between devices with their start and end apart: 2, of which 0 were waited for; matrix products, arithmetic and copies ran while one was open for 6% of the time, Pallas kernels for 24%

profile of v4, /device:TPU:0, one launch (start us, length us, event | category | flops | bytes accessed | tf_op | source)
XLA Modules:
  0.0 686.2 jit_solution(16524448969369236107)
XLA Ops:
  7.3 0.9 convert_dynamic-update-slice_fusion
  8.2 2.7 convolution_add_fusion
  11.0 1.0 fusion.13.pick_ref
  12.0 0.9 fusion.14.spread_ref
  13.7 1.2 pad_maximum_fusion.3.refs_0_
  14.8 62.7 %weight_gather.1 = bf16[8,144,4608]{2,1,0:T(8,128)(2,1)} custom-call(bf16[144,4608]{1,0:T(8,128)(2,1)} %pad_maximum_fusion.3.refs_0_), custom_call_target="tpu_custom_call" | custom-call | tf_op jit(solution)/shard_map/weight_gather/pallas_call | solution.py:174
  79.1 1.4 copy.56.cos_ref
  80.6 1.4 copy.57.next_ref
  82.0 1.4 copy.58.prev_ref
  83.4 0.6 convert_element_type.176
  84.1 0.6 pad_maximum_fusion.5.gains_ref
  84.7 1.3 pad_maximum_fusion.2.refs_0_
  87.3 1.5 gather_fusion
  89.6 25.4 %qkv_forward.1 = (bf16[2,256,1152]{2,1,0:T(8,128)(2,1)}, bf16[2,256,1152]{2,1,0:T(8,128)(2,1)}, bf16[2,256,1152]{2,1,0:T(8,128)(2,1)}, bf16[2,256,1152]{2,1,0:T(...) custom-call(bf16[2,256,1152]{2,1,0:T(8,128)(2,1)} %bitcast.126, ...), custom_call_target="tpu_custom_call" | custom-call | tf_op jit(solution)/shard_map/qkv_forward/pallas_call | solution.py:442
  115.1 120.7 %attention_forward.1 = (bf16[2,256,1152]{2,1,0:T(8,128)(2,1)}, f32[2,256,128]{2,1,0:T(8,128)}, bf16[2,2,1024,1152]{3,2,1,0:T(8,128)(2,1)}, bf16[8,144,6144]{2,1,0:T(8,128)(2,1)}, bf16[8,384,1152]{2,1,0:T(8,128)(2,1)}) custom-call(bf16[2,256,1152]{2,1,0:T(8,128)(2,1)} %get-tuple-element.33.q_ref, bf16[2,256,1152]{2,1,0:T(8,128)(2,1)} %get-tuple-element.34.k_ref, ...), custom_call_target="tpu_custom_call" | custom-call | tf_op jit(solution)/shard_map/attention_forward/pallas_call | solution.py:602
  235.9 5.5 multiply_reduce_fusion.4
  242.9 10.7 %fusion.35 = f32[512,6144]{1,0:T(8,128)} fusion(bf16[512,1152]{1,0:T(8,128)(2,1)S(1)} %bitcast.131, bf16[1152,6144]{1,0:T(8,128)(2,1)S(1)} %bitcast.137), kind=kOutput, calls=%fused_computation.126 | convolution fusion | flops 7247757312 | bytes 27918336 | tf_op jit(solution)/shard_map/dot_general | solution.py:866
  253.9 12.4 %fusion.4 = (bf16[512,3072]{1,0:T(8,128)(2,1)S(1)}, bf16[512,3072]{1,0:T(8,128)(2,1)S(1)}, bf16[512,3072]{1,0:T(8,128)(2,1)}) fusion(f32[512,6144]{1,0:T(8,128)} %fusion.35, bf16[512,1152]{1,0:T(8,128)(2,1)S(1)} %bitcast.129, bf16[3072,1152]{1,0:T(8,128)(2,1)} %bitcast.138), kind=kOutput, calls=%fused_computation.12 | convolution fusion | flops 3649044480 | bytes 30277632 | tf_op jit(solution)/shard_map/td,fd->tf/dot_general | solution.py:877
  266.3 3.2 pad_maximum_fusion.1
  269.5 10.4 %convolution_convert_fusion = bf16[1152,6144]{1,0:T(8,128)(2,1)} fusion(bf16[512,1152]{1,0:T(8,128)(2,1)S(1)} %bitcast.132, bf16[512,3072]{1,0:T(8,128)(2,1)S(1)} %get-tuple-element.62, bf16[512,3072]{1,0:T(8,128)(2,1)S(1)} %get-tuple-element.61), kind=kOutput, calls=%fused_computation.1 | convolution fusion | flops 7267418112 | bytes 21626880 | tf_op jit(solution)/shard_map/td,tf->df/dot_general | solution.py:879
  279.9 16.7 %multiply_reduce_fusion.1 = (f32[2,1152]{1,0:T(2,128)}, f32[2,256]{1,0:T(2,128)}, f32[2,1152]{1,0:T(2,128)}, f32[2,256,1152]{2,1,0:T(8,128)}) fusion(f32[2,256,1152]{2,1,0:T(8,128)S(1)} %get-tuple-element.60, f32[2,256]{1,0:T(2,128)} %copy-done.26, f32[2,1152]{1,0:T(2,128)} %copy-done.21, bf16[2,256,6144]{2,1,0:T(8,128)(2,1)} %bitcast.122, ...), kind=kOutput, calls=%fused_computation.28 | convolution fusion | flops 7251880960 | bytes 25197568 | tf_op jit(solution)/shard_map/tf,df->td/dot_general | solution.py:880
  296.6 0.7 multiply_multiply_fusion
  297.3 11.6 %multiply_reduce_fusion = (f32[2,1152]{1,0:T(2,128)}, bf16[2,256,1152]{2,1,0:T(8,128)(2,1)}, f32[2,1152]{1,0:T(2,128)}, f32[2,256,1152]{2,1,0:T(8,128)S(1)}) fusion(bf16[2,8,32,1152]{3,2,1,0:T(8,128)(2,1)S(1)} %copy-done.2, f32[2]{0:T(128)} %copy-done.28, f32[2,256,1152]{2,1,0:T(8,128)S(1)} %get-tuple-element.60, f32[2,1152]{1,0:T(2,128)S(1)} %get-tuple-element.88, ...), kind=kOutput, calls=%fused_computation.27 | convolution fusion | flops 3633311232 | bytes 22061064 | tf_op jit(solution)/shard_map/dot_general | solution.py:869
  309.1 5.8 convolution_convert_fusion.2
  314.9 0.8 copy.59
  315.7 139.5 %attention_backward.1 = (f32[2,256,1152]{2,1,0:T(8,128)}, bf16[2,2,256,1152]{3,2,1,0:T(8,128)(2,1)}, bf16[144,6144]{1,0:T(8,128)(2,1)}) custom-call(bf16[2,256,1152]{2,1,0:T(8,128)(2,1)} %get-tuple-element.33.q_ref, bf16[2,256,1152]{2,1,0:T(8,128)(2,1)} %bitcast.128, f32[2,128,256]{2,1,0:T(8,128)} %bitcast.133, ...), custom_call_target="tpu_custom_call" | custom-call | tf_op jit(solution)/shard_map/attention_backward/pallas_call | solution.py:731
  455.2 3.2 slice_bitcast_fusion
  458.4 31.0 %qkv_backward.1 = (bf16[2,256,3456]{2,1,0:T(8,128)(2,1)}, f32[2,256,1152]{2,1,0:T(8,128)}, f32[2,4,1152]{2,1,0:T(4,128)}) custom-call(bf16[2,256,1152]{2,1,0:T(8,128)(2,1)} %bitcast.127, f32[2,6,1152]{2,1,0:T(8,128)} %copy-done.13, f32[2,256,1152]{2,1,0:T(8,128)} %copy-done, f32[2,256,1152]{2,1,0:T(8,128)} %get-tuple-element.41.dq_ref, ...), custom_call_target="tpu_custom_call" | custom-call | tf_op jit(solution)/shard_map/qkv_backward/pallas_call | solution.py:491
  489.4 0.8 slice_reduce_fusion
  490.2 0.8 copy.63
  491.0 0.8 slice.80
  492.2 12.1 %psum.15 = f32[13968]{0:T(1024)S(1)} all-reduce(f32[13968]{0:T(1024)S(1)} %pad_maximum_fusion.4), channel_id=1, replica_groups=mesh['grp'=8,'band'=4] {'band'}, use_global_device_ids=true, to_apply=%region_9.10 | all-reduce | flops 13968 | bytes 111744 | tf_op jit(solution)/shard_map/psum | solution.py:907
  504.3 4.6 fusion.1
  509.7 0.7 copy-done.12
  510.8 9.1 %convolution_convert_fusion.1 = bf16[3072,1152]{1,0:T(8,128)(2,1)} fusion(bf16[512,3072]{1,0:T(8,128)(2,1)} %get-tuple-element.63, bf16[512,1152]{1,0:T(8,128)(2,1)S(1)} %fusion.9), kind=kOutput, calls=%fused_computation.4 | convolution fusion | flops 3627417600 | bytes 11403264 | tf_op jit(solution)/shard_map/tf,td->fd/dot_general | solution.py:876
  519.9 4.7 fusion
  524.6 4.6 pad_maximum_fusion
  529.3 102.2 %gradient_scatter.1 = (bf16[384,1152]{1,0:T(8,128)(2,1)}, bf16[144,4608]{1,0:T(8,128)(2,1)}) custom-call(bf16[8,384,1152]{2,1,0:T(8,128)(2,1)} %bitcast.121, bf16[8,144,4608]{2,1,0:T(8,128)(2,1)} %bitcast.119), custom_call_target="tpu_custom_call" | custom-call | tf_op jit(solution)/shard_map/gradient_scatter/pallas_call | solution.py:365
  631.5 2.7 slice_convert_fusion
  634.2 2.2 slice_convert_fusion.1
  636.4 2.0 slice_convert_fusion.3
  638.4 1.3 convert_element_type.190
  639.8 1.2 reshape.487
  642.0 3.6 fusion.12
  645.5 0.9 fusion.20
  646.4 30.5 %all-gather.1 = f32[8,144,8]{1,2,0:T(8,128)S(1)} all-gather(f32[1,144,8]{1,2,0:T(8,128)S(1)} %fusion.20), channel_id=1, replica_groups=mesh['grp'=8,'band'=4] {'grp'}, dimensions={0}, use_global_device_ids=true | all-gather | bytes 41472 | tf_op jit(solution)/shard_map/all_gather | solution.py:933
  676.9 0.7 reshape.493
  677.6 0.7 dynamic_slice.7
  (148 shorter events, 7.9 us)
Async XLA Ops:
  7.2 5.7 copy-start.36
  7.2 6.5 copy-start.17
  7.2 6.5 copy-start.11
  7.2 80.1 %all-reduce.4.cloned.1.call-start = ((), (), s32[]{:S(2)}) async-start(), calls=%async_computation | async-start | bytes 442368 | tf_op jit(solution)/shard_map/psum | solution.py:842
  10.9 628.9 %all-reduce.6.cloned.1.call-start = ((), (), s32[]{:S(2)}) async-start(), calls=%async_computation.1 | async-start | bytes 458752
  13.6 70.4 %copy-start.28 = (f32[2]{0:T(128)}, f32[2]{0:T(128)S(1)}, u32[]{:S(2)}) copy-start(f32[2]{0:T(128)S(1)} %compare_convert_fusion.1) | copy-start | bytes 28
  14.8 62.7 %copy-start.31 = (f32[72]{0:T(128)S(1)}, f32[72]{0:T(128)}, u32[]{:S(2)}) copy-start(f32[72]{0:T(128)} %param.25) | copy-start | bytes 868
  14.8 62.8 %copy-start.32 = (f32[72]{0:T(128)S(1)}, f32[72]{0:T(128)}, u32[]{:S(2)}) copy-start(f32[72]{0:T(128)} %param.24) | copy-start | bytes 868
  82.0 2.7 copy-start.14
  82.0 2.7 copy-start.15
  83.4 2.6 copy-start.37
  89.0 0.6 copy-start.13
  89.1 146.8 %copy-start.19 = (f32[2,1152]{1,0:T(2,128)}, f32[2,1152]{1,0:T(2,128)S(1)}, u32[]{:S(2)}) copy-start(f32[2,1152]{1,0:T(2,128)S(1)} %get-tuple-element.89) | copy-start | bytes 27652
  115.1 120.8 %copy-start.4 = (bf16[2,8,32,1152]{3,2,1,0:T(8,128)(2,1)S(1)}, bf16[2,8,32,1152]{3,2,1,0:T(8,128)(2,1)}, u32[]{:S(2)}) copy-start(bf16[2,8,32,1152]{3,2,1,0:T(8,128)(2,1)} %param.15) | copy-start | bytes 3538948
  235.8 7.0 %copy-start.33 = (bf16[8,144,6144]{2,1,0:T(8,128)(2,1)S(1)}, bf16[8,144,6144]{2,1,0:T(8,128)(2,1)}, u32[]{:S(2)}) copy-start(bf16[8,144,6144]{2,1,0:T(8,128)(2,1)} %get-tuple-element.37) | copy-start | bytes 42467332
  241.4 0.6 copy-start.27
  241.4 12.2 %copy-start.26 = (f32[2,256]{1,0:T(2,128)}, f32[2,256]{1,0:T(2,128)S(1)}, u32[]{:S(2)}) copy-start(f32[2,256]{1,0:T(2,128)S(1)} %fusion.24) | copy-start | bytes 6148
  241.9 11.6 %copy-start.21 = (f32[2,1152]{1,0:T(2,128)}, f32[2,1152]{1,0:T(2,128)S(1)}, u32[]{:S(2)}) copy-start(f32[2,1152]{1,0:T(2,128)S(1)} %get-tuple-element.87) | copy-start | bytes 27652
  242.3 11.3 %copy-start.9 = (bf16[2,256,1152]{2,1,0:T(8,128)(2,1)}, bf16[2,256,1152]{2,1,0:T(8,128)(2,1)S(1)}, u32[]{:S(2)}) copy-start(bf16[2,256,1152]{2,1,0:T(8,128)(2,1)S(1)} %add_convert_fusion) | copy-start | bytes 3538948
  242.9 10.7 %copy-start.2 = (bf16[2,8,32,1152]{3,2,1,0:T(8,128)(2,1)S(1)}, bf16[2,8,32,1152]{3,2,1,0:T(8,128)(2,1)}, u32[]{:S(2)}) copy-start(bf16[2,8,32,1152]{3,2,1,0:T(8,128)(2,1)} %param.16) | copy-start | bytes 3538948
  242.9 10.7 %copy-start.29 = (f32[2]{0:T(128)S(1)}, f32[2]{0:T(128)}, u32[]{:S(2)}) copy-start(f32[2]{0:T(128)} %copy-done.28) | copy-start | bytes 28
  266.3 3.2 copy-start.10
  297.3 11.6 %copy-start.20 = (f32[2,1152]{1,0:T(2,128)S(1)}, f32[2,1152]{1,0:T(2,128)}, u32[]{:S(2)}) copy-start(f32[2,1152]{1,0:T(2,128)} %copy-done.19) | copy-start | bytes 27652
  308.9 6.0 copy-start
  309.1 5.8 copy-start.7
  309.1 5.8 copy-start.18
  458.4 33.6 %copy-start.25 = (f32[2,1152]{1,0:T(2,128)S(1)}, f32[2,1152]{1,0:T(2,128)}, u32[]{:S(2)}) copy-start(f32[2,1152]{1,0:T(2,128)} %get-tuple-element.66) | copy-start | bytes 27652
  458.4 33.6 %copy-start.23 = (f32[2,1152]{1,0:T(2,128)S(1)}, f32[2,1152]{1,0:T(2,128)}, u32[]{:S(2)}) copy-start(f32[2,1152]{1,0:T(2,128)} %get-tuple-element.56) | copy-start | bytes 27652
  458.4 33.6 %copy-start.22 = (f32[2,1152]{1,0:T(2,128)S(1)}, f32[2,1152]{1,0:T(2,128)}, u32[]{:S(2)}) copy-start(f32[2,1152]{1,0:T(2,128)} %get-tuple-element.54) | copy-start | bytes 27652
  458.4 33.6 %copy-start.24 = (f32[2,1152]{1,0:T(2,128)S(1)}, f32[2,1152]{1,0:T(2,128)}, u32[]{:S(2)}) copy-start(f32[2,1152]{1,0:T(2,128)} %get-tuple-element.64) | copy-start | bytes 27652
  458.4 45.8 %copy-start.8 = (bf16[2,256,1152]{2,1,0:T(8,128)(2,1)S(1)}, bf16[2,256,1152]{2,1,0:T(8,128)(2,1)}, u32[]{:S(2)}) copy-start(bf16[2,256,1152]{2,1,0:T(8,128)(2,1)} %copy-done.7) | copy-start | bytes 3538948
  504.3 4.8 copy-start.30
  504.3 6.1 copy-start.3
  509.7 0.7 copy-start.12
  510.8 9.1 %copy-start.34 = (bf16[2,256,3456]{2,1,0:T(8,128)(2,1)S(1)}, bf16[2,256,3456]{2,1,0:T(8,128)(2,1)}, u32[]{:S(2)}) copy-start(bf16[2,256,3456]{2,1,0:T(8,128)(2,1)} %get-tuple-element.50) | copy-start | bytes 10616836
  510.8 9.1 %copy-start.35 = (bf16[2,256,1152]{2,1,0:T(8,128)(2,1)S(1)}, bf16[2,256,1152]{2,1,0:T(8,128)(2,1)}, u32[]{:S(2)}) copy-start(bf16[2,256,1152]{2,1,0:T(8,128)(2,1)} %get-tuple-element.49) | copy-start | bytes 3538948
  519.9 4.7 copy-start.5
  631.5 2.8 copy-start.6
  634.2 4.2 copy-start.16
  636.4 4.6 copy-start.1
Sparse Core Ops, SparseCore 0:
  12.0 74.0 all-reduce.3
  510.5 72.6 all-reduce.5

commit v5 on v4

--- a/solution.py
+++ b/solution.py
@@ -86,22 +86,25 @@
 def gather_steps(at, cuts, ins, outs, sems):
     n = len(cuts)
     lsem, zs, zr, xs, xr, ys, yr, cs, cr, ds = sems
+    ins, outs = ([refs[cut[5]] for cut in cuts] for refs in (ins, outs))
+    soon = sum(cut[5] == 0 for cut in cuts)
     x, y, z, c, far = at.x, at.y, at.z, at.c, at.far
 
     def piece(i, ref, yy, cc):
-        axis, half, a, b = cuts[i]
-        return span(ref, axis, cc * half + yy * b, a + b)
+        axis, half, a, b, base, _ = cuts[i]
+        return span(ref, axis, base + cc * half + yy * b, a + b)
 
     def bpart(i, ref, yy, cc):
-        axis, half, a, b = cuts[i]
-        return span(ref, axis, cc * half + yy * (a + b), b)
+        axis, half, a, b, base, _ = cuts[i]
+        return span(ref, axis, base + cc * half + yy * (a + b), b)
 
     def own(i):
         src, dst = piece(i, ins[i], y, c), piece(i, outs[i].at[at.g], y, c)
         at.send(src, dst, zs.at[i, 0], zr.at[i, z], (at.g + 2, at.band), z < 3)
         at.send(src, dst, ds.at[i], zr.at[i, z], (at.g - 2, at.band), z > 0)
         at.send(src, dst, xs.at[i, 0], xr.at[i, 0], at.xpeer)
-        at.keep(ins[i], outs[i].at[at.g], lsem.at[i])
+        if cuts[i][4] == 0 and not (at.draining and cuts[i][5] == 0):
+            at.keep(ins[i], outs[i].at[at.g], lsem.at[i])
 
     def down(i, slot, shard):
         p = bpart(i, outs[i].at[shard], y, c)
@@ -134,52 +137,34 @@
     order = [slots[k] for k in (3, 0, 4, 1, 5, 2, 6)]
     steps = [lambda: own(0)]
     for i in range(n):
-        steps.append(lambda i=i: zarr(i, 1))
+        mine = [lambda i=i: zarr(i, 1)]
         if i + 1 < n:
-            steps.append(lambda i=i: own(i + 1))
-        rest = [lambda i=i: xarr(i, 0)]
+            mine.append(lambda i=i: own(i + 1))
+        mine.append(lambda i=i: xarr(i, 0))
         for t in (2, 3):
-            rest += [lambda i=i, t=t: zarr(i, t), lambda i=i, t=t: xarr(i, t - 1)]
-        rest.append(lambda i=i: xarr(i, 3))
-        for k, step in enumerate(rest):
-            if i > 0:
-                steps.append(lambda i=i, k=k: yarr(i - 1, *order[k]))
-            steps.append(step)
+            mine += [lambda i=i, t=t: zarr(i, t), lambda i=i, t=t: xarr(i, t - 1)]
+        mine.append(lambda i=i: xarr(i, 3))
         if i > 0:
-            steps.append(lambda i=i: yarr(i - 1, *order[6]))
+            late = [lambda i=i, k=k: yarr(i - 1, *order[k]) for k in range(7)]
+            pace, held = 3 if i == soon else 1, list(late)
+            merged = []
+            while late or mine:
+                merged += late[:pace] + mine[:1]
+                late, mine = late[pace:], mine[1:]
+            mine = merged
+        if i == soon:
+            first = len(steps) + max(k for k, step in enumerate(mine) if step in held) + 1
+        steps += mine
     steps += [lambda k=k: yarr(n - 1, *order[k]) for k in range(7)]
 
-    def last():
-        for i in range(n):
-            for slot, s in slots:
-                at.arrived(piece(i, outs[i].at[s], y, 1 - c), cr.at[i, slot])
-                at.arrived(bpart(i, outs[i].at[s], 1 - y, 1 - c), cr.at[i, 7 + slot])
-
-    return steps, last
-
-
-def gather_kernel(cuts, *refs):
-    n = len(cuts)
-    at = Place()
-    at.greet_all()
-    steps, last = gather_steps(at, cuts, refs[:n], refs[n : 2 * n], refs[2 * n :])
-    for step in steps:
-        step()
-    last()
-    at.drain(steps)
-
-
-def gather(ws, cuts):
-    n = len(ws)
-    return pl.pallas_call(
-        functools.partial(gather_kernel, cuts),
-        out_shape=[jax.ShapeDtypeStruct((8,) + w.shape, w.dtype) for w in ws],
-        in_specs=[pl.BlockSpec(memory_space=pl.ANY)] * n,
-        out_specs=[pl.BlockSpec(memory_space=pl.ANY)] * n,
-        scratch_shapes=gather_sems(n),
-        compiler_params=pltpu.CompilerParams(collective_id=0, has_side_effects=True),
-        name="weight_gather",
-    )(*ws)
+    def last(i):
+        for slot, s in slots:
+            at.arrived(piece(i, outs[i].at[s], y, 1 - c), cr.at[i, slot])
+            at.arrived(bpart(i, outs[i].at[s], 1 - y, 1 - c), cr.at[i, 7 + slot])
+
+    return steps, first, last
+
+
 def add_into(dst, src):
     def step(r, _):
         rows = pl.ds(pl.multiple_of(r * 16, 16), 16)
@@ -203,7 +188,8 @@
     s = pltpu.SemaphoreType.DMA
 
     def buf(lead, k, size):
-        shape = (grads[k].shape[1], size) if cuts[k][0] == 1 else (size, grads[k].shape[2])
+        grad = grads[cuts[k][5]]
+        shape = (grad.shape[1], size) if cuts[k][0] == 1 else (size, grad.shape[2])
         return pltpu.VMEM(lead + shape, jnp.bfloat16)
 
     out = []
@@ -225,13 +211,14 @@
     own_half, core_buf, y_buf, x_buf, z_buf, fin_buf = (scratch[k * n : (k + 1) * n] for k in range(6))
     ls, cs, cr, ys, yr, xs, xr, zs, zr, fs, fr, es, er, ws = scratch[6 * n :]
     x, y, z, c, far = at.x, at.y, at.z, at.c, at.far
+    ins, outs = ([refs[cut[5]] for cut in cuts] for refs in (ins, outs))
 
     def piece(i, ref):
-        _, _, a, b = cuts[i]
+        _, _, a, b = cuts[i][:4]
         return span(ref, cuts[i][0], y * b, a + b)
 
     def bpart(i, ref, yy):
-        _, _, a, b = cuts[i]
+        _, _, a, b = cuts[i][:4]
         return span(ref, cuts[i][0], yy * (a + b), b)
 
     order = [(t, j) for t in (3, 2, 1, 0) for j in (1, 0)]
@@ -240,14 +227,14 @@
         return far[t] * 2 + (1 - x if j else x)
 
     def load(i, t, j):
-        axis, half, _, _ = cuts[i]
+        axis, half, _, _, base, _ = cuts[i]
         s, q = shard(t, j), order.index((t, j))
-        return pltpu.make_async_copy(span(ins[i].at[s], axis, c * half, half), own_half[i].at[s], ls.at[i, q])
+        return pltpu.make_async_copy(span(ins[i].at[s], axis, base + c * half, half), own_half[i].at[s], ls.at[i, q])
 
     def give(i, t, j):
-        axis, half, _, _ = cuts[i]
+        axis, half, _, _, base, _ = cuts[i]
         s, q = shard(t, j), order.index((t, j))
-        src = span(ins[i].at[s], axis, (1 - c) * half, half)
+        src = span(ins[i].at[s], axis, base + (1 - c) * half, half)
         at.send(src, core_buf[i].at[s], cs.at[i, q], cr.at[i, s], at.cpeer)
         if not at.draining:
             load(i, t, j).start()
@@ -310,7 +297,7 @@
                 to_fin(i).start()
 
     def fin(i):
-        axis, half, a, b = cuts[i]
+        axis, half, a, b, base, _ = cuts[i]
         own = own_half[i].at[at.g]
         if not at.draining:
             at.arrived(fin_buf[i], fr.at[i])
@@ -323,7 +310,7 @@
                     add_into(span(own, axis, b, a), span(fin_buf[i], axis, b if yy == 0 else 0, a))
                     move_into(span(own, axis, yy * (a + b), b), span(fin_buf[i], axis, 0 if yy == 0 else a, b))
 
-        o = span(outs[i], axis, c * half, half)
+        o = span(outs[i], axis, base + c * half, half)
         at.send(own, o, es.at[i], er.at[i], at.cpeer)
         at.keep(own, o, ws.at[i])
 
@@ -343,14 +330,13 @@
 
     def last():
         for i in range(n):
-            axis, half, _, _ = cuts[i]
-            at.arrived(span(outs[i], axis, (1 - c) * half, half), er.at[i])
+            axis, half, _, _, base, _ = cuts[i]
+            at.arrived(span(outs[i], axis, base + (1 - c) * half, half), er.at[i])
 
     return opening, [f for _, _, f in todo], last
 
 
-def scatter_kernel(cuts, lags, *refs):
-    n = len(cuts)
+def scatter_kernel(n, cuts, lags, *refs):
     at = Place()
     at.greet_all()
     opening, steps, last = scatter_steps(at, cuts, refs[:n], refs[n : 2 * n], refs[2 * n :], lags)
@@ -363,7 +349,7 @@
 def scatter(grads, cuts, lags):
     n = len(grads)
     return pl.pallas_call(
-        functools.partial(scatter_kernel, cuts, lags),
+        functools.partial(scatter_kernel, n, cuts, lags),
         out_shape=[jax.ShapeDtypeStruct(w.shape[1:], jnp.bfloat16) for w in grads],
         in_specs=[pl.BlockSpec(memory_space=pl.ANY)] * n,
         out_specs=[pl.BlockSpec(memory_space=pl.ANY)] * n,
@@ -388,9 +374,11 @@
     return lax.dot_general(left, right, (((0,), (0,)), ((), ())), preferred_element_type=jnp.float32)
 
 
-def exact_dot(left, right):
-    return jnp.dot(
-        left, right, precision=lax.Precision.HIGHEST, preferred_element_type=jnp.float32
+def pick_dot(values, chosen):
+    high = values.astype(jnp.bfloat16)
+    low = (values - high.astype(jnp.float32)).astype(jnp.bfloat16)
+    return jnp.dot(high, chosen, preferred_element_type=jnp.float32) + jnp.dot(
+        low, chosen, preferred_element_type=jnp.float32
     )
 
 
@@ -406,55 +394,6 @@
     after = pltpu.roll(values, width - HDIM // 4, 1)
     before = pltpu.roll(values, HDIM // 4, 1)
     return values * cos - after * sin_next - before * sin_prev
-
-
-def qkv_kernel(
-    x_ref, mod_ref, w_ref, gains_ref, cos_ref, next_ref, prev_ref, pick_ref, spread_ref,
-    normed_ref, q_ref, k_ref, v_ref, nq_ref, nk_ref, rq_ref, rk_ref,
-):
-    width = x_ref.shape[-1]
-    x = x_ref[0].astype(jnp.float32)
-    root = lax.rsqrt(jnp.mean(x * x, axis=-1, keepdims=True) + EPS)
-    shift, scale = mod_ref[0, 0:1, :], mod_ref[0, 1:2, :]
-    normed = (x * root * (1.0 + scale) + shift).astype(jnp.bfloat16)
-    normed_ref[0] = normed
-    tables = (cos_ref[...], next_ref[...], prev_ref[...])
-    outs = ((q_ref, nq_ref, rq_ref), (k_ref, nk_ref, rk_ref))
-    for part, (low_ref, n_ref, r_ref) in enumerate(outs):
-        raw = jnp.dot(
-            normed, w_ref[:, part * width : (part + 1) * width], preferred_element_type=jnp.float32
-        )
-        inv = lax.rsqrt(exact_dot(raw * raw, pick_ref[...]) * (1.0 / HDIM) + EPS)
-        r_ref[0] = inv
-        unit = raw * exact_dot(inv, spread_ref[...])
-        n_ref[0] = unit
-        low_ref[0] = turn(unit * gains_ref[part : part + 1, :], *tables).astype(jnp.bfloat16)
-    v_ref[0] = jnp.dot(
-        normed, w_ref[:, 2 * width : 3 * width], preferred_element_type=jnp.float32
-    ).astype(jnp.bfloat16)
-
-
-def qkv_forward(x, mod, qp_all, gains, tables, pick, spread):
-    images, length, width = x.shape
-    row = lambda w, d: (jax.ShapeDtypeStruct((images, length, w), d), pl.BlockSpec((1, length, w), lambda i: (i, 0, 0)))
-    whole = lambda a: pl.BlockSpec(a.shape, lambda i: (0,) * a.ndim)
-    outs = [row(width, jnp.bfloat16)] * 4 + [row(width, jnp.float32)] * 2 + [row(LANES, jnp.float32)] * 2
-    return pl.pallas_call(
-        qkv_kernel,
-        grid=(images,),
-        in_specs=[
-            pl.BlockSpec((1, length, width), lambda i: (i, 0, 0)),
-            pl.BlockSpec((1, 6, width), lambda i: (i, 0, 0)),
-            pl.BlockSpec((width, 3 * width), lambda i: (0, 0)),
-            whole(gains),
-        ]
-        + [whole(t) for t in tables]
-        + [whole(pick), whole(spread)],
-        out_shape=[s for s, _ in outs],
-        out_specs=[b for _, b in outs],
-        compiler_params=pltpu.CompilerParams(vmem_limit_bytes=60 * 2**20),
-        name="qkv_forward",
-    )(x, mod, qp_all, gains, *tables, pick, spread)
 
 
 def qkv_back_kernel(
@@ -470,8 +409,8 @@
         unit = n_ref[0]
         sums_ref[0, 2 + part : 3 + part, :] = jnp.sum(back * unit, axis=0, keepdims=True)
         inner = back * gains_ref[part : part + 1, :]
-        mean = exact_dot(inner * unit, pick_ref[...]) * (1.0 / HDIM)
-        grad = (inner - unit * exact_dot(mean, spread_ref[...])) * exact_dot(r_ref[0], spread_ref[...])
+        mean = pick_dot(inner * unit, pick_ref[...]) * (1.0 / HDIM)
+        grad = (inner - unit * pick_dot(mean, spread_ref[...])) * pick_dot(r_ref[0], spread_ref[...])
         dqkv_ref[0, :, part * width : (part + 1) * width] = grad.astype(jnp.bfloat16)
     dqkv_ref[0, :, 2 * width : 3 * width] = dv_ref[0]
     d_normed = dot_t(dqkv_ref[0], w_ref[...])
@@ -506,30 +445,48 @@
         compiler_params=pltpu.CompilerParams(vmem_limit_bytes=60 * 2**20),
         name="qkv_backward",
     )(x, mod, d_mid, dq, dk, dv, nq, nk, rq, rk, qp_all, gains, *tables, pick, spread)
-def attention_kernel(cuts, q_ref, k_ref, v_ref, *refs):
+def forward_kernel(cuts, refs):
     n = len(cuts)
-    ins, (o_ref, inv_ref, kv_out), outs = refs[:n], refs[n : n + 3], refs[n + 3 : 2 * n + 3]
-    kv, own_sem, ks, kr, os = refs[2 * n + 3 : 2 * n + 8]
-    images, length, width = q_ref.shape
+    soon = sum(cut[5] == 0 for cut in cuts)
     at = Place()
-    at.greet_all() if n else at.greet_band()
+    x_ref, part_ref, group_ref, gains_ref, cos_ref, next_ref, prev_ref, pick_ref, spread_ref = refs["in"]
+    normed_ref, q_ref, nq_ref, nk_ref, rq_ref, rk_ref, o_ref, inv_ref, mod_ref, kv_out = refs["out"]
+    kv, w_buf, mod_buf, mod_in, w_sem, ms, mr, ks, kr, os = refs["scratch"]
+    ins, outs = refs["shards"], refs["full"]
+    images, length, width = x_ref.shape
     parts = [(i, s) for i in range(images) for s in (0, 1)]
+    if n:
+        at.greet_all()
+        steps, first, last = gather_steps(at, cuts, ins, outs, refs["sems"])
+    else:
+        at.greet_band()
+        steps, first, last = [], 0, None
+
+    mod_buf[...] = part_ref[...]
+
+    def mod_copy(r):
+        peer = (at.xpeer, at.line(at.far[1]), at.line((at.z + 2) % 4))[r]
+        return at.copy(mod_buf, mod_in.at[r], ms.at[r], mr.at[r], peer)
+
+    def mod_step(r):
+        if at.draining:
+            return
+        if r > 0:
+            mod_copy(r - 1).wait()
+            mod_buf[...] = mod_buf[...] + mod_in[r - 1]
+        if r < 3:
+            mod_copy(r).start()
 
     def rows(s, i, band):
         return kv.at[s, i, pl.ds(pl.multiple_of(band * length, 16), length), :]
 
     here, over = at.band, (1 - at.y) * 2 + at.c
     beside, across = at.y * 2 + 1 - at.c, (1 - at.y) * 2 + 1 - at.c
+
     def give(i, s):
-        src, dst = (k_ref, v_ref)[s].at[i], rows(s, i, here)
-        at.send(src, dst, ks.at[i, s, 0], kr.at[i, s, 0], at.ypeer)
-        at.send(src, dst, ks.at[i, s, 1], kr.at[i, s, 1], at.cpeer)
-        if not at.draining:
-            at.keep(src, dst, own_sem.at[i, s])
-
-    for i, s in parts:
-        give(i, s)
-    steps, last = gather_steps(at, cuts, ins, outs, refs[2 * n + 8 :]) if n else ([], lambda: None)
+        p = rows(s, i, here)
+        at.send(p, p, ks.at[i, s, 0], kr.at[i, s, 0], at.ypeer)
+        at.send(p, p, ks.at[i, s, 1], kr.at[i, s, 1], at.cpeer)
 
     def pass_on(i, s):
         p = rows(s, i, over)
@@ -538,12 +495,43 @@
 
     def ready(i):
         for s in (0, 1):
-            if not at.draining:
-                src, dst = (k_ref, v_ref)[s].at[i], rows(s, i, here)
-                pltpu.make_async_copy(src, dst, own_sem.at[i, s]).wait()
             at.arrived(rows(s, i, beside), kr.at[i, s, 1])
             at.arrived(rows(s, i, across), kr.at[i, s, 2])
             at.keep(kv.at[s, i], kv_out.at[s, i], os.at[i, s])
+
+    def norm(i):
+        value = x_ref[i].astype(jnp.float32)
+        root = lax.rsqrt(jnp.mean(value * value, axis=-1, keepdims=True) + EPS)
+        chosen = jnp.sum(group_ref[:, i : i + 1] * mod_buf[...], axis=0, keepdims=True)
+        mod_ref[i : i + 1, :] = chosen
+        shift, scale = chosen[:, :width], chosen[:, width : 2 * width]
+        normed_ref[i] = (value * root * (1.0 + scale) + shift).astype(jnp.bfloat16)
+
+    def raw(i, part):
+        return jnp.dot(
+            normed_ref[i], w_buf[:, part * width : (part + 1) * width], preferred_element_type=jnp.float32
+        )
+
+    def project(i, part, n_ref, r_ref):
+        values = raw(i, part)
+        inv = lax.rsqrt(pick_dot(values * values, pick_ref[...]) * (1.0 / HDIM) + EPS)
+        r_ref[i] = inv
+        unit = values * pick_dot(inv, spread_ref[...])
+        n_ref[i] = unit
+        scaled = unit * gains_ref[part : part + 1, :]
+        return turn(scaled, cos_ref[...], next_ref[...], prev_ref[...]).astype(jnp.bfloat16)
+
+    def key_part(i):
+        norm(i)
+        kv[0, i, pl.ds(pl.multiple_of(here * length, 16), length), :] = project(i, 1, nk_ref, rk_ref)
+        give(i, 0)
+
+    def value_part(i):
+        kv[1, i, pl.ds(pl.multiple_of(here * length, 16), length), :] = raw(i, 2).astype(jnp.bfloat16)
+        give(i, 1)
+
+    def query_part(i):
+        q_ref[i] = project(i, 0, nq_ref, rq_ref)
 
     def head(i, h):
         win, inside = head_window(h)
@@ -558,32 +546,62 @@
         lane = lax.broadcasted_iota(jnp.int32, (1, LANES), 1)
         inv_ref[i] = jnp.where(lane == h, inv, inv_ref[i])
 
+    if n:
+        for k in range(3):
+            mod_step(k)
+            for step in steps[2 * k : 2 * k + 2]:
+                step()
+        mod_step(3)
+        for step in steps[6:first]:
+            step()
+        for i in range(soon):
+            last(i)
+        pltpu.make_async_copy(ins[0], outs[0].at[at.g], refs["sems"][0].at[0]).wait()
+        loads = [
+            pltpu.make_async_copy(
+                outs[0].at[k, :, pl.ds(0, 3 * width)],
+                w_buf.at[pl.ds(k * (width // 8), width // 8), :],
+                w_sem.at[k],
+            )
+            for k in range(8)
+        ]
+    else:
+        loads = [pltpu.make_async_copy(ins[0].at[:, pl.ds(0, 3 * width)], w_buf, w_sem.at[0])]
+    for d in loads:
+        d.start()
     o_ref[...] = jnp.zeros_like(o_ref)
     inv_ref[...] = jnp.zeros_like(inv_ref)
-    early = steps[:5]
-    for step in early:
-        step()
-    pass_on(0, 0)
-    pass_on(0, 1)
-    ready(0)
-    todo = steps[5:]
+    for d in loads:
+        d.wait()
+    todo = steps[first:]
     for i in range(images):
-        if i > 0:
-            pass_on(i, 0)
-            pass_on(i, 1)
-            ready(i)
-        mine, todo = (todo[:HEADS], todo[HEADS:])
+        for work in (key_part, value_part):
+            work(i)
+            for step in todo[:2]:
+                step()
+            todo = todo[2:]
+    for i in range(images):
+        query_part(i)
+        for step in todo[:2]:
+            step()
+        todo = todo[2:]
+    for i in range(images):
+        pass_on(i, 0)
+        pass_on(i, 1)
+        ready(i)
+        mine, todo = (todo[: HEADS // 2], todo[HEADS // 2 :])
 
         def body(h, _, i=i, mine=mine):
             for k, step in enumerate(mine):
-                pl.when(h == k)(step)
+                pl.when(h == 2 * k)(step)
             head(i, h)
             return 0
 
         lax.fori_loop(0, HEADS, body, 0)
     for step in todo:
         step()
-    last()
+    for i in range(soon, n):
+        last(i)
     at.drain(steps)
     for i, s in parts:
         at.drain([functools.partial(give, i, s), functools.partial(pass_on, i, s)])
@@ -591,39 +609,61 @@
         at.drain([functools.partial(ready, i)])
 
 
-def attention_forward(q, k, v, shards, cuts):
-    n = len(shards)
-    images, length, width = q.shape
+def forward(x, mod_part, groups, gains, tables, pick, spread, shards, cuts):
+    n = len(cuts)
+    images, length, width = x.shape
     bands = lax.axis_size("band")
     keys = (2, images, bands * length, width)
     s = pltpu.SemaphoreType.DMA
+    bf = jnp.bfloat16
     any_ref = pl.BlockSpec(memory_space=pl.ANY)
     vmem = pl.BlockSpec(memory_space=pltpu.VMEM)
+    args = [x, mod_part, groups, gains, *tables, pick, spread]
+    rows = lambda w, d: jax.ShapeDtypeStruct((images, length, w), d)
+    outs = [rows(width, bf)] * 2 + [rows(width, jnp.float32)] * 2 + [rows(LANES, jnp.float32)] * 2
+    outs += [rows(width, bf), rows(LANES, jnp.float32), jax.ShapeDtypeStruct((images, mod_part.shape[1]), jnp.float32)]
+    scratch = [
+        pltpu.VMEM(keys, bf),
+        pltpu.VMEM((width, 3 * width), bf),
+        pltpu.VMEM(mod_part.shape, jnp.float32),
+        pltpu.VMEM((3,) + mod_part.shape, jnp.float32),
+        s((8,)),
+        s((3,)),
+        s((3,)),
+        s((images, 2, 3)),
+        s((images, 2, 3)),
+        s((images, 2)),
+    ]
+    whole = len(shards) if n else 0
+    sizes = [len(args), len(shards), len(outs) + 1, whole, len(scratch), 10 if n else 0]
+
+    def kernel(*refs):
+        groups_of, start = [], 0
+        for size in sizes:
+            groups_of.append(refs[start : start + size])
+            start += size
+        names = ("in", "shards", "out", "full", "scratch", "sems")
+        forward_kernel(cuts, dict(zip(names, groups_of)))
+
     return pl.pallas_call(
-        functools.partial(attention_kernel, cuts),
-        out_shape=[
-            jax.ShapeDtypeStruct(q.shape, jnp.bfloat16),
-            jax.ShapeDtypeStruct((images, length, LANES), jnp.float32),
-            jax.ShapeDtypeStruct(keys, jnp.bfloat16),
-        ]
-        + [jax.ShapeDtypeStruct((8,) + w.shape, w.dtype) for w in shards],
-        in_specs=[vmem, any_ref, any_ref] + [any_ref] * n,
-        out_specs=[vmem, vmem, any_ref] + [any_ref] * n,
-        scratch_shapes=[
-            pltpu.VMEM(keys, jnp.bfloat16),
-            s((images, 2)),
-            s((images, 2, 3)),
-            s((images, 2, 3)),
-            s((images, 2)),
-        ]
-        + (gather_sems(n) if n else []),
+        kernel,
+        out_shape=outs
+        + [jax.ShapeDtypeStruct(keys, bf)]
+        + [jax.ShapeDtypeStruct((8,) + w.shape, w.dtype) for w in shards[:whole]],
+        in_specs=[vmem] * len(args) + [any_ref] * len(shards),
+        out_specs=[vmem] * len(outs) + [any_ref] * (1 + whole),
+        scratch_shapes=scratch + (gather_sems(n) if n else []),
         compiler_params=pltpu.CompilerParams(
             collective_id=2, has_side_effects=True, vmem_limit_bytes=60 * 2**20
         ),
-        name="attention_forward",
-    )(q, k, v, *shards)
-def attention_back_kernel(cuts, lags, q_ref, do_ref, inv_ref, kv_ref, *refs):
-    n = len(cuts)
+        name="forward",
+    )(*args, *shards)
+
+
+EACH = 9
+
+
+def attention_back_kernel(n, cuts, lags, q_ref, do_ref, inv_ref, kv_ref, *refs):
     ins, (dq_ref, d_out), outs = refs[:n], refs[n : n + 2], refs[n + 2 : 2 * n + 2]
     kv, dkv, core_buf, y_buf, load_sem, ks, kr, ys, yr, ws = refs[2 * n + 2 : 2 * n + 12]
     images, length, width = q_ref.shape
@@ -698,7 +738,7 @@
     exchange = []
     for i in range(images):
         loads[i].wait()
-        mine, todo = (todo[:HEADS], todo[HEADS:])
+        mine, todo = (todo[:EACH], todo[EACH:])
         due = exchange
         exchange = [functools.partial(f, i) for f in (core_add, y_add)]
 
@@ -706,7 +746,7 @@
             for k, step in enumerate(due):
                 pl.when(h == 1 + 12 * k)(step)
             for k, step in enumerate(mine):
-                pl.when(h == k)(step)
+                pl.when(h == k * HEADS // EACH)(step)
             head(i, h)
             return 0
 
@@ -729,7 +769,7 @@
     vmem = pl.BlockSpec(memory_space=pltpu.VMEM)
     bf = jnp.bfloat16
     return pl.pallas_call(
-        functools.partial(attention_back_kernel, cuts, lags),
+        functools.partial(attention_back_kernel, n, cuts, lags),
         out_shape=[
             jax.ShapeDtypeStruct(q.shape, jnp.float32),
             jax.ShapeDtypeStruct((2, images, length, width), bf),
@@ -779,9 +819,9 @@
     return [jnp.tile(t, (1, HEADS)) for t in tables]
 
 
-def half_cuts(axis, size, own_parts, shared_parts):
+def half_cuts(ref, axis, base, size, own_parts, shared_parts):
     unit = size // 2 // (own_parts + 2 * shared_parts)
-    return (axis, size // 2, own_parts * unit, shared_parts * unit)
+    return (axis, size // 2, own_parts * unit, shared_parts * unit, base, ref)
 
 
 def by_shard(grad):
@@ -816,21 +856,12 @@
         lax.axis_size("grp") == 8
         and w_qkv.shape[0] % 16 == 0
         and 4 * width % 4608 == 0
-        and 2 * ff % 1024 == 0
-        and w_down.shape[0] % 128 == 0
+        and 2 * ff % 3072 == 0
+        and w_down.shape[0] % 384 == 0
     )
-    qp_cut = half_cuts(1, 4 * width, 8, 5)
-    gu_cut = half_cuts(1, 2 * ff, 2, 1)
-    down_cut = half_cuts(0, w_down.shape[0], 2, 1)
-
     w_qp = jnp.concatenate([w_qkv, w_proj], axis=1)
     w_gu = jnp.concatenate([w_gate, w_up], axis=1)
     full = lambda w: w.reshape(-1, w.shape[-1])
-    if fits:
-        qp_all = full(gather([w_qp], (qp_cut,))[0])
-    else:
-        qp_all, gu_all, down_all = (lax.all_gather(w, "grp", axis=0, tiled=True) for w in (w_qp, w_gu, w_down))
-
     onehot = (group_ids[:, None] == jnp.arange(GROUPS, dtype=jnp.int32)[None, :]).astype(jnp.float32)
     cond_rows = lax.dynamic_slice_in_dim(cond_table, grp * ada_rows, ada_rows, axis=1)
     silu_rows, silu_pull = jax.vjp(jax.nn.silu, cond_rows)
@@ -839,9 +870,7 @@
     bias_part = lax.dynamic_update_slice_in_dim(
         jnp.zeros((ada_cols,), jnp.float32), b_ada.astype(jnp.float32), grp * bias_cols, axis=0
     )
-    mod_table = lax.psum(mod_part + bias_part[None, :], "grp")
-    mod = jnp.take(mod_table, group_ids, axis=0).reshape(images, 6, width)
-    gate_one, shift_two, scale_two, gate_two = (mod[:, k] for k in (2, 3, 4, 5))
+    mod_part = mod_part + bias_part[None, :]
     live_mask = (jnp.arange(images, dtype=jnp.int32) < live_count[0]).astype(jnp.float32)
 
     tables = rope_tables(band_order[0], rows, cols)
@@ -849,13 +878,23 @@
     head_of = jnp.arange(width, dtype=jnp.int32) // HDIM
     pick = (head_of[:, None] == jnp.arange(LANES, dtype=jnp.int32)[None, :]).astype(jnp.float32)
     spread = pick.T
+    pick, spread = pick.astype(bf), spread.astype(bf)
     x = patches.reshape(images, length, width)
-    normed_one, query, key, value, nq, nk, rq, rk = qkv_forward(x, mod, qp_all, gains, tables, pick, spread)
-    attended, inv, kv_all, *rest = attention_forward(
-        query, key, value, [w_gu, w_down] if fits else [], (gu_cut, down_cut) if fits else ()
-    )
+    groups = jnp.pad(onehot.T, ((0, 0), (0, LANES - images)))
+    common = (groups, gains, tables, pick, spread)
     if fits:
-        gu_all, down_all = full(rest[0]), full(rest[1])
+        shards = [w_qp, w_gu, w_down]
+        cuts = [half_cuts(0, 1, 0, 4 * width, 1, 1), half_cuts(1, 1, 0, 2 * ff, 4, 1)]
+        cuts += [half_cuts(2, 0, 0, w_down.shape[0], 4, 1)]
+    else:
+        qp_all, gu_all, down_all = (lax.all_gather(w, "grp", axis=0, tiled=True) for w in (w_qp, w_gu, w_down))
+        mod_part = lax.psum(mod_part, "grp")
+        shards, cuts = [qp_all], []
+    normed_one, query, nq, nk, rq, rk, attended, inv, mod, kv_all, *rest = forward(x, mod_part, *common, shards, cuts)
+    if fits:
+        qp_all, gu_all, down_all = (full(w) for w in rest)
+    mod = mod.reshape(images, 6, width)
+    gate_one, shift_two, scale_two, gate_two = (mod[:, k] for k in (2, 3, 4, 5))
     proj_all = qp_all[:, 3 * width :]
     flat = lambda a: a.reshape(images * length, a.shape[-1])
     attended_low = flat(attended)
@@ -890,7 +929,7 @@
         jnp.swapaxes(inv, 1, 2),
         kv_all,
         [by_shard(d_w_gu)] if fits else [],
-        (gu_cut,) if fits else (),
+        [half_cuts(0, 1, 0, 2 * ff, 4, 1)] if fits else [],
         (2, 2, 1, 2),
     )
     d_qkv, d_x, sums = qkv_backward(
@@ -934,7 +973,9 @@
 
     if fits:
         d_gu = rest[0]
-        d_down, d_qp = scatter([by_shard(d_w_down), by_shard(d_w_qp)], (down_cut, qp_cut), (2, 2, 1, 2))
+        cuts = [half_cuts(0, 0, 0, w_down.shape[0], 2, 1)]
+        cuts += [half_cuts(1, 1, 0, 4 * width, 8, 5)]
+        d_down, d_qp = scatter([by_shard(d_w_down), by_shard(d_w_qp)], cuts, (2, 2, 1, 2))
     else:
         d_gu, d_down, d_qp = (
             lax.psum(lax.psum_scatter(w, "grp", scatter_dimension=0, tiled=True), "band")

time: 690 us -> 639 us (0.926)
  Pallas kernels: 481 us -> 434 us
    pallas_call x5 -> x3, Pallas kernels: 451 us -> 413 us  [the longest x1 186 us: forward(): pl.pallas_call(kernel, out_shape=outs + [jax.ShapeDtypeStruct(keys, bf)]...]
    pallas_call x1, Pallas kernels: 31 us -> 21.6 us  [qkv_backward(): pl.pallas_call(qkv_back_kernel, grid=(images,), in_specs=[row(width), pl....]
  transfers between devices with their start and end apart: 2 -> 1, of which waited for: 0 -> 0; matrix products, arithmetic and copies ran while one was open for 6% -> 4% of each run, Pallas kernels for 24% -> 15%
where the time goes in v5:
time: 639 us; the launch traced here: 636 us
  Pallas kernels  434 us (68%)
  matrix products  93.1 us (15%)
  blocking collectives  43.9 us (7%)
  other arithmetic  26.4 us (4%)
  local copies, waits for them, and re-layouts  21.3 us (3%)
  between operations  16.8 us (3%)
    pallas_call x1, Pallas kernels, forward(): pl.pallas_call(kernel, out_shape=outs + [jax.ShapeDtypeStruct(keys, bf)]...  186 us
    pallas_call x1, Pallas kernels, attention_backward(): pl.pallas_call(functools.partial(attention_back_kernel, n, cuts, lags), o...  129 us
    pallas_call x1, Pallas kernels, scatter(): pl.pallas_call(functools.partial(scatter_kernel, n, cuts, lags), out_shap...  98.2 us
    all_gather x1, blocking collectives, body(): d_cond = lax.all_gather(silu_pull(d_silu)[0], 'grp', axis=1, tiled=True)  30.5 us
    pallas_call x1, Pallas kernels, qkv_backward(): pl.pallas_call(qkv_back_kernel, grid=(images,), in_specs=[row(width), pl....  21.6 us
    dot_general x1, matrix products, body(): jnp.einsum('tf,df->td', d_pre, gu_all, preferred_element_type=jnp.float32)  16.6 us
    psum x1, blocking collectives, body(): lax.psum(jnp.concatenate([d_mod_part.reshape(-1), gain_part.reshape(-1)])...  13.4 us
  transfers between devices with their start and end apart: 1, of which 0 were waited for; matrix products, arithmetic and copies ran while one was open for 4% of the time, Pallas kernels for 15%

profile of v5, /device:TPU:0, one launch (start us, length us, event | category | flops | bytes accessed | tf_op | source)
XLA Modules:
  0.0 635.8 jit_solution(5530632536589364023)
XLA Ops:
  7.3 0.9 convert_convert_fusion.1.refs_7_.pick_ref
  8.2 0.8 convert_convert_fusion.refs_8_.spread_ref
  10.1 0.7 iota_compare_fusion.2
  11.4 0.7 tile.19
  12.2 0.7 tile.18
  14.3 1.4 copy.56.refs_4_.cos_ref
  15.7 1.4 copy.57.refs_5_.next_ref
  17.2 1.4 copy.58.refs_6_.prev_ref
  19.3 1.2 pad_maximum_fusion.3.refs_9_
  20.4 1.3 pad_maximum_fusion.2.refs_10_
  22.0 0.6 copy-done.1
  22.6 1.8 convolution_add_fusion.refs_1_
  24.5 185.7 %forward.1 = (bf16[2,256,1152]{2,1,0:T(8,128)(2,1)}, bf16[2,256,1152]{2,1,0:T(8,128)(2,1)}, f32[2,256,1152]{2,1,0:T(8,128)}, f32[2,256,1152]{2,1,0:T(8,128)}, f3...) custom-call(bf16[2,256,1152]{2,1,0:T(8,128)(2,1)} %bitcast.129, ...), custom_call_target="tpu_custom_call" | custom-call | tf_op jit(solution)/shard_map/forward/pallas_call | solution.py:648
  210.1 0.9 reshape.449.mod_ref
  211.7 5.5 multiply_reduce_fusion.4
  217.8 1.2 copy-done.30
  219.0 10.7 %fusion.33 = f32[512,6144]{1,0:T(8,128)} fusion(bf16[512,1152]{1,0:T(8,128)(2,1)S(1)} %bitcast.134, bf16[1152,6144]{1,0:T(8,128)(2,1)S(1)} %bitcast.149), kind=kOutput, calls=%fused_computation.123 | convolution fusion | flops 7247757312 | bytes 27918336 | tf_op jit(solution)/shard_map/dot_general | solution.py:905
  230.0 12.3 %fusion.4 = (bf16[512,3072]{1,0:T(8,128)(2,1)S(1)}, bf16[512,3072]{1,0:T(8,128)(2,1)S(1)}, bf16[512,3072]{1,0:T(8,128)(2,1)}) fusion(f32[512,6144]{1,0:T(8,128)} %fusion.33, bf16[512,1152]{1,0:T(8,128)(2,1)S(1)} %bitcast.132, bf16[3072,1152]{1,0:T(8,128)(2,1)} %bitcast.150), kind=kOutput, calls=%fused_computation.11 | convolution fusion | flops 3649044480 | bytes 30277632 | tf_op jit(solution)/shard_map/td,fd->tf/dot_general | solution.py:916
  242.4 3.2 pad_maximum_fusion.1
  245.5 10.9 %convolution_convert_fusion = bf16[1152,6144]{1,0:T(8,128)(2,1)} fusion(bf16[512,1152]{1,0:T(8,128)(2,1)S(1)} %bitcast.135, bf16[512,3072]{1,0:T(8,128)(2,1)S(1)} %get-tuple-element.62, bf16[512,3072]{1,0:T(8,128)(2,1)S(1)} %get-tuple-element.61), kind=kOutput, calls=%fused_computation | convolution fusion | flops 7267418112 | bytes 21626880 | tf_op jit(solution)/shard_map/td,tf->df/dot_general | solution.py:918
  256.5 16.6 %multiply_reduce_fusion.1 = (f32[2,1152]{1,0:T(2,128)}, f32[2,256]{1,0:T(2,128)}, f32[2,1152]{1,0:T(2,128)}, f32[2,256,1152]{2,1,0:T(8,128)}) fusion(f32[2,256,1152]{2,1,0:T(8,128)S(1)} %get-tuple-element.60, f32[2,256]{1,0:T(2,128)S(1)} %fusion.22, f32[2,1152]{1,0:T(2,128)} %bitcast.144, bf16[2,256,6144]{2,1,0:T(8,128)(2,1)} %bitcast.125, ...), kind=kOutput, calls=%fused_computation.27 | convolution fusion | flops 7251880960 | bytes 25197568 | tf_op jit(solution)/shard_map/tf,df->td/dot_general | solution.py:919
  273.1 0.7 multiply_multiply_fusion
  273.8 11.7 %multiply_reduce_fusion = (f32[2,1152]{1,0:T(2,128)}, bf16[2,256,1152]{2,1,0:T(8,128)(2,1)}, f32[2,1152]{1,0:T(2,128)}, f32[2,256,1152]{2,1,0:T(8,128)S(1)}) fusion(bf16[2,8,32,1152]{3,2,1,0:T(8,128)(2,1)S(1)} %copy-done.3, f32[2]{0:T(128)} %compare_convert_fusion.1, f32[2,256,1152]{2,1,0:T(8,128)S(1)} %get-tuple-element.60, f32[2,1152]{1,0:T(2,128)S(1)} %bitcast.138, ...), kind=kOutput, calls=%fused_computation.26 | convolution fusion | flops 3633311232 | bytes 22061064 | tf_op jit(solution)/shard_map/dot_general | solution.py:908
  285.7 5.8 convolution_convert_fusion.2
  291.5 0.8 copy.59
  292.3 128.7 %attention_backward.1 = (f32[2,256,1152]{2,1,0:T(8,128)}, bf16[2,2,256,1152]{3,2,1,0:T(8,128)(2,1)}, bf16[144,6144]{1,0:T(8,128)(2,1)}) custom-call(bf16[2,256,1152]{2,1,0:T(8,128)(2,1)} %get-tuple-element.38.q_ref, bf16[2,256,1152]{2,1,0:T(8,128)(2,1)} %bitcast.131, f32[2,128,256]{2,1,0:T(8,128)} %bitcast.136, ...), custom_call_target="tpu_custom_call" | custom-call | tf_op jit(solution)/shard_map/attention_backward/pallas_call | solution.py:771
  421.0 3.2 slice_bitcast_fusion
  424.3 21.6 %qkv_backward.1 = (bf16[2,256,3456]{2,1,0:T(8,128)(2,1)}, f32[2,256,1152]{2,1,0:T(8,128)}, f32[2,4,1152]{2,1,0:T(4,128)}) custom-call(bf16[2,256,1152]{2,1,0:T(8,128)(2,1)} %bitcast.130, f32[2,6,1152]{2,1,0:T(8,128)} %copy-done.16, f32[2,256,1152]{2,1,0:T(8,128)} %copy-done, f32[2,256,1152]{2,1,0:T(8,128)} %get-tuple-element.41.dq_ref, ...), custom_call_target="tpu_custom_call" | custom-call | tf_op jit(solution)/shard_map/qkv_backward/pallas_call | solution.py:430
  445.9 0.8 slice_reduce_fusion
  446.7 0.8 copy.63
  447.5 0.8 slice.80
  448.7 13.4 %psum.7 = f32[13968]{0:T(1024)S(1)} all-reduce(f32[13968]{0:T(1024)S(1)} %pad_maximum_fusion.4), channel_id=1, replica_groups=mesh['grp'=8,'band'=4] {'band'}, use_global_device_ids=true, to_apply=%region_8.9 | all-reduce | flops 13968 | bytes 111744 | tf_op jit(solution)/shard_map/psum | solution.py:946
  464.3 0.7 copy-done.12
  465.1 1.7 fusion.1
  467.3 6.3 convolution_convert_fusion.1
  473.7 4.7 fusion
  478.4 4.6 pad_maximum_fusion
  483.0 98.2 %gradient_scatter.1 = (bf16[384,1152]{1,0:T(8,128)(2,1)}, bf16[144,4608]{1,0:T(8,128)(2,1)}) custom-call(bf16[8,384,1152]{2,1,0:T(8,128)(2,1)} %bitcast.124, bf16[8,144,4608]{2,1,0:T(8,128)(2,1)} %bitcast.119), custom_call_target="tpu_custom_call" | custom-call | tf_op jit(solution)/shard_map/gradient_scatter/pallas_call | solution.py:351
  581.2 2.7 slice_convert_fusion
  584.0 2.2 slice_convert_fusion.1
  586.2 2.0 slice_convert_fusion.3
  588.2 1.3 convert_element_type.206
  589.5 1.2 reshape.471
  591.7 3.6 fusion.12
  595.3 0.9 fusion.18
  596.1 30.5 %all-gather.1 = f32[8,144,8]{1,2,0:T(8,128)S(1)} all-gather(f32[1,144,8]{1,2,0:T(8,128)S(1)} %fusion.18), channel_id=1, replica_groups=mesh['grp'=8,'band'=4] {'grp'}, dimensions={0}, use_global_device_ids=true | all-gather | bytes 41472 | tf_op jit(solution)/shard_map/all_gather | solution.py:972
  626.7 0.7 reshape.476
  627.4 0.7 dynamic_slice.7
  (140 shorter events, 8.9 us)
Async XLA Ops:
  7.2 582.3 %all-reduce.4.cloned.1.call-start = ((), (), s32[]{:S(2)}) async-start(), calls=%async_computation | async-start | bytes 458752
  17.1 2.1 copy-start.11
  17.1 2.1 copy-start.17
  17.2 3.2 copy-start.13
  18.6 1.8 copy-start.14
  20.4 1.3 copy-start.29
  20.4 2.2 copy-start.1
  24.5 187.2 %copy-start.5 = (bf16[2,8,32,1152]{3,2,1,0:T(8,128)(2,1)S(1)}, bf16[2,8,32,1152]{3,2,1,0:T(8,128)(2,1)}, u32[]{:S(2)}) copy-start(bf16[2,8,32,1152]{3,2,1,0:T(8,128)(2,1)} %param.15) | copy-start | bytes 3538948
  211.0 0.6 copy-start.16
  211.1 6.1 copy-start.19
  211.7 7.3 %copy-start.30 = (bf16[8,144,6144]{2,1,0:T(8,128)(2,1)S(1)}, bf16[8,144,6144]{2,1,0:T(8,128)(2,1)}, u32[]{:S(2)}) copy-start(bf16[8,144,6144]{2,1,0:T(8,128)(2,1)} %get-tuple-element.36) | copy-start | bytes 42467332
  217.2 0.6 copy-start.26
  217.2 0.6 copy-start.21
  217.6 12.1 %copy-start.9 = (bf16[2,256,1152]{2,1,0:T(8,128)(2,1)}, bf16[2,256,1152]{2,1,0:T(8,128)(2,1)S(1)}, u32[]{:S(2)}) copy-start(bf16[2,256,1152]{2,1,0:T(8,128)(2,1)S(1)} %add_convert_fusion) | copy-start | bytes 3538948
  219.0 10.7 %copy-start.3 = (bf16[2,8,32,1152]{3,2,1,0:T(8,128)(2,1)S(1)}, bf16[2,8,32,1152]{3,2,1,0:T(8,128)(2,1)}, u32[]{:S(2)}) copy-start(bf16[2,8,32,1152]{3,2,1,0:T(8,128)(2,1)} %param.16) | copy-start | bytes 3538948
  219.0 10.7 %copy-start.27 = (f32[2]{0:T(128)S(1)}, f32[2]{0:T(128)}, u32[]{:S(2)}) copy-start(f32[2]{0:T(128)} %compare_convert_fusion.1) | copy-start | bytes 28
  242.4 3.2 copy-start.10
  273.8 11.7 %copy-start.20 = (f32[2,1,1152]{2,0,1:T(2,128)S(1)}, f32[2,1,1152]{2,0,1:T(2,128)}, u32[]{:S(2)}) copy-start(f32[2,1,1152]{2,0,1:T(2,128)} %copy-done.19) | copy-start | bytes 27652
  285.5 6.0 copy-start
  285.7 5.8 copy-start.7
  285.7 5.8 copy-start.18
  424.3 24.0 %copy-start.34 = (s32[2]{0:T(128)S(1)}, s32[2]{0:T(128)}, u32[]{:S(2)}) copy-start(s32[2]{0:T(128)} %param.18) | copy-start | bytes 28
  424.3 24.3 %copy-start.25 = (f32[2,1152]{1,0:T(2,128)S(1)}, f32[2,1152]{1,0:T(2,128)}, u32[]{:S(2)}) copy-start(f32[2,1152]{1,0:T(2,128)} %get-tuple-element.66) | copy-start | bytes 27652
  424.3 24.3 %copy-start.23 = (f32[2,1152]{1,0:T(2,128)S(1)}, f32[2,1152]{1,0:T(2,128)}, u32[]{:S(2)}) copy-start(f32[2,1152]{1,0:T(2,128)} %get-tuple-element.56) | copy-start | bytes 27652
  424.3 24.3 %copy-start.22 = (f32[2,1152]{1,0:T(2,128)S(1)}, f32[2,1152]{1,0:T(2,128)}, u32[]{:S(2)}) copy-start(f32[2,1152]{1,0:T(2,128)} %get-tuple-element.54) | copy-start | bytes 27652
  424.3 24.4 %copy-start.24 = (f32[2,1152]{1,0:T(2,128)S(1)}, f32[2,1152]{1,0:T(2,128)}, u32[]{:S(2)}) copy-start(f32[2,1152]{1,0:T(2,128)} %get-tuple-element.64) | copy-start | bytes 27652
  424.3 38.1 %copy-start.36 = (u32[32]{0:T(128)S(1)}, u32[32]{0:T(128)}, u32[]{:S(2)}) copy-start(u32[32]{0:T(128)} %constant.94) | copy-start | bytes 388
  424.3 40.7 %copy-start.28 = (f32[2]{0:T(128)S(1)}, f32[2]{0:T(128)}, u32[]{:S(2)}) copy-start(f32[2]{0:T(128)} %compare_convert_fusion.1) | copy-start | bytes 28
  424.3 40.8 %copy-start.8 = (bf16[2,256,1152]{2,1,0:T(8,128)(2,1)S(1)}, bf16[2,256,1152]{2,1,0:T(8,128)(2,1)}, u32[]{:S(2)}) copy-start(bf16[2,256,1152]{2,1,0:T(8,128)(2,1)} %copy-done.7) | copy-start | bytes 3538948
  424.3 40.8 %copy-start.33 = (bf16[2,256,1152]{2,1,0:T(8,128)(2,1)S(1)}, bf16[2,256,1152]{2,1,0:T(8,128)(2,1)}, u32[]{:S(2)}) copy-start(bf16[2,256,1152]{2,1,0:T(8,128)(2,1)} %get-tuple-element.34) | copy-start | bytes 3538948
  464.3 0.7 copy-start.12
  465.1 1.8 copy-start.4
  465.1 2.3 copy-start.35
  467.3 6.3 copy-start.31
  467.3 6.3 copy-start.32
  581.2 2.8 copy-start.6
  584.0 4.2 copy-start.15
  586.2 4.6 copy-start.2
Sparse Core Ops, SparseCore 0:
  465.1 68.1 all-reduce.3

commit v6 on v5

--- a/solution.py
+++ b/solution.py
@@ -1,4 +1,5 @@
 import functools
+import math
 
 import jax
 import jax.numpy as jnp
@@ -336,29 +337,6 @@
     return opening, [f for _, _, f in todo], last
 
 
-def scatter_kernel(n, cuts, lags, *refs):
-    at = Place()
-    at.greet_all()
-    opening, steps, last = scatter_steps(at, cuts, refs[:n], refs[n : 2 * n], refs[2 * n :], lags)
-    for step in opening + steps:
-        step()
-    last()
-    at.drain(opening + steps)
-
-
-def scatter(grads, cuts, lags):
-    n = len(grads)
-    return pl.pallas_call(
-        functools.partial(scatter_kernel, n, cuts, lags),
-        out_shape=[jax.ShapeDtypeStruct(w.shape[1:], jnp.bfloat16) for w in grads],
-        in_specs=[pl.BlockSpec(memory_space=pl.ANY)] * n,
-        out_specs=[pl.BlockSpec(memory_space=pl.ANY)] * n,
-        scratch_shapes=scatter_scratch(grads, cuts),
-        compiler_params=pltpu.CompilerParams(
-            collective_id=1, has_side_effects=True, vmem_limit_bytes=60 * 2**20
-        ),
-        name="gradient_scatter",
-    )(*grads)
 def head_window(h):
     first = jnp.minimum(h * HDIM // LANES, HEADS * HDIM // LANES - 2) * LANES
     lane = lax.broadcasted_iota(jnp.int32, (1, 2 * LANES), 1) + first
@@ -382,6 +360,32 @@
     )
 
 
+def head_pick(width):
+    row = lax.broadcasted_iota(jnp.int32, (width, LANES), 0)
+    first = lax.broadcasted_iota(jnp.int32, (width, LANES), 1) * HDIM
+    return ((row >= first) & (row < first + HDIM)).astype(jnp.float32).astype(jnp.bfloat16)
+
+
+def head_spread(width):
+    lane = lax.broadcasted_iota(jnp.int32, (LANES, width), 1)
+    first = lax.broadcasted_iota(jnp.int32, (LANES, width), 0) * HDIM
+    return ((lane >= first) & (lane < first + HDIM)).astype(jnp.float32).astype(jnp.bfloat16)
+
+
+def rope_tables(band, rows, cols, width):
+    quarter = HDIM // 4
+    shape = (rows * cols, width)
+    token = lax.broadcasted_iota(jnp.int32, shape, 0)
+    lane = lax.broadcasted_iota(jnp.int32, shape, 1) % HDIM
+    power = (lane % quarter).astype(jnp.float32) * (-math.log(10000.0) / quarter)
+    by_row = band * rows + (token // cols).astype(jnp.float32)
+    index = jnp.where(lane < 2 * quarter, by_row, (token % cols).astype(jnp.float32))
+    angle = index * jnp.exp(power)
+    sine = jnp.sin(angle)
+    low = (lane // quarter) % 2 == 0
+    return jnp.cos(angle), jnp.where(low, -sine, 0.0), jnp.where(low, 0.0, sine)
+
+
 def turn(values, cos, sin_next, sin_prev):
     width = values.shape[-1]
     after = pltpu.roll(values, width - HDIM // 4, 1)
@@ -398,19 +402,20 @@
 
 def qkv_back_kernel(
     x_ref, mod_ref, mid_ref, dq_ref, dk_ref, dv_ref, nq_ref, nk_ref, rq_ref, rk_ref, w_ref,
-    gains_ref, cos_ref, next_ref, prev_ref, pick_ref, spread_ref,
+    gains_ref, cos_ref, next_ref, prev_ref,
     dqkv_ref, dx_ref, sums_ref,
 ):
     width = x_ref.shape[-1]
     tables = (cos_ref[...], next_ref[...], prev_ref[...])
+    pick, spread = head_pick(width), head_spread(width)
     ins = ((dq_ref, nq_ref, rq_ref), (dk_ref, nk_ref, rk_ref))
     for part, (d_ref, n_ref, r_ref) in enumerate(ins):
         back = turn_back(d_ref[0].astype(jnp.float32) * HDIM ** (-0.5), *tables)
         unit = n_ref[0]
         sums_ref[0, 2 + part : 3 + part, :] = jnp.sum(back * unit, axis=0, keepdims=True)
         inner = back * gains_ref[part : part + 1, :]
-        mean = pick_dot(inner * unit, pick_ref[...]) * (1.0 / HDIM)
-        grad = (inner - unit * pick_dot(mean, spread_ref[...])) * pick_dot(r_ref[0], spread_ref[...])
+        mean = pick_dot(inner * unit, pick) * (1.0 / HDIM)
+        grad = (inner - unit * pick_dot(mean, spread)) * pick_dot(r_ref[0], spread)
         dqkv_ref[0, :, part * width : (part + 1) * width] = grad.astype(jnp.bfloat16)
     dqkv_ref[0, :, 2 * width : 3 * width] = dv_ref[0]
     d_normed = dot_t(dqkv_ref[0], w_ref[...])
@@ -423,7 +428,7 @@
     dx_ref[0] = mid_ref[0] + root * (inner - unit * jnp.mean(inner * unit, axis=-1, keepdims=True))
 
 
-def qkv_backward(x, mod, d_mid, dq, dk, dv, nq, nk, rq, rk, qp_all, gains, tables, pick, spread):
+def qkv_backward(x, mod, d_mid, dq, dk, dv, nq, nk, rq, rk, qp_all, gains, tables):
     images, length, width = x.shape
     row = lambda w: pl.BlockSpec((1, length, w), lambda i: (i, 0, 0))
     whole = lambda a: pl.BlockSpec(a.shape, lambda i: (0,) * a.ndim)
@@ -434,8 +439,7 @@
         + [row(width)] * 6
         + [row(LANES)] * 2
         + [pl.BlockSpec((width, 3 * width), lambda i: (0, 0)), whole(gains)]
-        + [whole(t) for t in tables]
-        + [whole(pick), whole(spread)],
+        + [whole(t) for t in tables],
         out_shape=[
             jax.ShapeDtypeStruct((images, length, 3 * width), jnp.bfloat16),
             jax.ShapeDtypeStruct((images, length, width), jnp.float32),
@@ -444,14 +448,136 @@
         out_specs=[row(3 * width), row(width), pl.BlockSpec((1, 4, width), lambda i: (i, 0, 0))],
         compiler_params=pltpu.CompilerParams(vmem_limit_bytes=60 * 2**20),
         name="qkv_backward",
-    )(x, mod, d_mid, dq, dk, dv, nq, nk, rq, rk, qp_all, gains, *tables, pick, spread)
-def forward_kernel(cuts, refs):
+    )(x, mod, d_mid, dq, dk, dv, nq, nk, rq, rk, qp_all, gains, *tables)
+def tail_scratch():
+    s = pltpu.SemaphoreType.DMA
+    wide = SMALL_COLS
+    return [
+        pltpu.VMEM((SMALL_ROWS, wide), jnp.float32),
+        pltpu.VMEM((2, SMALL_ROWS, wide), jnp.float32),
+        pltpu.VMEM((8, SMALL_ROWS, wide), jnp.bfloat16),
+        pltpu.VMEM((8, GROUPS, 2 * LANES), jnp.float32),
+        s((8,)),
+        s((8,)),
+    ]
+
+
+def tail_steps(at, ins, outs, scratch):
+    part_ref, ada_ref, slope_ref = ins
+    all_ref, cond_ref = outs
+    acc, inbox, blocks, cond, ss, rs = scratch
+    width = HEADS * HDIM
+    z = at.z
+    line = (at.xpeer, at.line(at.far[1]), at.line((z + 2) % 4))
+
+    def copy(r):
+        if r < 2:
+            return at.copy(acc, inbox.at[r], ss.at[r], rs.at[r], (at.cpeer, at.ypeer)[r])
+        ref, k = (blocks, r - 2) if r < 5 else (cond, r - 5)
+        start, size = ((at.g, 1), (2 * z, 2), (4 * (z // 2), 4))[k]
+        src = ref.at[pl.ds(start, size)]
+        return at.copy(src, src, ss.at[r], rs.at[r], line[k])
+
+    def pack():
+        row = lax.broadcasted_iota(jnp.int32, (SMALL_ROWS, 1), 0)
+        value = acc[...]
+        rest = value - value.astype(jnp.bfloat16).astype(jnp.float32)
+        last = rest - rest.astype(jnp.bfloat16).astype(jnp.float32)
+        value = jnp.where(row == GAIN_ROW + 1, rest, jnp.where(row == GAIN_ROW + 2, last, value))
+        blocks[at.g] = value.astype(jnp.bfloat16)
+
+    def cond_rows():
+        flat = blocks[...].reshape(8 * SMALL_ROWS, SMALL_COLS)
+        row = lax.broadcasted_iota(jnp.int32, (8 * SMALL_ROWS, 1), 0) % SMALL_ROWS
+        silu = jnp.zeros((8 * SMALL_ROWS, ada_ref.shape[0]), jnp.float32)
+        for k in range(6):
+            product = dot_t(flat[:, :width], ada_ref[:, k * width : (k + 1) * width])
+            silu = jnp.where((row % 6 == k) & (row < GAIN_ROW), product, silu)
+        by_group = lax.dot_general(
+            flat[:, width:].astype(jnp.float32),
+            silu,
+            (((0,), (0,)), ((), ())),
+            precision=lax.Precision.HIGHEST,
+            preferred_element_type=jnp.float32,
+        )
+        cond[at.g] = jnp.zeros((GROUPS, 2 * LANES), jnp.float32)
+        cond[at.g, :, : ada_ref.shape[0]] = by_group[:GROUPS] * slope_ref[...]
+
+    def step(r):
+        if at.draining:
+            return
+        if r > 0:
+            copy(r - 1).wait()
+        if r == 0:
+            acc[...] = part_ref[...]
+        elif r <= 2:
+            acc[...] = acc[...] + inbox[r - 1]
+        if r == 2:
+            pack()
+        if r == 5:
+            cond_rows()
+        if r < 8:
+            copy(r).start()
+        else:
+            all_ref[...] = blocks[...]
+            cond_ref[...] = cond[...]
+
+    return [functools.partial(step, r) for r in range(9)]
+
+
+SMALL_ROWS, SMALL_COLS, GAIN_ROW = 16, HEADS * HDIM + LANES, 12
+
+
+def scatter_kernel(n, cuts, lags, *refs):
+    at = Place()
+    at.greet_all()
+    ins, small_in = refs[:n], refs[n : n + 3]
+    outs, small_out = refs[n + 3 : 2 * n + 3], refs[2 * n + 3 : 2 * n + 5]
+    small = tail_steps(at, small_in, small_out, refs[2 * n + 5 : 2 * n + 11])
+    opening, steps, last = scatter_steps(at, cuts, ins, outs, refs[2 * n + 11 :], lags)
+    small[0]()
+    for step in opening:
+        step()
+    small = small[1:]
+    for k, step in enumerate(steps):
+        step()
+        if k % 3 == 2 and small:
+            small[0]()
+            small = small[1:]
+    for step in small:
+        step()
+    last()
+    at.drain(opening + steps)
+
+
+def scatter(grads, cuts, lags, part, w_ada, slope):
+    n = len(grads)
+    any_ref = pl.BlockSpec(memory_space=pl.ANY)
+    vmem = pl.BlockSpec(memory_space=pltpu.VMEM)
+    return pl.pallas_call(
+        functools.partial(scatter_kernel, n, cuts, lags),
+        out_shape=[jax.ShapeDtypeStruct(w.shape[1:], jnp.bfloat16) for w in grads]
+        + [
+            jax.ShapeDtypeStruct((8, SMALL_ROWS, SMALL_COLS), jnp.bfloat16),
+            jax.ShapeDtypeStruct((8, GROUPS, 2 * LANES), jnp.float32),
+        ],
+        in_specs=[any_ref] * n + [vmem] * 3,
+        out_specs=[any_ref] * n + [vmem] * 2,
+        scratch_shapes=tail_scratch() + scatter_scratch(grads, cuts),
+        compiler_params=pltpu.CompilerParams(
+            collective_id=1, has_side_effects=True, vmem_limit_bytes=60 * 2**20
+        ),
+        name="gradient_scatter",
+    )(*grads, part, w_ada, slope)
+
+
+def forward_kernel(cuts, cols, refs):
     n = len(cuts)
     soon = sum(cut[5] == 0 for cut in cuts)
     at = Place()
-    x_ref, part_ref, group_ref, gains_ref, cos_ref, next_ref, prev_ref, pick_ref, spread_ref = refs["in"]
-    normed_ref, q_ref, nq_ref, nk_ref, rq_ref, rk_ref, o_ref, inv_ref, mod_ref, kv_out = refs["out"]
-    kv, w_buf, mod_buf, mod_in, w_sem, ms, mr, ks, kr, os = refs["scratch"]
+    x_ref, part_ref, group_ref, gains_ref, band_ref = refs["in"]
+    normed_ref, q_ref, nq_ref, nk_ref, rq_ref, rk_ref, o_ref, inv_ref, mod_ref, *table_refs, kv_out = refs["out"]
+    kv, w_buf, pick_ref, spread_ref, mod_buf, mod_in, w_sem, ms, mr, ks, kr, os = refs["scratch"]
     ins, outs = refs["shards"], refs["full"]
     images, length, width = x_ref.shape
     parts = [(i, s) for i in range(images) for s in (0, 1)]
@@ -519,7 +645,7 @@
         unit = values * pick_dot(inv, spread_ref[...])
         n_ref[i] = unit
         scaled = unit * gains_ref[part : part + 1, :]
-        return turn(scaled, cos_ref[...], next_ref[...], prev_ref[...]).astype(jnp.bfloat16)
+        return turn(scaled, *(t[...] for t in table_refs)).astype(jnp.bfloat16)
 
     def key_part(i):
         norm(i)
@@ -546,11 +672,28 @@
         lane = lax.broadcasted_iota(jnp.int32, (1, LANES), 1)
         inv_ref[i] = jnp.where(lane == h, inv, inv_ref[i])
 
+    def prepare():
+        pick_ref[...] = head_pick(width)
+        spread_ref[...] = head_spread(width)
+
+        def block(r, _):
+            rows_of = pl.ds(pl.multiple_of(r * cols, cols), cols)
+            row = band_ref[0:1, 0:1] * (length // cols) + r.astype(jnp.float32)
+            for ref, value in zip(table_refs, rope_tables(row, 1, cols, width)):
+                ref[rows_of, :] = value
+            return 0
+
+        lax.fori_loop(0, length // cols, block, 0)
+
+    if not n:
+        prepare()
     if n:
         for k in range(3):
             mod_step(k)
             for step in steps[2 * k : 2 * k + 2]:
                 step()
+                if k == 0 and step is steps[0]:
+                    prepare()
         mod_step(3)
         for step in steps[6:first]:
             step()
@@ -609,7 +752,7 @@
         at.drain([functools.partial(ready, i)])
 
 
-def forward(x, mod_part, groups, gains, tables, pick, spread, shards, cuts):
+def forward(x, mod_part, groups, gains, band, cols, shards, cuts):
     n = len(cuts)
     images, length, width = x.shape
     bands = lax.axis_size("band")
@@ -618,13 +761,16 @@
     bf = jnp.bfloat16
     any_ref = pl.BlockSpec(memory_space=pl.ANY)
     vmem = pl.BlockSpec(memory_space=pltpu.VMEM)
-    args = [x, mod_part, groups, gains, *tables, pick, spread]
+    args = [x, mod_part, groups, gains, band]
     rows = lambda w, d: jax.ShapeDtypeStruct((images, length, w), d)
     outs = [rows(width, bf)] * 2 + [rows(width, jnp.float32)] * 2 + [rows(LANES, jnp.float32)] * 2
     outs += [rows(width, bf), rows(LANES, jnp.float32), jax.ShapeDtypeStruct((images, mod_part.shape[1]), jnp.float32)]
+    outs += [jax.ShapeDtypeStruct((length, width), jnp.float32)] * 3
     scratch = [
         pltpu.VMEM(keys, bf),
         pltpu.VMEM((width, 3 * width), bf),
+        pltpu.VMEM((width, LANES), bf),
+        pltpu.VMEM((LANES, width), bf),
         pltpu.VMEM(mod_part.shape, jnp.float32),
         pltpu.VMEM((3,) + mod_part.shape, jnp.float32),
         s((8,)),
@@ -643,7 +789,7 @@
             groups_of.append(refs[start : start + size])
             start += size
         names = ("in", "shards", "out", "full", "scratch", "sems")
-        forward_kernel(cuts, dict(zip(names, groups_of)))
+        forward_kernel(cuts, cols, dict(zip(names, groups_of)))
 
     return pl.pallas_call(
         kernel,
@@ -804,21 +950,6 @@
     return jax.nn.silu(gate_in) * up_in
 
 
-def rope_tables(band, rows, cols):
-    quarter = HDIM // 4
-    lane = jnp.arange(HDIM, dtype=jnp.int32)
-    part = lane // quarter
-    frequency = 10000.0 ** (-(lane % quarter).astype(jnp.float32) / quarter)
-    row_index = jnp.repeat(band * rows + jnp.arange(rows, dtype=jnp.int32), cols)
-    col_index = jnp.tile(jnp.arange(cols, dtype=jnp.int32), rows)
-    index = jnp.where(part[None, :] < 2, row_index[:, None], col_index[:, None])
-    angle = index.astype(jnp.float32) * frequency[None, :]
-    sine = jnp.sin(angle)
-    low = (part % 2 == 0)[None, :]
-    tables = (jnp.cos(angle), jnp.where(low, -sine, 0.0), jnp.where(low, 0.0, sine))
-    return [jnp.tile(t, (1, HEADS)) for t in tables]
-
-
 def half_cuts(ref, axis, base, size, own_parts, shared_parts):
     unit = size // 2 // (own_parts + 2 * shared_parts)
     return (axis, size // 2, own_parts * unit, shared_parts * unit, base, ref)
@@ -854,6 +985,8 @@
     ada_rows, ada_cols, bias_cols = w_ada.shape[0], w_ada.shape[1], b_ada.shape[0]
     fits = (
         lax.axis_size("grp") == 8
+        and images == 2
+        and width == HEADS * HDIM
         and w_qkv.shape[0] % 16 == 0
         and 4 * width % 4608 == 0
         and 2 * ff % 3072 == 0
@@ -864,8 +997,9 @@
     full = lambda w: w.reshape(-1, w.shape[-1])
     onehot = (group_ids[:, None] == jnp.arange(GROUPS, dtype=jnp.int32)[None, :]).astype(jnp.float32)
     cond_rows = lax.dynamic_slice_in_dim(cond_table, grp * ada_rows, ada_rows, axis=1)
-    silu_rows, silu_pull = jax.vjp(jax.nn.silu, cond_rows)
-    silu_rows = silu_rows.astype(bf)
+    sigmoid = jax.nn.sigmoid(cond_rows)
+    silu_rows = (cond_rows * sigmoid).astype(bf)
+    silu_slope = sigmoid * (1.0 + cond_rows * (1.0 - sigmoid))
     mod_part = jnp.dot(silu_rows, w_ada, preferred_element_type=jnp.float32)
     bias_part = lax.dynamic_update_slice_in_dim(
         jnp.zeros((ada_cols,), jnp.float32), b_ada.astype(jnp.float32), grp * bias_cols, axis=0
@@ -873,15 +1007,11 @@
     mod_part = mod_part + bias_part[None, :]
     live_mask = (jnp.arange(images, dtype=jnp.int32) < live_count[0]).astype(jnp.float32)
 
-    tables = rope_tables(band_order[0], rows, cols)
     gains = jnp.stack([jnp.tile(q_gain, HEADS), jnp.tile(k_gain, HEADS)])
-    head_of = jnp.arange(width, dtype=jnp.int32) // HDIM
-    pick = (head_of[:, None] == jnp.arange(LANES, dtype=jnp.int32)[None, :]).astype(jnp.float32)
-    spread = pick.T
-    pick, spread = pick.astype(bf), spread.astype(bf)
     x = patches.reshape(images, length, width)
     groups = jnp.pad(onehot.T, ((0, 0), (0, LANES - images)))
-    common = (groups, gains, tables, pick, spread)
+    band = jnp.broadcast_to(band_order.astype(jnp.float32)[:, None], (1, LANES))
+    common = (groups, gains, band, cols)
     if fits:
         shards = [w_qp, w_gu, w_down]
         cuts = [half_cuts(0, 1, 0, 4 * width, 1, 1), half_cuts(1, 1, 0, 2 * ff, 4, 1)]
@@ -890,7 +1020,9 @@
         qp_all, gu_all, down_all = (lax.all_gather(w, "grp", axis=0, tiled=True) for w in (w_qp, w_gu, w_down))
         mod_part = lax.psum(mod_part, "grp")
         shards, cuts = [qp_all], []
-    normed_one, query, nq, nk, rq, rk, attended, inv, mod, kv_all, *rest = forward(x, mod_part, *common, shards, cuts)
+    outs = forward(x, mod_part, *common, shards, cuts)
+    normed_one, query, nq, nk, rq, rk, attended, inv, mod = outs[:9]
+    tables, kv_all, rest = outs[9:12], outs[12], outs[13:]
     if fits:
         qp_all, gu_all, down_all = (full(w) for w in rest)
     mod = mod.reshape(images, 6, width)
@@ -933,54 +1065,52 @@
         (2, 2, 1, 2),
     )
     d_qkv, d_x, sums = qkv_backward(
-        x, mod, d_middle, d_query, d_kv[0], d_kv[1], nq, nk, rq, rk, qp_all, gains, tables, pick, spread
+        x, mod, d_middle, d_query, d_kv[0], d_kv[1], nq, nk, rq, rk, qp_all, gains, tables
     )
     d_patches = d_x.reshape(images, rows, cols, width)
     d_w_qkv = jnp.einsum("td,te->de", flat(normed_one), flat(d_qkv), preferred_element_type=jnp.float32).astype(bf)
     d_w_qp = jnp.concatenate([d_w_qkv, d_w_proj], axis=1)
 
-    d_mod_part = jnp.concatenate(
-        [sums[:, 0], sums[:, 1], d_gate_one, d_shift_two, d_scale_two, d_gate_two], axis=-1
-    )
+    d_mod_part = jnp.stack([sums[:, 0], sums[:, 1], d_gate_one, d_shift_two, d_scale_two, d_gate_two], axis=1)
     gain_part = jnp.sum(sums[:, 2:4].reshape(images, 2, HEADS, HDIM), axis=(0, 2))
-    summed = lax.psum(jnp.concatenate([d_mod_part.reshape(-1), gain_part.reshape(-1)]), "band")
-    d_modulation = summed[: images * ada_cols].reshape(images, ada_cols).astype(bf)
-    gain_sum = summed[images * ada_cols :]
-    high = lax.reduce_precision(gain_sum, 8, 7)
-    middle_part = lax.reduce_precision(gain_sum - high, 8, 7)
-    pieces = jnp.stack([high, middle_part, gain_sum - high - middle_part]).astype(bf)
-    payload = jnp.concatenate([d_modulation.reshape(-1), onehot.astype(bf).reshape(-1), pieces.reshape(-1)])
-    payload = lax.all_gather(payload, "grp", axis=0)
-    parts = payload.shape[0]
-    at_onehot = images * ada_cols
-    at_gain = at_onehot + images * GROUPS
-    d_mod_all = payload[:, :at_onehot].reshape(parts * images, ada_cols)
-    onehot_all = payload[:, at_onehot:at_gain].reshape(parts * images, GROUPS)
-    gain_all = jnp.sum(payload[:, at_gain:].astype(jnp.float32).reshape(parts * 3, 2, HDIM), axis=0)
+    if fits:
+        tags = jnp.pad(jnp.repeat(onehot * (1.0 / lax.axis_size("band")), 6, axis=0), ((0, 0), (0, LANES - GROUPS)))
+        small = jnp.concatenate([d_mod_part.reshape(images * 6, width), tags], axis=1)
+        gain_row = jnp.pad(gain_part.reshape(1, -1), ((0, 0), (0, SMALL_COLS - 2 * HDIM)))
+        small = jnp.concatenate([small, gain_row, gain_row, gain_row, jnp.zeros_like(gain_row)])
+        cuts = [half_cuts(0, 0, 0, w_down.shape[0], 2, 1), half_cuts(1, 1, 0, 4 * width, 8, 5)]
+        d_gu = rest[0]
+        d_down, d_qp, gathered, cond_blocks = scatter(
+            [by_shard(d_w_down), by_shard(d_w_qp)], cuts, (2, 2, 1, 2), small, w_ada, silu_slope
+        )
+        d_mod_all = gathered[:, :GAIN_ROW, :width].reshape(-1, ada_cols)
+        onehot_all = gathered[:, 0:GAIN_ROW:6, width : width + GROUPS].reshape(-1, GROUPS)
+        gain_all = gathered[:, GAIN_ROW : GAIN_ROW + 3, : 2 * HDIM].astype(jnp.float32)
+        gain_all = jnp.sum(gain_all, axis=(0, 1)).reshape(2, HDIM)
+        d_cond = jnp.swapaxes(cond_blocks[:, :, :ada_rows], 0, 1).reshape(GROUPS, -1)
+    else:
+        d_gu, d_down, d_qp = (
+            lax.psum(lax.psum_scatter(w, "grp", scatter_dimension=0, tiled=True), "band")
+            for w in (d_w_gu, d_w_down, d_w_qp)
+        )
+        d_modulation = lax.psum(d_mod_part.reshape(images, ada_cols), "band").astype(bf)
+        gain_all = lax.psum(gain_part, ("grp", "band"))
+        payload = jnp.concatenate([d_modulation, onehot.astype(bf)], axis=1)
+        payload = lax.all_gather(payload, "grp", axis=0, tiled=True)
+        d_mod_all, onehot_all = payload[:, :ada_cols], payload[:, ada_cols:]
+        d_silu = jnp.einsum("be,de->bd", d_mod_all, w_ada, preferred_element_type=jnp.float32)
+        d_silu = jnp.dot(
+            onehot_all.astype(jnp.float32).T,
+            d_silu,
+            precision=lax.Precision.HIGHEST,
+            preferred_element_type=jnp.float32,
+        )
+        d_cond = lax.all_gather(d_silu * silu_slope, "grp", axis=1, tiled=True)
     silu_all = jnp.dot(onehot_all, silu_rows, preferred_element_type=jnp.float32).astype(bf)
     d_w_ada = jnp.einsum("bd,be->de", silu_all, d_mod_all, preferred_element_type=jnp.float32)
     d_b_ada = lax.dynamic_slice_in_dim(
         jnp.sum(d_mod_all.astype(jnp.float32), axis=0), grp * bias_cols, bias_cols, axis=0
     )
-    d_silu = jnp.einsum("be,de->bd", d_mod_all, w_ada, preferred_element_type=jnp.float32)
-    d_silu = jnp.dot(
-        onehot_all.astype(jnp.float32).T,
-        d_silu,
-        precision=lax.Precision.HIGHEST,
-        preferred_element_type=jnp.float32,
-    )
-    d_cond = lax.all_gather(silu_pull(d_silu)[0], "grp", axis=1, tiled=True)
-
-    if fits:
-        d_gu = rest[0]
-        cuts = [half_cuts(0, 0, 0, w_down.shape[0], 2, 1)]
-        cuts += [half_cuts(1, 1, 0, 4 * width, 8, 5)]
-        d_down, d_qp = scatter([by_shard(d_w_down), by_shard(d_w_qp)], cuts, (2, 2, 1, 2))
-    else:
-        d_gu, d_down, d_qp = (
-            lax.psum(lax.psum_scatter(w, "grp", scatter_dimension=0, tiled=True), "band")
-            for w in (d_w_gu, d_w_down, d_w_qp)
-        )
     wide = lambda a: a.astype(jnp.float32)
     return (
         patches_out,

time: 639 us -> 599 us (0.937); the launches traced: 636 us -> 589 us
  blocking collectives: 43.9 us -> 0 us
  between operations: 16.8 us -> 2.94 us
  Pallas kernels: 434 us -> 446 us
    all_gather x1 -> x0, blocking collectives: 30.5 us -> none  [body(): d_cond = lax.all_gather(silu_pull(d_silu)[0], 'grp', axis=1, tiled=True)]
    psum x1 -> x0, blocking collectives: 13.4 us -> none  [body(): lax.psum(jnp.concatenate([d_mod_part.reshape(-1), gain_part.reshape(-1)])...]
    pallas_call x1, Pallas kernels: 98.2 us -> 110 us  [scatter(): pl.pallas_call(functools.partial(scatter_kernel, n, cuts, lags), out_shap...]
  transfers between devices with their start and end apart: 1 -> 0, of which waited for: 0 -> 0; matrix products, arithmetic and copies ran while one was open for 4% -> 0% of each run, Pallas kernels for 15% -> 0%
where the time goes in v6:
time: 599 us; the launch traced here: 589 us
  Pallas kernels  446 us (74%)
  matrix products  97.7 us (16%)
  other arithmetic  24 us (4%)
  local copies, waits for them, and re-layouts  18.4 us (3%)
    pallas_call x1, Pallas kernels, forward(): pl.pallas_call(kernel, out_shape=outs + [jax.ShapeDtypeStruct(keys, bf)]...  186 us
    pallas_call x1, Pallas kernels, attention_backward(): pl.pallas_call(functools.partial(attention_back_kernel, n, cuts, lags), o...  129 us
    pallas_call x1, Pallas kernels, scatter(): pl.pallas_call(functools.partial(scatter_kernel, n, cuts, lags), out_shap...  110 us
    pallas_call x1, Pallas kernels, qkv_backward(): pl.pallas_call(qkv_back_kernel, grid=(images,), in_specs=[row(width), pl....  21.8 us
    dot_general x1, matrix products, body(): jnp.einsum('tf,df->td', d_pre, gu_all, preferred_element_type=jnp.float32)  17 us
    dot_general x1, matrix products, body(): jnp.einsum('td,fd->tf', d_mlp, down_all, preferred_element_type=jnp.float32)  12.5 us
    dot_general x1, matrix products, body(): jnp.einsum('td,tf->df', normed_two_low, d_pre, preferred_element_type=jnp...  12.3 us

profile of v6, /device:TPU:0, one launch (start us, length us, event | category | flops | bytes accessed | tf_op | source)
XLA Modules:
  0.0 588.9 jit_solution(4341307662407154105)
XLA Ops:
  1.4 0.5 compare_convert_fusion
  1.9 0.8 convert_dynamic-update-slice_fusion
  2.7 2.8 convolution_add_fusion.refs_1_
  5.5 0.7 iota_compare_fusion.2
  6.2 0.6 pad_convert_fusion.refs_2_
  6.8 0.7 tile.5
  7.5 0.7 tile.4
  8.3 0.6 pad_maximum_fusion.4.refs_3_.gains_ref
  9.6 0.5 broadcast_in_dim.11.refs_4_
  10.1 1.2 pad_maximum_fusion.3.refs_5_
  11.2 1.3 pad_maximum_fusion.2.refs_6_
  12.6 185.5 %forward.1 = (bf16[2,256,1152]{2,1,0:T(8,128)(2,1)}, bf16[2,256,1152]{2,1,0:T(8,128)(2,1)}, f32[2,256,1152]{2,1,0:T(8,128)}, f32[2,256,1152]{2,1,0:T(8,128)}, f3...) custom-call(bf16[2,256,1152]{2,1,0:T(8,128)(2,1)} %bitcast.102, ...), custom_call_target="tpu_custom_call" | custom-call | tf_op jit(solution)/shard_map/forward/pallas_call | solution.py:794
  198.1 0.9 reshape.187.mod_ref
  199.1 0.6 copy-done.16
  199.6 5.5 multiply_reduce_fusion.4
  205.8 1.2 copy-done.31
  207.0 11.0 %fusion.18 = f32[512,6144]{1,0:T(8,128)} fusion(bf16[512,1152]{1,0:T(8,128)(2,1)S(1)} %bitcast.107, bf16[1152,6144]{1,0:T(8,128)(2,1)S(1)} %bitcast.113), kind=kOutput, calls=%fused_computation.75 | convolution fusion | flops 7247757312 | bytes 27918336 | tf_op jit(solution)/shard_map/dot_general | solution.py:1037
  218.3 12.5 %fusion.4 = (bf16[512,3072]{1,0:T(8,128)(2,1)S(1)}, bf16[512,3072]{1,0:T(8,128)(2,1)S(1)}, bf16[512,3072]{1,0:T(8,128)(2,1)}) fusion(f32[512,6144]{1,0:T(8,128)} %fusion.18, bf16[512,1152]{1,0:T(8,128)(2,1)S(1)} %bitcast.105, bf16[3072,1152]{1,0:T(8,128)(2,1)} %bitcast.114), kind=kOutput, calls=%fused_computation.11 | convolution fusion | flops 3649044480 | bytes 30277632 | tf_op jit(solution)/shard_map/td,fd->tf/dot_general | solution.py:1048
  230.8 3.4 pad_maximum_fusion.1
  234.3 1.1 copy-done.6
  235.4 17.0 %multiply_reduce_fusion.1 = (f32[2,1152]{1,0:T(2,128)}, f32[2,256]{1,0:T(2,128)}, f32[2,1152]{1,0:T(2,128)}, f32[2,256,1152]{2,1,0:T(8,128)}) fusion(f32[2,256,1152]{2,1,0:T(8,128)S(1)} %get-tuple-element.70, f32[2,256]{1,0:T(2,128)S(1)} %fusion.14, f32[2,1152]{1,0:T(2,128)} %copy-done.22, bf16[2,256,6144]{2,1,0:T(8,128)(2,1)} %bitcast.101, ...), kind=kOutput, calls=%fused_computation.27 | convolution fusion | flops 7251880960 | bytes 25197568 | tf_op jit(solution)/shard_map/tf,df->td/dot_general | solution.py:1051
  252.4 0.7 multiply_multiply_fusion
  253.1 11.7 %multiply_reduce_fusion = (f32[2,1152]{1,0:T(2,128)}, bf16[2,256,1152]{2,1,0:T(8,128)(2,1)}, f32[2,1152]{1,0:T(2,128)}, f32[2,256,1152]{2,1,0:T(8,128)S(1)}) fusion(bf16[2,8,32,1152]{3,2,1,0:T(8,128)(2,1)S(1)} %copy-done.2, f32[2]{0:T(128)} %compare_convert_fusion, f32[2,256,1152]{2,1,0:T(8,128)S(1)} %get-tuple-element.70, ...), kind=kOutput, calls=%fused_computation.26 | convolution fusion | flops 3633311232 | bytes 22061064 | tf_op jit(solution)/shard_map/dot_general | solution.py:1040
  264.9 5.8 convolution_convert_fusion.2
  270.7 0.8 copy.38
  271.6 12.3 %convolution_convert_fusion = bf16[1152,6144]{1,0:T(8,128)(2,1)} fusion(bf16[512,1152]{1,0:T(8,128)(2,1)} %bitcast.108, bf16[512,3072]{1,0:T(8,128)(2,1)} %copy-done.6, bf16[512,3072]{1,0:T(8,128)(2,1)S(1)} %copy-done.5), kind=kOutput, calls=%fused_computation | convolution fusion | flops 7267418112 | bytes 21626880 | tf_op jit(solution)/shard_map/td,tf->df/dot_general | solution.py:1050
  283.9 128.7 %attention_backward.1 = (f32[2,256,1152]{2,1,0:T(8,128)}, bf16[2,2,256,1152]{3,2,1,0:T(8,128)(2,1)}, bf16[144,6144]{1,0:T(8,128)(2,1)}) custom-call(bf16[2,256,1152]{2,1,0:T(8,128)(2,1)} %get-tuple-element.43.q_ref, bf16[2,256,1152]{2,1,0:T(8,128)(2,1)} %bitcast.104, f32[2,128,256]{2,1,0:T(8,128)} %bitcast.109, ...), custom_call_target="tpu_custom_call" | custom-call | tf_op jit(solution)/shard_map/attention_backward/pallas_call | solution.py:917
  412.6 3.2 slice_bitcast_fusion
  415.8 21.8 %qkv_backward.1 = (bf16[2,256,3456]{2,1,0:T(8,128)(2,1)}, f32[2,256,1152]{2,1,0:T(8,128)}, f32[2,4,1152]{2,1,0:T(4,128)}) custom-call(bf16[2,256,1152]{2,1,0:T(8,128)(2,1)} %bitcast.103, f32[2,6,1152]{2,1,0:T(8,128)} %copy-done.16, f32[2,256,1152]{2,1,0:T(8,128)} %copy-done, f32[2,256,1152]{2,1,0:T(8,128)} %get-tuple-element.46.dq_ref, ...), custom_call_target="tpu_custom_call" | custom-call | tf_op jit(solution)/shard_map/qkv_backward/pallas_call | solution.py:435
  438.1 9.1 %convolution_convert_fusion.1 = bf16[3072,1152]{1,0:T(8,128)(2,1)} fusion(bf16[512,3072]{1,0:T(8,128)(2,1)} %get-tuple-element.73, bf16[512,1152]{1,0:T(8,128)(2,1)S(1)} %fusion.9), kind=kOutput, calls=%fused_computation.3 | convolution fusion | flops 3627417600 | bytes 11403264 | tf_op jit(solution)/shard_map/tf,td->fd/dot_general | solution.py:1047
  447.2 1.7 fusion.1
  449.5 4.7 fusion
  454.3 4.8 pad_maximum_fusion
  459.9 2.1 concatenate.23.refs_2_
  461.9 1.4 add_multiply_fusion.refs_4_
  463.3 109.9 %gradient_scatter.1 = (bf16[384,1152]{1,0:T(8,128)(2,1)}, bf16[144,4608]{1,0:T(8,128)(2,1)}, bf16[8,16,1280]{2,1,0:T(8,128)(2,1)}, f32[8,8,256]{2,1,0:T(8,128)}) custom-call(bf16[8,384,1152]{2,1,0:T(8,128)(2,1)} %bitcast.100, bf16[8,144,4608]{2,1,0:T(8,128)(2,1)} %bitcast.95, f32[16,1280]{1,0:T(8,128)} %concatenate.23.refs_2_, bf16[144,6912]{1,0:T(8,128)(2,1)} %refs_3_.1, ...), custom_call_target="tpu_custom_call" | custom-call | tf_op jit(solution)/shard_map/gradient_scatter/pallas_call | solution.py:557
  573.2 0.8 slice_bitcast_fusion.2
  574.1 0.7 reshape.204
  574.8 1.0 slice.80
  576.0 0.9 slice.79
  576.9 3.6 fusion.12
  580.6 0.7 dynamic_slice.7
  581.3 1.4 slice_convert_fusion
  582.7 0.8 convert_reduce_fusion.1
  583.5 0.6 fusion.17
  584.0 0.9 slice_convert_fusion.3
  584.9 2.2 slice_convert_fusion.1
  587.1 1.3 convert_element_type.148
  (100 shorter events, 3.5 us)
Async XLA Ops:
  0.6 9.4 %copy-start.17 = (bf16[144,1152]{1,0:T(8,128)(2,1)S(1)}, bf16[144,1152]{1,0:T(8,128)(2,1)}, u32[]{:S(2)}) copy-start(bf16[144,1152]{1,0:T(8,128)(2,1)} %param.26) | copy-start | bytes 995332
  0.7 9.4 %copy-start.12 = (bf16[144,3456]{1,0:T(8,128)(2,1)S(1)}, bf16[144,3456]{1,0:T(8,128)(2,1)}, u32[]{:S(2)}) copy-start(bf16[144,3456]{1,0:T(8,128)(2,1)} %param.23) | copy-start | bytes 2985988
  2.7 8.5 %copy-start.13 = (bf16[144,3072]{1,0:T(8,128)(2,1)S(1)}, bf16[144,3072]{1,0:T(8,128)(2,1)}, u32[]{:S(2)}) copy-start(bf16[144,3072]{1,0:T(8,128)(2,1)} %param.28) | copy-start | bytes 2654212
  2.7 8.5 %copy-start.14 = (bf16[144,3072]{1,0:T(8,128)(2,1)S(1)}, bf16[144,3072]{1,0:T(8,128)(2,1)}, u32[]{:S(2)}) copy-start(bf16[144,3072]{1,0:T(8,128)(2,1)} %param.27) | copy-start | bytes 2654212
  12.6 187.0 %copy-start.1 = (bf16[2,8,32,1152]{3,2,1,0:T(8,128)(2,1)S(1)}, bf16[2,8,32,1152]{3,2,1,0:T(8,128)(2,1)}, u32[]{:S(2)}) copy-start(bf16[2,8,32,1152]{3,2,1,0:T(8,128)(2,1)} %param.15) | copy-start | bytes 3538948
  199.0 0.6 copy-start.16
  199.1 6.1 %copy-start.20 = (f32[2,1152]{1,0:T(2,128)}, f32[2,1152]{1,0:T(2,128)S(1)}, u32[]{:S(2)}) copy-start(f32[2,1152]{1,0:T(2,128)S(1)} %get-tuple-element.95) | copy-start | bytes 27652
  199.6 7.3 %copy-start.31 = (bf16[8,144,6144]{2,1,0:T(8,128)(2,1)S(1)}, bf16[8,144,6144]{2,1,0:T(8,128)(2,1)}, u32[]{:S(2)}) copy-start(bf16[8,144,6144]{2,1,0:T(8,128)(2,1)} %get-tuple-element.41) | copy-start | bytes 42467332
  205.1 0.6 copy-start.27
  205.2 0.6 copy-start.22
  205.5 12.4 %copy-start.11 = (bf16[2,256,1152]{2,1,0:T(8,128)(2,1)}, bf16[2,256,1152]{2,1,0:T(8,128)(2,1)S(1)}, u32[]{:S(2)}) copy-start(bf16[2,256,1152]{2,1,0:T(8,128)(2,1)S(1)} %add_convert_fusion) | copy-start | bytes 3538948
  206.9 11.0 %copy-start.2 = (bf16[2,8,32,1152]{3,2,1,0:T(8,128)(2,1)S(1)}, bf16[2,8,32,1152]{3,2,1,0:T(8,128)(2,1)}, u32[]{:S(2)}) copy-start(bf16[2,8,32,1152]{3,2,1,0:T(8,128)(2,1)} %param.16) | copy-start | bytes 3538948
  207.0 11.0 %copy-start.28 = (f32[2]{0:T(128)S(1)}, f32[2]{0:T(128)}, u32[]{:S(2)}) copy-start(f32[2]{0:T(128)} %compare_convert_fusion) | copy-start | bytes 28
  230.8 3.5 copy-start.4
  230.8 4.6 copy-start.6
  253.1 11.7 %copy-start.21 = (f32[2,1152]{1,0:T(2,128)S(1)}, f32[2,1152]{1,0:T(2,128)}, u32[]{:S(2)}) copy-start(f32[2,1152]{1,0:T(2,128)} %copy-done.20) | copy-start | bytes 27652
  264.7 6.0 %copy-start = (f32[2,256,1152]{2,1,0:T(8,128)}, f32[2,256,1152]{2,1,0:T(8,128)S(1)}, u32[]{:S(2)}) copy-start(f32[2,256,1152]{2,1,0:T(8,128)S(1)} %get-tuple-element.77.mid_ref) | copy-start | bytes 7077892
  264.9 5.8 copy-start.9
  264.9 5.8 copy-start.18
  264.9 6.6 %copy-start.5 = (bf16[512,3072]{1,0:T(8,128)(2,1)S(1)}, bf16[512,3072]{1,0:T(8,128)(2,1)}, u32[]{:S(2)}) copy-start(bf16[512,3072]{1,0:T(8,128)(2,1)} %copy-done.4) | copy-start | bytes 9437188
  415.8 21.8 %copy-start.29 = (f32[2]{0:T(128)S(1)}, f32[2]{0:T(128)}, u32[]{:S(2)}) copy-start(f32[2]{0:T(128)} %compare_convert_fusion) | copy-start | bytes 28
  415.8 21.9 %copy-start.3 = (bf16[2,8,32,1152]{3,2,1,0:T(8,128)(2,1)S(1)}, bf16[2,8,32,1152]{3,2,1,0:T(8,128)(2,1)}, u32[]{:S(2)}) copy-start(bf16[2,8,32,1152]{3,2,1,0:T(8,128)(2,1)} %param.16) | copy-start | bytes 3538948
  438.1 9.1 %copy-start.10 = (bf16[2,256,1152]{2,1,0:T(8,128)(2,1)S(1)}, bf16[2,256,1152]{2,1,0:T(8,128)(2,1)}, u32[]{:S(2)}) copy-start(bf16[2,256,1152]{2,1,0:T(8,128)(2,1)} %copy-done.9) | copy-start | bytes 3538948
  438.1 9.1 %copy-start.34 = (bf16[2,256,1152]{2,1,0:T(8,128)(2,1)S(1)}, bf16[2,256,1152]{2,1,0:T(8,128)(2,1)}, u32[]{:S(2)}) copy-start(bf16[2,256,1152]{2,1,0:T(8,128)(2,1)} %get-tuple-element.39) | copy-start | bytes 3538948
  447.2 2.0 copy-start.32
  447.2 2.3 copy-start.33
  454.2 4.9 copy-start.30
  454.2 5.2 copy-start.19
  454.2 5.2 copy-start.26
  454.3 5.2 copy-start.24
  454.3 5.2 copy-start.23
  454.3 5.2 copy-start.25
  576.0 5.2 copy-start.8
  580.5 4.4 copy-start.7
  584.9 2.2 copy-start.15

commit v7 on v6

--- a/solution.py
+++ b/solution.py
@@ -941,13 +941,116 @@
         ),
         name="attention_backward",
     )(q, d_att, inv_rows, kv_all, *grads)
-def modulate(values, shift_in, scale_in):
-    root = lax.rsqrt(jnp.mean(values * values, axis=-1, keepdims=True) + EPS)
-    return values * root * (1.0 + scale_in[:, None, :]) + shift_in[:, None, :]
-
-
-def swiglu(gate_in, up_in):
-    return jax.nn.silu(gate_in) * up_in
+def mlp_kernel(
+    x_ref, gout_ref, att_ref, mod_ref, live_ref, proj_ref, gate_ref, up_ref, down_ref,
+    out_ref, dmid_ref, dproj_ref, datt_ref, sums_ref, dgu_ref, ddown_ref,
+    mid, proj, mlp, dnorm, normed, normed_t, dmlp,
+):
+    step, steps = pl.program_id(0), pl.num_programs(0)
+    images, length, width = x_ref.shape
+    chunk = gate_ref.shape[1]
+
+    def piece(i, k):
+        return mod_ref[i : i + 1, k * width : (k + 1) * width]
+
+    def rows(i):
+        return pl.ds(i * length, length)
+
+    def live(i):
+        return live_ref[i : i + 1, 0:1]
+
+    def unit(i):
+        value = mid[rows(i), :]
+        root = lax.rsqrt(jnp.mean(value * value, axis=-1, keepdims=True) + EPS)
+        return value * root, root
+
+    @pl.when(step == 0)
+    def _():
+        for i in range(images):
+            proj[rows(i), :] = jnp.dot(att_ref[i], proj_ref[...], preferred_element_type=jnp.float32)
+            mid[rows(i), :] = x_ref[i].astype(jnp.float32) + piece(i, 2) * proj[rows(i), :]
+            value = (unit(i)[0] * (1.0 + piece(i, 4)) + piece(i, 3)).astype(jnp.bfloat16)
+            normed[rows(i), :] = value
+            normed_t[:, rows(i)] = value.T
+            dmlp[rows(i), :] = (piece(i, 5) * (gout_ref[i].astype(jnp.float32) * live(i))).astype(jnp.bfloat16)
+        mlp[...] = jnp.zeros_like(mlp)
+        dnorm[...] = jnp.zeros_like(dnorm)
+
+    gate = jnp.dot(normed[...], gate_ref[...], preferred_element_type=jnp.float32)
+    up = jnp.dot(normed[...], up_ref[...], preferred_element_type=jnp.float32)
+    dhidden = dot_t(dmlp[...], down_ref[...])
+    sigmoid = 1.0 / (1.0 + jnp.exp(-gate))
+    silu = gate * sigmoid
+    hidden = (silu * up).astype(jnp.bfloat16)
+    dgate = (dhidden * up * (sigmoid * (1.0 + gate * (1.0 - sigmoid)))).astype(jnp.bfloat16)
+    dup = (dhidden * silu).astype(jnp.bfloat16)
+    mlp[...] += jnp.dot(hidden, down_ref[...], preferred_element_type=jnp.float32)
+    dnorm[...] += dot_t(dgate, gate_ref[...]) + dot_t(dup, up_ref[...])
+    ddown_ref[...] = first_dot(hidden, dmlp[...]).astype(jnp.bfloat16)
+    dgu_ref[:, :chunk] = jnp.dot(normed_t[...], dgate, preferred_element_type=jnp.float32).astype(jnp.bfloat16)
+    dgu_ref[:, chunk:] = jnp.dot(normed_t[...], dup, preferred_element_type=jnp.float32).astype(jnp.bfloat16)
+
+    @pl.when(step == steps - 1)
+    def _():
+        total = lambda v: jnp.sum(v, axis=0, keepdims=True)
+        for i in range(images):
+            gy = gout_ref[i].astype(jnp.float32) * live(i)
+            value = mlp[rows(i), :]
+            out_ref[i] = ((mid[rows(i), :] + piece(i, 5) * value) * live(i)).astype(jnp.bfloat16)
+            sums_ref[i, 3:4, :] = total(gy * value)
+            n, root = unit(i)
+            dn = dnorm[rows(i), :]
+            sums_ref[i, 1:2, :] = total(dn)
+            sums_ref[i, 2:3, :] = total(dn * n)
+            e = dn * (1.0 + piece(i, 4))
+            d_mid = gy + root * (e - n * jnp.mean(e * n, axis=-1, keepdims=True))
+            dmid_ref[i] = d_mid
+            sums_ref[i, 0:1, :] = total(d_mid * proj[rows(i), :])
+            d_proj = (piece(i, 2) * d_mid).astype(jnp.bfloat16)
+            dproj_ref[i] = d_proj
+            datt_ref[i] = dot_t(d_proj, proj_ref[...]).astype(jnp.bfloat16)
+
+
+def mlp_chunk(ff):
+    return 512 if ff % 512 == 0 else 128
+
+
+def mlp_block(x, grad_out, attended, mod, live, qp_all, gu_all, down_all):
+    images, length, width = x.shape
+    ff = down_all.shape[0]
+    chunk = mlp_chunk(ff)
+    steps = ff // chunk
+    bf = jnp.bfloat16
+    whole = lambda s: pl.BlockSpec(s, lambda k: (0,) * len(s))
+    rows = lambda d: jax.ShapeDtypeStruct(x.shape, d)
+    tokens = images * length
+    return pl.pallas_call(
+        mlp_kernel,
+        grid=(steps,),
+        in_specs=[whole(x.shape)] * 3
+        + [whole(mod.shape), whole(live.shape), pl.BlockSpec((width, width), lambda k: (0, 3))]
+        + [
+            pl.BlockSpec((width, chunk), lambda k: (0, k)),
+            pl.BlockSpec((width, chunk), lambda k: (0, steps + k)),
+            pl.BlockSpec((chunk, width), lambda k: (k, 0)),
+        ],
+        out_shape=[rows(bf), rows(jnp.float32), rows(bf), rows(bf)]
+        + [
+            jax.ShapeDtypeStruct((images, 4, width), jnp.float32),
+            jax.ShapeDtypeStruct((width, 2 * ff), bf),
+            jax.ShapeDtypeStruct((ff, width), bf),
+        ],
+        out_specs=[whole(x.shape)] * 4
+        + [
+            whole((images, 4, width)),
+            pl.BlockSpec((width, 2 * chunk), lambda k: (0, k)),
+            pl.BlockSpec((chunk, width), lambda k: (k, 0)),
+        ],
+        scratch_shapes=[pltpu.VMEM((tokens, width), jnp.float32)] * 4
+        + [pltpu.VMEM((tokens, width), bf), pltpu.VMEM((width, tokens), bf), pltpu.VMEM((tokens, width), bf)],
+        compiler_params=pltpu.CompilerParams(vmem_limit_bytes=60 * 2**20),
+        name="mlp_block",
+    )(x, grad_out, attended, mod, live, qp_all, gu_all, gu_all, down_all)
 
 
 def half_cuts(ref, axis, base, size, own_parts, shared_parts):
@@ -1025,39 +1128,17 @@
     tables, kv_all, rest = outs[9:12], outs[12], outs[13:]
     if fits:
         qp_all, gu_all, down_all = (full(w) for w in rest)
+    live = jnp.broadcast_to(live_mask[:, None], (images, LANES))
+    flat = lambda a: a.reshape(images * length, a.shape[-1])
+    patches_out, d_middle, d_proj, d_attended, mid_sums, d_w_gu, d_w_down = mlp_block(
+        x, grad_out.reshape(images, length, width), attended, mod, live, qp_all, gu_all, down_all
+    )
+    patches_out = patches_out.reshape(images, rows, cols, width)
     mod = mod.reshape(images, 6, width)
-    gate_one, shift_two, scale_two, gate_two = (mod[:, k] for k in (2, 3, 4, 5))
-    proj_all = qp_all[:, 3 * width :]
-    flat = lambda a: a.reshape(images * length, a.shape[-1])
-    attended_low = flat(attended)
-    proj = jnp.dot(attended_low, proj_all, preferred_element_type=jnp.float32).reshape(images, length, width)
-    middle = x.astype(jnp.float32) + gate_one[:, None, :] * proj
-    normed_two, norm_two_pull = jax.vjp(modulate, middle, shift_two, scale_two)
-    normed_two_low = flat(normed_two.astype(bf))
-    pre = jnp.dot(normed_two_low, gu_all, preferred_element_type=jnp.float32)
-    hidden, swiglu_pull = jax.vjp(swiglu, pre[:, :ff], pre[:, ff:])
-    hidden_low = hidden.astype(bf)
-    mlp = jnp.dot(hidden_low, down_all, preferred_element_type=jnp.float32).reshape(images, length, width)
-    output = (middle + gate_two[:, None, :] * mlp) * live_mask[:, None, None]
-    patches_out = output.astype(bf).reshape(images, rows, cols, width)
-
-    grad_y = grad_out.reshape(images, length, width).astype(jnp.float32) * live_mask[:, None, None]
-    d_gate_two = jnp.sum(grad_y * mlp, axis=1)
-    d_mlp = flat((grad_y * gate_two[:, None, :]).astype(bf))
-    d_w_down = jnp.einsum("tf,td->fd", hidden_low, d_mlp, preferred_element_type=jnp.float32).astype(bf)
-    d_hidden = jnp.einsum("td,fd->tf", d_mlp, down_all, preferred_element_type=jnp.float32)
-    d_pre = jnp.concatenate([d.astype(bf) for d in swiglu_pull(d_hidden)], axis=1)
-    d_w_gu = jnp.einsum("td,tf->df", normed_two_low, d_pre, preferred_element_type=jnp.float32).astype(bf)
-    d_normed_two = jnp.einsum("tf,df->td", d_pre, gu_all, preferred_element_type=jnp.float32)
-    d_middle_norm, d_shift_two, d_scale_two = norm_two_pull(d_normed_two.reshape(images, length, width))
-    d_middle = grad_y + d_middle_norm
-    d_gate_one = jnp.sum(d_middle * proj, axis=1)
-    d_proj = flat((d_middle * gate_one[:, None, :]).astype(bf))
-    d_w_proj = jnp.einsum("td,te->de", attended_low, d_proj, preferred_element_type=jnp.float32).astype(bf)
-    d_attended = jnp.einsum("te,de->td", d_proj, proj_all, preferred_element_type=jnp.float32).astype(bf)
+    d_w_proj = jnp.einsum("td,te->de", flat(attended), flat(d_proj), preferred_element_type=jnp.float32).astype(bf)
     d_query, d_kv, *rest = attention_backward(
         query,
-        d_attended.reshape(images, length, width),
+        d_attended,
         jnp.swapaxes(inv, 1, 2),
         kv_all,
         [by_shard(d_w_gu)] if fits else [],
@@ -1071,7 +1152,7 @@
     d_w_qkv = jnp.einsum("td,te->de", flat(normed_one), flat(d_qkv), preferred_element_type=jnp.float32).astype(bf)
     d_w_qp = jnp.concatenate([d_w_qkv, d_w_proj], axis=1)
 
-    d_mod_part = jnp.stack([sums[:, 0], sums[:, 1], d_gate_one, d_shift_two, d_scale_two, d_gate_two], axis=1)
+    d_mod_part = jnp.concatenate([sums[:, 0:2], mid_sums], axis=1)
     gain_part = jnp.sum(sums[:, 2:4].reshape(images, 2, HEADS, HDIM), axis=(0, 2))
     if fits:
         tags = jnp.pad(jnp.repeat(onehot * (1.0 / lax.axis_size("band")), 6, axis=0), ((0, 0), (0, LANES - GROUPS)))
@@ -1112,6 +1193,8 @@
         jnp.sum(d_mod_all.astype(jnp.float32), axis=0), grp * bias_cols, bias_cols, axis=0
     )
     wide = lambda a: a.astype(jnp.float32)
+    chunk = mlp_chunk(ff)
+    d_gu = d_gu.reshape(d_gu.shape[0], ff // chunk, 2, chunk)
     return (
         patches_out,
         d_patches,
@@ -1122,8 +1205,8 @@
         gain_all[0],
         gain_all[1],
         wide(d_qp[:, 3 * width :]),
-        wide(d_gu[:, :ff]),
-        wide(d_gu[:, ff:]),
+        wide(d_gu[:, :, 0].reshape(-1, ff)),
+        wide(d_gu[:, :, 1].reshape(-1, ff)),
         wide(d_down),
     )
 

time: 599 us -> 582 us (0.972)
  matrix products: 97.7 us -> 15.2 us
  Pallas kernels: 446 us -> 506 us
    dot_general x9 -> x1, matrix products: 86.5 us -> 1.73 us  [body(): jnp.einsum('td,te->de', flat(attended), flat(d_proj), preferred_element_t...]
    pallas_call x0 -> x1, Pallas kernels: none -> 51.5 us  [mlp_block(): pl.pallas_call(mlp_kernel, grid=(steps,), in_specs=[whole(x.shape)] * 3 +...]
    pallas_call x1, Pallas kernels: 129 us -> 138 us  [attention_backward(): pl.pallas_call(functools.partial(attention_back_kernel, n, cuts, lags), o...]
    convert_element_type x4, other arithmetic: 5.81 us -> 14.3 us  [body(): wide = lambda a: a.astype(jnp.float32)]
where the time goes in v7:
time: 582 us; the launch traced here: 572 us
  Pallas kernels  506 us (87%)
  other arithmetic  26.7 us (5%)
  local copies, waits for them, and re-layouts  21.3 us (4%)
  matrix products  15.2 us (3%)
    pallas_call x1, Pallas kernels, forward(): pl.pallas_call(kernel, out_shape=outs + [jax.ShapeDtypeStruct(keys, bf)]...  185 us
    pallas_call x1, Pallas kernels, attention_backward(): pl.pallas_call(functools.partial(attention_back_kernel, n, cuts, lags), o...  138 us
    pallas_call x1, Pallas kernels, scatter(): pl.pallas_call(functools.partial(scatter_kernel, n, cuts, lags), out_shap...  110 us
    pallas_call x1, Pallas kernels, mlp_block(): pl.pallas_call(mlp_kernel, grid=(steps,), in_specs=[whole(x.shape)] * 3 +...  51.5 us
    pallas_call x1, Pallas kernels, qkv_backward(): pl.pallas_call(qkv_back_kernel, grid=(images,), in_specs=[row(width), pl....  21.6 us
    convert_element_type x4, other arithmetic, body(): wide = lambda a: a.astype(jnp.float32)  14.3 us

profile of v7, /device:TPU:0, one launch (start us, length us, event | category | flops | bytes accessed | tf_op | source)
XLA Modules:
  0.0 572.1 jit_solution(9204272281241440701)
XLA Ops:
  0.7 0.9 convert_dynamic-update-slice_fusion
  1.6 2.7 convolution_add_fusion.refs_1_
  4.3 0.1 stack_tile.6
  4.4 0.0 copy-done.14
  4.5 0.1 stack_tile.7
  4.5 0.6 pad_maximum_fusion.4.refs_3_.gains_ref
  5.2 1.3 pad_maximum_fusion.1.refs_6_
  6.5 1.2 pad_maximum_fusion.2.refs_5_
  7.7 0.0 copy-done.15
  7.7 0.6 pad_convert_fusion.refs_2_
  8.9 0.5 broadcast_in_dim.11.refs_4_
  9.4 185.4 %forward.1 = (bf16[2,256,1152]{2,1,0:T(8,128)(2,1)}, bf16[2,256,1152]{2,1,0:T(8,128)(2,1)}, f32[2,256,1152]{2,1,0:T(8,128)}, f32[2,256,1152]{2,1,0:T(8,128)}, f3...) custom-call(bf16[2,256,1152]{2,1,0:T(8,128)(2,1)} %bitcast.48, ...), custom_call_target="tpu_custom_call" | custom-call | tf_op jit(solution)/shard_map/forward/pallas_call | solution.py:794
  195.5 0.6 broadcast_in_dim.12.live_ref
  196.1 51.5 %mlp_block.1 = (bf16[2,256,1152]{2,1,0:T(8,128)(2,1)}, f32[2,256,1152]{2,1,0:T(8,128)}, bf16[2,256,1152]{2,1,0:T(8,128)(2,1)}, bf16[2,256,1152]{2,1,0:T(8,128)(2...) custom-call(bf16[2,256,1152]{2,1,0:T(8,128)(2,1)} %bitcast.49, ...), custom_call_target="tpu_custom_call" | custom-call | tf_op jit(solution)/shard_map/mlp_block/pallas_call | solution.py:1027
  247.6 0.8 copy.38
  248.5 138.3 %attention_backward.1 = (f32[2,256,1152]{2,1,0:T(8,128)}, bf16[2,2,256,1152]{3,2,1,0:T(8,128)(2,1)}, bf16[144,6144]{1,0:T(8,128)(2,1)}) custom-call(bf16[2,256,1152]{2,1,0:T(8,128)(2,1)} %get-tuple-element.52.q_ref, bf16[2,256,1152]{2,1,0:T(8,128)(2,1)} %get-tuple-element.53.do_ref, f32[2,128,256]{2,1,0:T(8,128)} %bitcast.58, ...), custom_call_target="tpu_custom_call" | custom-call | tf_op jit(solution)/shard_map/attention_backward/pallas_call | solution.py:917
  386.7 3.2 slice_bitcast_fusion
  390.0 0.7 reshape.115.mod_ref
  390.7 21.6 %qkv_backward.1 = (bf16[2,256,3456]{2,1,0:T(8,128)(2,1)}, f32[2,256,1152]{2,1,0:T(8,128)}, f32[2,4,1152]{2,1,0:T(4,128)}) custom-call(bf16[2,256,1152]{2,1,0:T(8,128)(2,1)} %bitcast.50, f32[2,6,1152]{2,1,0:T(8,128)} %reshape.115.mod_ref, f32[2,256,1152]{2,1,0:T(8,128)} %get-tuple-element.51.mid_ref, f32[2,256,1152]{2,1,0:T(8,128)} %get-tuple-element.57.dq_ref, ...), custom_call_target="tpu_custom_call" | custom-call | tf_op jit(solution)/shard_map/qkv_backward/pallas_call | solution.py:435
  412.2 0.9 slice_reduce_fusion
  413.2 0.1 broadcast_in_dim.13
  413.2 0.1 reshape.121
  413.3 0.1 copy.42
  413.4 0.1 reduce_sum.35
  413.5 0.1 reshape.122
  413.6 2.1 concatenate.23.refs_2_
  415.7 7.1 %fusion = bf16[1152,3456]{1,0:T(8,128)(2,1)S(1)} fusion(bf16[2,256,1152]{2,1,0:T(8,128)(2,1)S(1)} %copy-done.16, bf16[2,256,3456]{2,1,0:T(8,128)(2,1)} %get-tuple-element.69), kind=kOutput, calls=%fused_computation.1 | convolution fusion | flops 4080844800 | bytes 12681216 | tf_op jit(solution)/shard_map/td,te->de/dot_general | solution.py:1152
  422.8 1.7 fusion.1
  424.6 4.6 pad_maximum_fusion
  429.2 1.4 add_multiply_fusion.refs_4_
  430.6 109.5 %gradient_scatter.1 = (bf16[384,1152]{1,0:T(8,128)(2,1)}, bf16[144,4608]{1,0:T(8,128)(2,1)}, bf16[8,16,1280]{2,1,0:T(8,128)(2,1)}, f32[8,8,256]{2,1,0:T(8,128)}) custom-call(bf16[8,384,1152]{2,1,0:T(8,128)(2,1)} %bitcast.54, bf16[8,144,4608]{2,1,0:T(8,128)(2,1)} %bitcast.44, f32[16,1280]{1,0:T(8,128)} %concatenate.23.refs_2_, bf16[144,6912]{1,0:T(8,128)(2,1)} %refs_3_.1, ...), custom_call_target="tpu_custom_call" | custom-call | tf_op jit(solution)/shard_map/gradient_scatter/pallas_call | solution.py:557
  540.1 1.0 slice.50
  541.1 0.3 reshape.125
  541.4 0.8 slice.49
  542.2 3.7 fusion.4
  545.8 1.4 slice_convert_fusion.2
  547.3 0.0 copy-done.7
  547.3 1.3 convert_element_type.75
  548.6 0.9 slice_convert_fusion.3
  549.5 0.1 convert_reduce_fusion
  549.6 0.7 dynamic_slice.7
  550.3 0.7 reshape.123
  551.0 0.8 convert_reduce_fusion.1
  551.8 0.6 fusion.6
  552.4 1.5 reshape.126
  553.9 10.7 %fusion.2 = (f32[144,6,512]{2,1,0:T(8,128)}, f32[144,6,512]{2,1,0:T(8,128)}) fusion(bf16[144,6,2,512]{3,2,1,0:T(2,128)(2,1)S(1)} %reshape.126), kind=kLoop, calls=%fused_computation.7 | loop fusion | flops 884736 | bytes 5308416 | tf_op jit(solution)/shard_map/convert_element_type | solution.py:1195
  564.6 4.5 copy.48
  569.1 2.6 copy.49
  (47 shorter events, 0.2 us)
Async XLA Ops:
  0.6 3.7 copy-start.13
  0.7 3.8 copy-start.14
  0.7 4.5 copy-start.6
  0.7 4.5 copy-start.5
  4.3 2.2 copy-start.4
  4.3 2.2 copy-start.8
  6.5 1.2 copy-start.15
  196.1 51.5 %copy-start.9 = (f32[2,256,128]{2,1,0:T(8,128)S(1)}, f32[2,256,128]{2,1,0:T(8,128)}, u32[]{:S(2)}) copy-start(f32[2,256,128]{2,1,0:T(8,128)} %get-tuple-element.54) | copy-start | bytes 786436
  386.7 3.2 copy-start.10
  390.7 22.4 %copy-start.12 = (f32[2,4,1152]{2,1,0:T(4,128)S(1)}, f32[2,4,1152]{2,1,0:T(4,128)}, u32[]{:S(2)}) copy-start(f32[2,4,1152]{2,1,0:T(4,128)} %get-tuple-element.72) | copy-start | bytes 110596
  390.7 25.1 %copy-start.16 = (bf16[2,256,1152]{2,1,0:T(8,128)(2,1)S(1)}, bf16[2,256,1152]{2,1,0:T(8,128)(2,1)}, u32[]{:S(2)}) copy-start(bf16[2,256,1152]{2,1,0:T(8,128)(2,1)} %get-tuple-element.68) | copy-start | bytes 3538948
  415.7 7.1 %copy-start.3 = (bf16[2,256,1152]{2,1,0:T(8,128)(2,1)S(1)}, bf16[2,256,1152]{2,1,0:T(8,128)(2,1)}, u32[]{:S(2)}) copy-start(bf16[2,256,1152]{2,1,0:T(8,128)(2,1)} %get-tuple-element.45.att_ref) | copy-start | bytes 3538948
  415.7 7.1 %copy-start.17 = (bf16[2,256,1152]{2,1,0:T(8,128)(2,1)S(1)}, bf16[2,256,1152]{2,1,0:T(8,128)(2,1)}, u32[]{:S(2)}) copy-start(bf16[2,256,1152]{2,1,0:T(8,128)(2,1)} %get-tuple-element.70) | copy-start | bytes 3538948
  542.2 3.7 copy-start.2
  545.8 1.5 copy-start.7
  547.3 3.0 copy-start.11
  547.3 5.1 copy-start.1
  564.6 4.5 copy-start

commit v8 on v7

--- a/solution.py
+++ b/solution.py
@@ -189,8 +189,8 @@
     s = pltpu.SemaphoreType.DMA
 
     def buf(lead, k, size):
-        grad = grads[cuts[k][5]]
-        shape = (grad.shape[1], size) if cuts[k][0] == 1 else (size, grad.shape[2])
+        rows, cols = grads[cuts[k][5]].shape[-2:]
+        shape = (rows, size) if cuts[k][0] == 1 else (size, cols)
         return pltpu.VMEM(lead + shape, jnp.bfloat16)
 
     out = []
@@ -214,6 +214,18 @@
     x, y, z, c, far = at.x, at.y, at.z, at.c, at.far
     ins, outs = ([refs[cut[5]] for cut in cuts] for refs in (ins, outs))
 
+    def in_half(i, s, cc):
+        axis, half, _, _, base, _ = cuts[i]
+        if base is None:
+            return ins[i].at[cc, s]
+        return span(ins[i].at[s], axis, base + cc * half, half)
+
+    def out_half(i, cc):
+        axis, half, _, _, base, _ = cuts[i]
+        if base is None:
+            return outs[i].at[cc]
+        return span(outs[i], axis, base + cc * half, half)
+
     def piece(i, ref):
         _, _, a, b = cuts[i][:4]
         return span(ref, cuts[i][0], y * b, a + b)
@@ -228,14 +240,12 @@
         return far[t] * 2 + (1 - x if j else x)
 
     def load(i, t, j):
-        axis, half, _, _, base, _ = cuts[i]
         s, q = shard(t, j), order.index((t, j))
-        return pltpu.make_async_copy(span(ins[i].at[s], axis, base + c * half, half), own_half[i].at[s], ls.at[i, q])
+        return pltpu.make_async_copy(in_half(i, s, c), own_half[i].at[s], ls.at[i, q])
 
     def give(i, t, j):
-        axis, half, _, _, base, _ = cuts[i]
         s, q = shard(t, j), order.index((t, j))
-        src = span(ins[i].at[s], axis, base + (1 - c) * half, half)
+        src = in_half(i, s, 1 - c)
         at.send(src, core_buf[i].at[s], cs.at[i, q], cr.at[i, s], at.cpeer)
         if not at.draining:
             load(i, t, j).start()
@@ -311,7 +321,7 @@
                     add_into(span(own, axis, b, a), span(fin_buf[i], axis, b if yy == 0 else 0, a))
                     move_into(span(own, axis, yy * (a + b), b), span(fin_buf[i], axis, 0 if yy == 0 else a, b))
 
-        o = span(outs[i], axis, base + c * half, half)
+        o = out_half(i, c)
         at.send(own, o, es.at[i], er.at[i], at.cpeer)
         at.keep(own, o, ws.at[i])
 
@@ -331,8 +341,7 @@
 
     def last():
         for i in range(n):
-            axis, half, _, _, base, _ = cuts[i]
-            at.arrived(span(outs[i], axis, base + (1 - c) * half, half), er.at[i])
+            at.arrived(out_half(i, 1 - c), er.at[i])
 
     return opening, [f for _, _, f in todo], last
 
@@ -541,7 +550,7 @@
     small = small[1:]
     for k, step in enumerate(steps):
         step()
-        if k % 3 == 2 and small:
+        if k % 6 == 5 and small:
             small[0]()
             small = small[1:]
     for step in small:
@@ -896,7 +905,7 @@
             head(i, h)
             return 0
 
-        lax.fori_loop(0, HEADS, body, 0)
+        lax.fori_loop(0, HEADS, body, 0, unroll=2)
         to_core(i)
         steps += [functools.partial(to_core, i)] + exchange
     exchange[0]()
@@ -920,7 +929,7 @@
             jax.ShapeDtypeStruct(q.shape, jnp.float32),
             jax.ShapeDtypeStruct((2, images, length, width), bf),
         ]
-        + [jax.ShapeDtypeStruct(w.shape[1:], bf) for w in grads],
+        + [jax.ShapeDtypeStruct(w.shape[:-3] + w.shape[-2:], bf) for w in grads],
         in_specs=[vmem, vmem, vmem, any_ref] + [any_ref] * n,
         out_specs=[vmem, any_ref] + [any_ref] * n,
         scratch_shapes=[
@@ -948,7 +957,6 @@
 ):
     step, steps = pl.program_id(0), pl.num_programs(0)
     images, length, width = x_ref.shape
-    chunk = gate_ref.shape[1]
 
     def piece(i, k):
         return mod_ref[i : i + 1, k * width : (k + 1) * width]
@@ -987,8 +995,8 @@
     mlp[...] += jnp.dot(hidden, down_ref[...], preferred_element_type=jnp.float32)
     dnorm[...] += dot_t(dgate, gate_ref[...]) + dot_t(dup, up_ref[...])
     ddown_ref[...] = first_dot(hidden, dmlp[...]).astype(jnp.bfloat16)
-    dgu_ref[:, :chunk] = jnp.dot(normed_t[...], dgate, preferred_element_type=jnp.float32).astype(jnp.bfloat16)
-    dgu_ref[:, chunk:] = jnp.dot(normed_t[...], dup, preferred_element_type=jnp.float32).astype(jnp.bfloat16)
+    dgu_ref[0] = jnp.dot(normed_t[...], dgate, preferred_element_type=jnp.float32).astype(jnp.bfloat16)
+    dgu_ref[1] = jnp.dot(normed_t[...], dup, preferred_element_type=jnp.float32).astype(jnp.bfloat16)
 
     @pl.when(step == steps - 1)
     def _():
@@ -1011,14 +1019,10 @@
             datt_ref[i] = dot_t(d_proj, proj_ref[...]).astype(jnp.bfloat16)
 
 
-def mlp_chunk(ff):
-    return 512 if ff % 512 == 0 else 128
-
-
 def mlp_block(x, grad_out, attended, mod, live, qp_all, gu_all, down_all):
     images, length, width = x.shape
     ff = down_all.shape[0]
-    chunk = mlp_chunk(ff)
+    chunk = 512 if ff % 512 == 0 else LANES
     steps = ff // chunk
     bf = jnp.bfloat16
     whole = lambda s: pl.BlockSpec(s, lambda k: (0,) * len(s))
@@ -1037,13 +1041,13 @@
         out_shape=[rows(bf), rows(jnp.float32), rows(bf), rows(bf)]
         + [
             jax.ShapeDtypeStruct((images, 4, width), jnp.float32),
-            jax.ShapeDtypeStruct((width, 2 * ff), bf),
+            jax.ShapeDtypeStruct((2, width, ff), bf),
             jax.ShapeDtypeStruct((ff, width), bf),
         ],
         out_specs=[whole(x.shape)] * 4
         + [
             whole((images, 4, width)),
-            pl.BlockSpec((width, 2 * chunk), lambda k: (0, k)),
+            pl.BlockSpec((2, width, chunk), lambda k: (0, 0, k)),
             pl.BlockSpec((chunk, width), lambda k: (k, 0)),
         ],
         scratch_shapes=[pltpu.VMEM((tokens, width), jnp.float32)] * 4
@@ -1141,8 +1145,8 @@
         d_attended,
         jnp.swapaxes(inv, 1, 2),
         kv_all,
-        [by_shard(d_w_gu)] if fits else [],
-        [half_cuts(0, 1, 0, 2 * ff, 4, 1)] if fits else [],
+        [d_w_gu.reshape(2, -1, w_gate.shape[0], ff)] if fits else [],
+        [half_cuts(0, 1, None, 2 * ff, 4, 1)] if fits else [],
         (2, 2, 1, 2),
     )
     d_qkv, d_x, sums = qkv_backward(
@@ -1162,7 +1166,7 @@
         cuts = [half_cuts(0, 0, 0, w_down.shape[0], 2, 1), half_cuts(1, 1, 0, 4 * width, 8, 5)]
         d_gu = rest[0]
         d_down, d_qp, gathered, cond_blocks = scatter(
-            [by_shard(d_w_down), by_shard(d_w_qp)], cuts, (2, 2, 1, 2), small, w_ada, silu_slope
+            [by_shard(d_w_down), by_shard(d_w_qp)], cuts, (2, 1, 0, 2), small, w_ada, silu_slope
         )
         d_mod_all = gathered[:, :GAIN_ROW, :width].reshape(-1, ada_cols)
         onehot_all = gathered[:, 0:GAIN_ROW:6, width : width + GROUPS].reshape(-1, GROUPS)
@@ -1171,7 +1175,7 @@
         d_cond = jnp.swapaxes(cond_blocks[:, :, :ada_rows], 0, 1).reshape(GROUPS, -1)
     else:
         d_gu, d_down, d_qp = (
-            lax.psum(lax.psum_scatter(w, "grp", scatter_dimension=0, tiled=True), "band")
+            lax.psum(lax.psum_scatter(w, "grp", scatter_dimension=w.ndim - 2, tiled=True), "band")
             for w in (d_w_gu, d_w_down, d_w_qp)
         )
         d_modulation = lax.psum(d_mod_part.reshape(images, ada_cols), "band").astype(bf)
@@ -1193,8 +1197,6 @@
         jnp.sum(d_mod_all.astype(jnp.float32), axis=0), grp * bias_cols, bias_cols, axis=0
     )
     wide = lambda a: a.astype(jnp.float32)
-    chunk = mlp_chunk(ff)
-    d_gu = d_gu.reshape(d_gu.shape[0], ff // chunk, 2, chunk)
     return (
         patches_out,
         d_patches,
@@ -1205,8 +1207,8 @@
         gain_all[0],
         gain_all[1],
         wide(d_qp[:, 3 * width :]),
-        wide(d_gu[:, :, 0].reshape(-1, ff)),
-        wide(d_gu[:, :, 1].reshape(-1, ff)),
+        wide(d_gu[0]),
+        wide(d_gu[1]),
         wide(d_down),
     )
 

time: 582 us -> 547 us (0.940); the launches traced: 572 us -> 544 us
  Pallas kernels: 506 us -> 495 us
  local copies, waits for them, and re-layouts: 21.3 us -> 12.7 us
  other arithmetic: 26.7 us -> 18.3 us
    pallas_call x1, Pallas kernels: 110 us -> 101 us  [scatter(): pl.pallas_call(functools.partial(scatter_kernel, n, cuts, lags), out_shap...]
    convert_element_type x4, other arithmetic: 14.3 us -> 5.82 us  [body(): wide = lambda a: a.astype(jnp.float32)]
    unnamed x38 -> x34, local copies, waits for them, and re-layouts: 7.2 us -> 0.1 us
where the time goes in v8:
time: 547 us; the launch traced here: 544 us
  Pallas kernels  495 us (90%)
  other arithmetic  18.3 us (3%)
  matrix products  15.2 us (3%)
  local copies, waits for them, and re-layouts  12.7 us (2%)
    pallas_call x1, Pallas kernels, forward(): pl.pallas_call(kernel, out_shape=outs + [jax.ShapeDtypeStruct(keys, bf)]...  185 us
    pallas_call x1, Pallas kernels, attention_backward(): pl.pallas_call(functools.partial(attention_back_kernel, n, cuts, lags), o...  136 us
    pallas_call x1, Pallas kernels, scatter(): pl.pallas_call(functools.partial(scatter_kernel, n, cuts, lags), out_shap...  101 us
    pallas_call x1, Pallas kernels, mlp_block(): pl.pallas_call(mlp_kernel, grid=(steps,), in_specs=[whole(x.shape)] * 3 +...  51.5 us
    pallas_call x1, Pallas kernels, qkv_backward(): pl.pallas_call(qkv_back_kernel, grid=(images,), in_specs=[row(width), pl....  21.6 us

profile of v8, /device:TPU:0, one launch (start us, length us, event | category | flops | bytes accessed | tf_op | source)
XLA Modules:
  0.0 543.7 jit_solution(9126004776625679286)
XLA Ops:
  0.6 0.0 copy-start.12
  0.7 0.0 copy-start.13
  0.7 0.0 copy-start.5
  0.7 0.9 convert_dynamic-update-slice_fusion
  1.6 2.7 convolution_add_fusion.refs_1_
  4.3 0.1 stack_tile.6
  4.4 0.0 copy-done.13
  4.5 0.1 stack_tile.7
  4.5 0.6 pad_maximum_fusion.4.refs_3_.gains_ref
  5.2 0.0 copy-done.4
  5.2 1.3 pad_maximum_fusion.1.refs_6_
  6.5 1.2 pad_maximum_fusion.2.refs_5_
  7.7 0.6 pad_convert_fusion.refs_2_
  8.9 0.5 broadcast_in_dim.11.refs_4_
  9.4 185.5 %forward.1 = (bf16[2,256,1152]{2,1,0:T(8,128)(2,1)}, bf16[2,256,1152]{2,1,0:T(8,128)(2,1)}, f32[2,256,1152]{2,1,0:T(8,128)}, f32[2,256,1152]{2,1,0:T(8,128)}, f3...) custom-call(bf16[2,256,1152]{2,1,0:T(8,128)(2,1)} %bitcast.50, ...), custom_call_target="tpu_custom_call" | custom-call | tf_op jit(solution)/shard_map/forward/pallas_call | solution.py:803
  195.5 0.6 broadcast_in_dim.12.live_ref
  196.2 51.5 %mlp_block.1 = (bf16[2,256,1152]{2,1,0:T(8,128)(2,1)}, f32[2,256,1152]{2,1,0:T(8,128)}, bf16[2,256,1152]{2,1,0:T(8,128)(2,1)}, bf16[2,256,1152]{2,1,0:T(8,128)(2...) custom-call(bf16[2,256,1152]{2,1,0:T(8,128)(2,1)} %bitcast.51, ...), custom_call_target="tpu_custom_call" | custom-call | tf_op jit(solution)/shard_map/mlp_block/pallas_call | solution.py:1031
  247.7 0.8 copy.38
  248.5 136.1 %attention_backward.1 = (f32[2,256,1152]{2,1,0:T(8,128)}, bf16[2,2,256,1152]{3,2,1,0:T(8,128)(2,1)}, bf16[2,144,3072]{2,1,0:T(8,128)(2,1)}) custom-call(bf16[2,256,1152]{2,1,0:T(8,128)(2,1)} %get-tuple-element.52.q_ref, bf16[2,256,1152]{2,1,0:T(8,128)(2,1)} %get-tuple-element.53.do_ref, f32[2,128,256]{2,1,0:T(8,128)} %bitcast.56, ...), custom_call_target="tpu_custom_call" | custom-call | tf_op jit(solution)/shard_map/attention_backward/pallas_call | solution.py:926
  384.6 3.2 slice_bitcast_fusion
  387.9 0.7 reshape.112.mod_ref
  388.6 21.6 %qkv_backward.1 = (bf16[2,256,3456]{2,1,0:T(8,128)(2,1)}, f32[2,256,1152]{2,1,0:T(8,128)}, f32[2,4,1152]{2,1,0:T(4,128)}) custom-call(bf16[2,256,1152]{2,1,0:T(8,128)(2,1)} %bitcast.52, f32[2,6,1152]{2,1,0:T(8,128)} %reshape.112.mod_ref, f32[2,256,1152]{2,1,0:T(8,128)} %get-tuple-element.51.mid_ref, f32[2,256,1152]{2,1,0:T(8,128)} %get-tuple-element.57.dq_ref, ...), custom_call_target="tpu_custom_call" | custom-call | tf_op jit(solution)/shard_map/qkv_backward/pallas_call | solution.py:444
  410.1 0.9 slice_reduce_fusion
  411.1 0.1 broadcast_in_dim.13
  411.1 0.1 reshape.118
  411.2 0.1 copy.42
  411.3 0.1 reduce_sum.35
  411.4 0.1 reshape.119
  411.5 2.1 concatenate.23.refs_2_
  413.6 7.1 %fusion = bf16[1152,3456]{1,0:T(8,128)(2,1)S(1)} fusion(bf16[2,256,1152]{2,1,0:T(8,128)(2,1)S(1)} %copy-done.15, bf16[2,256,3456]{2,1,0:T(8,128)(2,1)} %get-tuple-element.69), kind=kOutput, calls=%fused_computation.1 | convolution fusion | flops 4080844800 | bytes 12681216 | tf_op jit(solution)/shard_map/td,te->de/dot_general | solution.py:1156
  420.7 1.7 fusion.1
  422.5 4.6 pad_maximum_fusion
  427.1 1.4 add_multiply_fusion.refs_4_
  428.5 100.6 %gradient_scatter.1 = (bf16[384,1152]{1,0:T(8,128)(2,1)}, bf16[144,4608]{1,0:T(8,128)(2,1)}, bf16[8,16,1280]{2,1,0:T(8,128)(2,1)}, f32[8,8,256]{2,1,0:T(8,128)}) custom-call(bf16[8,384,1152]{2,1,0:T(8,128)(2,1)} %bitcast.54, bf16[8,144,4608]{2,1,0:T(8,128)(2,1)} %bitcast.46, f32[16,1280]{1,0:T(8,128)} %concatenate.23.refs_2_, bf16[144,6912]{1,0:T(8,128)(2,1)} %refs_3_.1, ...), custom_call_target="tpu_custom_call" | custom-call | tf_op jit(solution)/shard_map/gradient_scatter/pallas_call | solution.py:566
  529.1 1.0 slice.50
  530.1 0.3 reshape.122
  530.3 0.8 slice.49
  531.1 3.7 fusion.2
  534.8 1.4 slice_convert_fusion
  536.2 0.0 copy-done.6
  536.3 1.3 convert_element_type.75
  537.6 0.9 slice_convert_fusion.1
  538.5 0.1 convert_reduce_fusion
  538.5 0.7 dynamic_slice.7
  539.3 0.7 reshape.120
  540.0 0.8 convert_reduce_fusion.1
  540.8 0.6 fusion.4
  541.3 2.2 bitcast_convert_fusion
  (42 shorter events, 0.2 us)
Async XLA Ops:
  0.6 3.7 copy-start.12
  0.7 3.8 copy-start.13
  0.7 4.5 copy-start.5
  0.7 4.5 copy-start.4
  4.3 2.2 copy-start.3
  4.3 2.2 copy-start.7
  6.5 1.2 copy-start.14
  196.2 51.5 %copy-start.8 = (f32[2,256,128]{2,1,0:T(8,128)S(1)}, f32[2,256,128]{2,1,0:T(8,128)}, u32[]{:S(2)}) copy-start(f32[2,256,128]{2,1,0:T(8,128)} %get-tuple-element.54) | copy-start | bytes 786436
  384.6 3.2 copy-start.9
  388.6 22.4 %copy-start.11 = (f32[2,4,1152]{2,1,0:T(4,128)S(1)}, f32[2,4,1152]{2,1,0:T(4,128)}, u32[]{:S(2)}) copy-start(f32[2,4,1152]{2,1,0:T(4,128)} %get-tuple-element.72) | copy-start | bytes 110596
  388.6 25.1 %copy-start.15 = (bf16[2,256,1152]{2,1,0:T(8,128)(2,1)S(1)}, bf16[2,256,1152]{2,1,0:T(8,128)(2,1)}, u32[]{:S(2)}) copy-start(bf16[2,256,1152]{2,1,0:T(8,128)(2,1)} %get-tuple-element.68) | copy-start | bytes 3538948
  413.6 7.1 %copy-start.2 = (bf16[2,256,1152]{2,1,0:T(8,128)(2,1)S(1)}, bf16[2,256,1152]{2,1,0:T(8,128)(2,1)}, u32[]{:S(2)}) copy-start(bf16[2,256,1152]{2,1,0:T(8,128)(2,1)} %get-tuple-element.45.att_ref) | copy-start | bytes 3538948
  413.6 7.1 %copy-start.16 = (bf16[2,256,1152]{2,1,0:T(8,128)(2,1)S(1)}, bf16[2,256,1152]{2,1,0:T(8,128)(2,1)}, u32[]{:S(2)}) copy-start(bf16[2,256,1152]{2,1,0:T(8,128)(2,1)} %get-tuple-element.70) | copy-start | bytes 3538948
  531.1 3.7 copy-start.1
  534.8 1.5 copy-start.6
  536.2 3.0 copy-start.10
  536.3 5.1 copy-start

commit v9 on v8

--- a/solution.py
+++ b/solution.py
@@ -139,11 +139,14 @@
     steps = [lambda: own(0)]
     for i in range(n):
         mine = [lambda i=i: zarr(i, 1)]
-        if i + 1 < n:
+        if 0 < i and i + 1 < n:
             mine.append(lambda i=i: own(i + 1))
         mine.append(lambda i=i: xarr(i, 0))
         for t in (2, 3):
-            mine += [lambda i=i, t=t: zarr(i, t), lambda i=i, t=t: xarr(i, t - 1)]
+            mine.append(lambda i=i, t=t: zarr(i, t))
+            if i == 0 and t == 3 and n > 1:
+                mine.append(lambda: own(1))
+            mine.append(lambda i=i, t=t: xarr(i, t - 1))
         mine.append(lambda i=i: xarr(i, 3))
         if i > 0:
             late = [lambda i=i, k=k: yarr(i - 1, *order[k]) for k in range(7)]
@@ -437,7 +440,7 @@
     dx_ref[0] = mid_ref[0] + root * (inner - unit * jnp.mean(inner * unit, axis=-1, keepdims=True))
 
 
-def qkv_backward(x, mod, d_mid, dq, dk, dv, nq, nk, rq, rk, qp_all, gains, tables):
+def qkv_backward(x, mod, d_mid, dq, d_kv, nq, nk, rq, rk, qp_all, gains, tables):
     images, length, width = x.shape
     row = lambda w: pl.BlockSpec((1, length, w), lambda i: (i, 0, 0))
     whole = lambda a: pl.BlockSpec(a.shape, lambda i: (0,) * a.ndim)
@@ -445,7 +448,9 @@
         qkv_back_kernel,
         grid=(images,),
         in_specs=[row(width), pl.BlockSpec((1, 6, width), lambda i: (i, 0, 0))]
-        + [row(width)] * 6
+        + [row(width)] * 2
+        + [pl.BlockSpec((None, 1, length, width), lambda i, s=s: (s, i, 0, 0)) for s in (0, 1)]
+        + [row(width)] * 2
         + [row(LANES)] * 2
         + [pl.BlockSpec((width, 3 * width), lambda i: (0, 0)), whole(gains)]
         + [whole(t) for t in tables],
@@ -457,7 +462,41 @@
         out_specs=[row(3 * width), row(width), pl.BlockSpec((1, 4, width), lambda i: (i, 0, 0))],
         compiler_params=pltpu.CompilerParams(vmem_limit_bytes=60 * 2**20),
         name="qkv_backward",
-    )(x, mod, d_mid, dq, dk, dv, nq, nk, rq, rk, qp_all, gains, *tables)
+    )(x, mod, d_mid, dq, d_kv, d_kv, nq, nk, rq, rk, qp_all, gains, *tables)
+
+
+def weight_kernel(normed_ref, att_ref, dqkv_ref, dproj_ref, out_ref, turned):
+    step = pl.program_id(0)
+
+    @pl.when(step == 0)
+    def _():
+        turned[...] = normed_ref[...].T
+
+    @pl.when(step == 3)
+    def _():
+        turned[...] = att_ref[...].T
+        out_ref[...] = jnp.dot(turned[...], dproj_ref[...], preferred_element_type=jnp.float32).astype(jnp.bfloat16)
+
+    @pl.when(step < 3)
+    def _():
+        out_ref[...] = jnp.dot(turned[...], dqkv_ref[...], preferred_element_type=jnp.float32).astype(jnp.bfloat16)
+
+
+def weight_grads(normed, attended, d_qkv, d_proj):
+    tokens, width = normed.shape
+    whole = pl.BlockSpec((tokens, width), lambda k: (0, 0))
+    return pl.pallas_call(
+        weight_kernel,
+        grid=(4,),
+        in_specs=[whole, whole, pl.BlockSpec((tokens, width), lambda k: (0, jnp.minimum(k, 2))), whole],
+        out_shape=jax.ShapeDtypeStruct((width, 4 * width), jnp.bfloat16),
+        out_specs=pl.BlockSpec((width, width), lambda k: (0, k)),
+        scratch_shapes=[pltpu.VMEM((width, tokens), jnp.bfloat16)],
+        compiler_params=pltpu.CompilerParams(vmem_limit_bytes=60 * 2**20),
+        name="weight_grads",
+    )(normed, attended, d_qkv, d_proj)
+
+
 def tail_scratch():
     s = pltpu.SemaphoreType.DMA
     wide = SMALL_COLS
@@ -472,7 +511,7 @@
 
 
 def tail_steps(at, ins, outs, scratch):
-    part_ref, ada_ref, slope_ref = ins
+    sums_ref, mid_ref, tag_ref, ada_ref, slope_ref = ins
     all_ref, cond_ref = outs
     acc, inbox, blocks, cond, ss, rs = scratch
     width = HEADS * HDIM
@@ -487,13 +526,21 @@
         src = ref.at[pl.ds(start, size)]
         return at.copy(src, src, ss.at[r], rs.at[r], line[k])
 
+    def collect():
+        acc[...] = jnp.zeros_like(acc)
+        for i in range(2):
+            acc[6 * i : 6 * i + 2, :width] = sums_ref[i, 0:2, :]
+            acc[6 * i + 2 : 6 * i + 6, :width] = mid_ref[i]
+        acc[:GAIN_ROW, width:] = tag_ref[...]
+        gains = sums_ref[0, 2:4, :] + sums_ref[1, 2:4, :]
+        acc[GAIN_ROW : GAIN_ROW + 2, :width] = gains
+        acc[GAIN_ROW + 2 :, :width] = gains
+
     def pack():
         row = lax.broadcasted_iota(jnp.int32, (SMALL_ROWS, 1), 0)
         value = acc[...]
         rest = value - value.astype(jnp.bfloat16).astype(jnp.float32)
-        last = rest - rest.astype(jnp.bfloat16).astype(jnp.float32)
-        value = jnp.where(row == GAIN_ROW + 1, rest, jnp.where(row == GAIN_ROW + 2, last, value))
-        blocks[at.g] = value.astype(jnp.bfloat16)
+        blocks[at.g] = jnp.where(row >= GAIN_ROW + 2, rest, value).astype(jnp.bfloat16)
 
     def cond_rows():
         flat = blocks[...].reshape(8 * SMALL_ROWS, SMALL_COLS)
@@ -518,7 +565,7 @@
         if r > 0:
             copy(r - 1).wait()
         if r == 0:
-            acc[...] = part_ref[...]
+            collect()
         elif r <= 2:
             acc[...] = acc[...] + inbox[r - 1]
         if r == 2:
@@ -540,10 +587,10 @@
 def scatter_kernel(n, cuts, lags, *refs):
     at = Place()
     at.greet_all()
-    ins, small_in = refs[:n], refs[n : n + 3]
-    outs, small_out = refs[n + 3 : 2 * n + 3], refs[2 * n + 3 : 2 * n + 5]
-    small = tail_steps(at, small_in, small_out, refs[2 * n + 5 : 2 * n + 11])
-    opening, steps, last = scatter_steps(at, cuts, ins, outs, refs[2 * n + 11 :], lags)
+    ins, small_in = refs[:n], refs[n : n + 5]
+    outs, small_out = refs[n + 5 : 2 * n + 5], refs[2 * n + 5 : 2 * n + 7]
+    small = tail_steps(at, small_in, small_out, refs[2 * n + 7 : 2 * n + 13])
+    opening, steps, last = scatter_steps(at, cuts, ins, outs, refs[2 * n + 13 :], lags)
     small[0]()
     for step in opening:
         step()
@@ -559,7 +606,7 @@
     at.drain(opening + steps)
 
 
-def scatter(grads, cuts, lags, part, w_ada, slope):
+def scatter(grads, cuts, lags, sums, mid_sums, tags, w_ada, slope):
     n = len(grads)
     any_ref = pl.BlockSpec(memory_space=pl.ANY)
     vmem = pl.BlockSpec(memory_space=pltpu.VMEM)
@@ -570,14 +617,14 @@
             jax.ShapeDtypeStruct((8, SMALL_ROWS, SMALL_COLS), jnp.bfloat16),
             jax.ShapeDtypeStruct((8, GROUPS, 2 * LANES), jnp.float32),
         ],
-        in_specs=[any_ref] * n + [vmem] * 3,
+        in_specs=[any_ref] * n + [vmem] * 5,
         out_specs=[any_ref] * n + [vmem] * 2,
         scratch_shapes=tail_scratch() + scatter_scratch(grads, cuts),
         compiler_params=pltpu.CompilerParams(
             collective_id=1, has_side_effects=True, vmem_limit_bytes=60 * 2**20
         ),
         name="gradient_scatter",
-    )(*grads, part, w_ada, slope)
+    )(*grads, sums, mid_sums, tags, w_ada, slope)
 
 
 def forward_kernel(cuts, cols, refs):
@@ -1139,7 +1186,6 @@
     )
     patches_out = patches_out.reshape(images, rows, cols, width)
     mod = mod.reshape(images, 6, width)
-    d_w_proj = jnp.einsum("td,te->de", flat(attended), flat(d_proj), preferred_element_type=jnp.float32).astype(bf)
     d_query, d_kv, *rest = attention_backward(
         query,
         d_attended,
@@ -1150,34 +1196,30 @@
         (2, 2, 1, 2),
     )
     d_qkv, d_x, sums = qkv_backward(
-        x, mod, d_middle, d_query, d_kv[0], d_kv[1], nq, nk, rq, rk, qp_all, gains, tables
+        x, mod, d_middle, d_query, d_kv, nq, nk, rq, rk, qp_all, gains, tables
     )
     d_patches = d_x.reshape(images, rows, cols, width)
-    d_w_qkv = jnp.einsum("td,te->de", flat(normed_one), flat(d_qkv), preferred_element_type=jnp.float32).astype(bf)
-    d_w_qp = jnp.concatenate([d_w_qkv, d_w_proj], axis=1)
-
-    d_mod_part = jnp.concatenate([sums[:, 0:2], mid_sums], axis=1)
-    gain_part = jnp.sum(sums[:, 2:4].reshape(images, 2, HEADS, HDIM), axis=(0, 2))
+    d_w_qp = weight_grads(flat(normed_one), flat(attended), flat(d_qkv), flat(d_proj))
     if fits:
-        tags = jnp.pad(jnp.repeat(onehot * (1.0 / lax.axis_size("band")), 6, axis=0), ((0, 0), (0, LANES - GROUPS)))
-        small = jnp.concatenate([d_mod_part.reshape(images * 6, width), tags], axis=1)
-        gain_row = jnp.pad(gain_part.reshape(1, -1), ((0, 0), (0, SMALL_COLS - 2 * HDIM)))
-        small = jnp.concatenate([small, gain_row, gain_row, gain_row, jnp.zeros_like(gain_row)])
+        tags = jnp.repeat(onehot * (1.0 / lax.axis_size("band")), 6, axis=0)
+        tags = jnp.pad(tags, ((0, 0), (0, LANES - GROUPS)))
         cuts = [half_cuts(0, 0, 0, w_down.shape[0], 2, 1), half_cuts(1, 1, 0, 4 * width, 8, 5)]
         d_gu = rest[0]
         d_down, d_qp, gathered, cond_blocks = scatter(
-            [by_shard(d_w_down), by_shard(d_w_qp)], cuts, (2, 1, 0, 2), small, w_ada, silu_slope
+            [by_shard(d_w_down), by_shard(d_w_qp)], cuts, (2, 1, 0, 2), sums, mid_sums, tags, w_ada, silu_slope
         )
         d_mod_all = gathered[:, :GAIN_ROW, :width].reshape(-1, ada_cols)
         onehot_all = gathered[:, 0:GAIN_ROW:6, width : width + GROUPS].reshape(-1, GROUPS)
-        gain_all = gathered[:, GAIN_ROW : GAIN_ROW + 3, : 2 * HDIM].astype(jnp.float32)
-        gain_all = jnp.sum(gain_all, axis=(0, 1)).reshape(2, HDIM)
+        gain_all = gathered[:, GAIN_ROW:, :width].astype(jnp.float32).reshape(-1, 2, 2, HEADS, HDIM)
+        gain_all = jnp.sum(gain_all, axis=(0, 1, 3))
         d_cond = jnp.swapaxes(cond_blocks[:, :, :ada_rows], 0, 1).reshape(GROUPS, -1)
     else:
         d_gu, d_down, d_qp = (
             lax.psum(lax.psum_scatter(w, "grp", scatter_dimension=w.ndim - 2, tiled=True), "band")
             for w in (d_w_gu, d_w_down, d_w_qp)
         )
+        d_mod_part = jnp.concatenate([sums[:, 0:2], mid_sums], axis=1)
+        gain_part = jnp.sum(sums[:, 2:4].reshape(images, 2, HEADS, HDIM), axis=(0, 2))
         d_modulation = lax.psum(d_mod_part.reshape(images, ada_cols), "band").astype(bf)
         gain_all = lax.psum(gain_part, ("grp", "band"))
         payload = jnp.concatenate([d_modulation, onehot.astype(bf)], axis=1)

time: 547 us -> 537 us (0.982)
  matrix products: 15.2 us -> 6.38 us
  Pallas kernels: 495 us -> 502 us
    pallas_call x0 -> x1, Pallas kernels: none -> 11.7 us  [weight_grads(): pl.pallas_call(weight_kernel, grid=(4,), in_specs=[whole, whole, pl.Block...]
    dot_general x2 -> x0, matrix products: 8.81 us -> none  [the longest x1 7.08 us: body(): jnp.einsum('td,te->de', flat(normed_one), flat(d_qkv), preferred_element_...]
where the time goes in v9:
time: 537 us; the launch traced here: 532 us
  Pallas kernels  502 us (93%)
  other arithmetic  12.9 us (2%)
  local copies, waits for them, and re-layouts  8.39 us (2%)
  matrix products  6.38 us (1%)
    pallas_call x1, Pallas kernels, forward(): pl.pallas_call(kernel, out_shape=outs + [jax.ShapeDtypeStruct(keys, bf)]...  183 us
    pallas_call x1, Pallas kernels, attention_backward(): pl.pallas_call(functools.partial(attention_back_kernel, n, cuts, lags), o...  135 us
    pallas_call x1, Pallas kernels, scatter(): pl.pallas_call(functools.partial(scatter_kernel, n, cuts, lags), out_shap...  99.1 us
    pallas_call x1, Pallas kernels, mlp_block(): pl.pallas_call(mlp_kernel, grid=(steps,), in_specs=[whole(x.shape)] * 3 +...  51.5 us
    pallas_call x1, Pallas kernels, qkv_backward(): pl.pallas_call(qkv_back_kernel, grid=(images,), in_specs=[row(width), pl....  21.6 us
    pallas_call x1, Pallas kernels, weight_grads(): pl.pallas_call(weight_kernel, grid=(4,), in_specs=[whole, whole, pl.Block...  11.7 us

profile of v9, /device:TPU:0, one launch (start us, length us, event | category | flops | bytes accessed | tf_op | source)
XLA Modules:
  0.0 532.3 jit_solution(17030212126154702183)
XLA Ops:
  0.6 0.0 copy-start.10
  0.7 0.0 copy-start.11
  0.7 0.0 copy-start.4
  0.7 0.0 copy-start.3
  0.7 0.9 convert_dynamic-update-slice_fusion
  1.6 2.7 convolution_add_fusion.refs_1_
  4.3 0.0 copy-done.10
  4.3 0.1 stack_tile.6
  4.4 0.0 copy-done.11
  4.4 0.1 stack_tile.7
  4.5 0.6 pad_maximum_fusion.2.refs_3_.gains_ref
  5.2 0.0 copy-done.4
  5.2 0.0 copy-done.3
  5.2 1.3 pad_maximum_fusion.refs_6_
  6.5 0.2 copy-done.2
  6.7 0.3 copy-done.6
  7.1 1.2 pad_maximum_fusion.1.refs_5_
  8.2 0.6 pad_convert_fusion.refs_2_
  9.5 0.5 broadcast_in_dim.9.refs_4_
  10.0 183.0 %forward.1 = (bf16[2,256,1152]{2,1,0:T(8,128)(2,1)}, bf16[2,256,1152]{2,1,0:T(8,128)(2,1)}, f32[2,256,1152]{2,1,0:T(8,128)}, f32[2,256,1152]{2,1,0:T(8,128)}, f3...) custom-call(bf16[2,256,1152]{2,1,0:T(8,128)(2,1)} %bitcast.42, ...), custom_call_target="tpu_custom_call" | custom-call | tf_op jit(solution)/shard_map/forward/pallas_call | solution.py:850
  193.7 0.6 broadcast_in_dim.10.live_ref
  194.3 51.5 %mlp_block.1 = (bf16[2,256,1152]{2,1,0:T(8,128)(2,1)}, f32[2,256,1152]{2,1,0:T(8,128)}, bf16[2,256,1152]{2,1,0:T(8,128)(2,1)}, bf16[2,256,1152]{2,1,0:T(8,128)(2...) custom-call(bf16[2,256,1152]{2,1,0:T(8,128)(2,1)} %bitcast.43, ...), custom_call_target="tpu_custom_call" | custom-call | tf_op jit(solution)/shard_map/mlp_block/pallas_call | solution.py:1078
  245.8 0.8 copy.32
  246.7 135.5 %attention_backward.1 = (f32[2,256,1152]{2,1,0:T(8,128)}, bf16[2,2,256,1152]{3,2,1,0:T(8,128)(2,1)}, bf16[2,144,3072]{2,1,0:T(8,128)(2,1)}) custom-call(bf16[2,256,1152]{2,1,0:T(8,128)(2,1)} %get-tuple-element.52.q_ref, bf16[2,256,1152]{2,1,0:T(8,128)(2,1)} %get-tuple-element.53.do_ref, f32[2,128,256]{2,1,0:T(8,128)} %bitcast.52, ...), custom_call_target="tpu_custom_call" | custom-call | tf_op jit(solution)/shard_map/attention_backward/pallas_call | solution.py:973
  382.1 0.7 reshape.109.mod_ref
  382.8 21.6 %qkv_backward.1 = (bf16[2,256,3456]{2,1,0:T(8,128)(2,1)}, f32[2,256,1152]{2,1,0:T(8,128)}, f32[2,4,1152]{2,1,0:T(4,128)}) custom-call(bf16[2,256,1152]{2,1,0:T(8,128)(2,1)} %bitcast.44, f32[2,6,1152]{2,1,0:T(8,128)} %reshape.109.mod_ref, f32[2,256,1152]{2,1,0:T(8,128)} %get-tuple-element.51.mid_ref, f32[2,256,1152]{2,1,0:T(8,128)} %get-tuple-element.57.dq_ref, ...), custom_call_target="tpu_custom_call" | custom-call | tf_op jit(solution)/shard_map/qkv_backward/pallas_call | solution.py:447
  404.4 11.7 %weight_grads.1 = bf16[1152,4608]{1,0:T(8,128)(2,1)} custom-call(bf16[512,1152]{1,0:T(8,128)(2,1)} %bitcast.50, bf16[512,1152]{1,0:T(8,128)(2,1)} %bitcast.47, bf16[512,3456]{1,0:T(8,128)(2,1)} %bitcast.48, bf16[512,1152]{1,0:T(8,128)(2,1)} %bitcast.51), custom_call_target="tpu_custom_call" | custom-call | tf_op jit(solution)/shard_map/weight_grads/pallas_call | solution.py:488
  416.1 1.4 add_multiply_fusion.refs_6_
  417.5 0.1 broadcast_in_dim.11
  417.6 0.1 reshape.118
  417.6 0.1 copy.33
  417.7 0.6 pad.12.refs_4_
  418.3 99.1 %gradient_scatter.1 = (bf16[384,1152]{1,0:T(8,128)(2,1)}, bf16[144,4608]{1,0:T(8,128)(2,1)}, bf16[8,16,1280]{2,1,0:T(8,128)(2,1)}, f32[8,8,256]{2,1,0:T(8,128)}) custom-call(bf16[8,384,1152]{2,1,0:T(8,128)(2,1)} %bitcast.46, bf16[8,144,4608]{2,1,0:T(8,128)(2,1)} %bitcast.38, f32[2,4,1152]{2,1,0:T(4,128)} %get-tuple-element.71.refs_2_, ...), custom_call_target="tpu_custom_call" | custom-call | tf_op jit(solution)/shard_map/gradient_scatter/pallas_call | solution.py:613
  517.4 1.0 slice.32
  518.4 0.3 reshape.121
  518.7 0.8 slice.31
  519.5 3.7 fusion
  523.2 1.4 slice_convert_fusion
  524.6 0.0 copy-done.5
  524.6 1.3 convert_element_type.65
  525.9 0.9 slice_convert_fusion.1
  526.8 0.1 convert_reduce_fusion
  526.9 0.7 dynamic_slice.7
  527.6 0.7 reshape.119
  528.3 1.0 convert_reduce_fusion.1
  529.3 0.1 reduce_sum.27
  529.4 0.5 slice_bitcast_fusion.1
  529.9 2.2 bitcast_convert_fusion
  (24 shorter events, 0.1 us)
Async XLA Ops:
  0.6 3.7 copy-start.10
  0.7 3.8 copy-start.11
  0.7 4.5 copy-start.4
  0.7 4.5 copy-start.3
  5.2 1.6 copy-start.2
  5.2 1.9 copy-start.6
  7.0 1.2 copy-start.12
  194.3 51.5 %copy-start.7 = (f32[2,256,128]{2,1,0:T(8,128)S(1)}, f32[2,256,128]{2,1,0:T(8,128)}, u32[]{:S(2)}) copy-start(f32[2,256,128]{2,1,0:T(8,128)} %get-tuple-element.54) | copy-start | bytes 786436
  246.7 135.5 %copy-start.8 = (f32[2,6912]{1,0:T(2,128)S(1)}, f32[2,6912]{1,0:T(2,128)}, u32[]{:S(2)}) copy-start(f32[2,6912]{1,0:T(2,128)} %get-tuple-element.46.mod_ref) | copy-start | bytes 165892
  519.5 3.7 copy-start.1
  523.2 1.5 copy-start.5
  524.6 3.0 copy-start.9
  524.6 5.3 copy-start

commit v10 on v9

--- a/solution.py
+++ b/solution.py
@@ -415,9 +415,11 @@
 def qkv_back_kernel(
     x_ref, mod_ref, mid_ref, dq_ref, dk_ref, dv_ref, nq_ref, nk_ref, rq_ref, rk_ref, w_ref,
     gains_ref, cos_ref, next_ref, prev_ref,
-    dqkv_ref, dx_ref, sums_ref,
+    dqkv_ref, dx_ref, sums_ref, w_buf, w_sem,
 ):
     width = x_ref.shape[-1]
+    load = pltpu.make_async_copy(w_ref.at[:, pl.ds(0, 3 * width)], w_buf, w_sem)
+    pl.when(pl.program_id(0) == 0)(load.start)
     tables = (cos_ref[...], next_ref[...], prev_ref[...])
     pick, spread = head_pick(width), head_spread(width)
     ins = ((dq_ref, nq_ref, rq_ref), (dk_ref, nk_ref, rk_ref))
@@ -430,7 +432,8 @@
         grad = (inner - unit * pick_dot(mean, spread)) * pick_dot(r_ref[0], spread)
         dqkv_ref[0, :, part * width : (part + 1) * width] = grad.astype(jnp.bfloat16)
     dqkv_ref[0, :, 2 * width : 3 * width] = dv_ref[0]
-    d_normed = dot_t(dqkv_ref[0], w_ref[...])
+    pl.when(pl.program_id(0) == 0)(load.wait)
+    d_normed = dot_t(dqkv_ref[0], w_buf[...])
     x = x_ref[0].astype(jnp.float32)
     root = lax.rsqrt(jnp.mean(x * x, axis=-1, keepdims=True) + EPS)
     unit = x * root
@@ -452,7 +455,7 @@
         + [pl.BlockSpec((None, 1, length, width), lambda i, s=s: (s, i, 0, 0)) for s in (0, 1)]
         + [row(width)] * 2
         + [row(LANES)] * 2
-        + [pl.BlockSpec((width, 3 * width), lambda i: (0, 0)), whole(gains)]
+        + [pl.BlockSpec(memory_space=pl.ANY), whole(gains)]
         + [whole(t) for t in tables],
         out_shape=[
             jax.ShapeDtypeStruct((images, length, 3 * width), jnp.bfloat16),
@@ -460,6 +463,7 @@
             jax.ShapeDtypeStruct((images, 4, width), jnp.float32),
         ],
         out_specs=[row(3 * width), row(width), pl.BlockSpec((1, 4, width), lambda i: (i, 0, 0))],
+        scratch_shapes=[pltpu.VMEM((width, 3 * width), jnp.bfloat16), pltpu.SemaphoreType.DMA],
         compiler_params=pltpu.CompilerParams(vmem_limit_bytes=60 * 2**20),
         name="qkv_backward",
     )(x, mod, d_mid, dq, d_kv, d_kv, nq, nk, rq, rk, qp_all, gains, *tables)
@@ -631,7 +635,7 @@
     n = len(cuts)
     soon = sum(cut[5] == 0 for cut in cuts)
     at = Place()
-    x_ref, part_ref, group_ref, gains_ref, band_ref = refs["in"]
+    x_ref, *part_refs, group_ref, gains_ref, band_ref = refs["in"]
     normed_ref, q_ref, nq_ref, nk_ref, rq_ref, rk_ref, o_ref, inv_ref, mod_ref, *table_refs, kv_out = refs["out"]
     kv, w_buf, pick_ref, spread_ref, mod_buf, mod_in, w_sem, ms, mr, ks, kr, os = refs["scratch"]
     ins, outs = refs["shards"], refs["full"]
@@ -644,7 +648,12 @@
         at.greet_band()
         steps, first, last = [], 0, None
 
-    mod_buf[...] = part_ref[...]
+    if n:
+        silu_ref, ada_ref, bias_ref = part_refs
+        silu = silu_ref[...].astype(jnp.bfloat16)
+        mod_buf[...] = jnp.dot(silu, ada_ref[...], preferred_element_type=jnp.float32) + bias_ref[...]
+    else:
+        mod_buf[...] = part_refs[0][...]
 
     def mod_copy(r):
         peer = (at.xpeer, at.line(at.far[1]), at.line((at.z + 2) % 4))[r]
@@ -808,7 +817,7 @@
         at.drain([functools.partial(ready, i)])
 
 
-def forward(x, mod_part, groups, gains, band, cols, shards, cuts):
+def forward(x, mod_parts, groups, gains, band, cols, shards, cuts):
     n = len(cuts)
     images, length, width = x.shape
     bands = lax.axis_size("band")
@@ -817,18 +826,19 @@
     bf = jnp.bfloat16
     any_ref = pl.BlockSpec(memory_space=pl.ANY)
     vmem = pl.BlockSpec(memory_space=pltpu.VMEM)
-    args = [x, mod_part, groups, gains, band]
+    args = [x, *mod_parts, groups, gains, band]
+    table = (GROUPS, mod_parts[-1].shape[1])
     rows = lambda w, d: jax.ShapeDtypeStruct((images, length, w), d)
     outs = [rows(width, bf)] * 2 + [rows(width, jnp.float32)] * 2 + [rows(LANES, jnp.float32)] * 2
-    outs += [rows(width, bf), rows(LANES, jnp.float32), jax.ShapeDtypeStruct((images, mod_part.shape[1]), jnp.float32)]
+    outs += [rows(width, bf), rows(LANES, jnp.float32), jax.ShapeDtypeStruct((images, table[1]), jnp.float32)]
     outs += [jax.ShapeDtypeStruct((length, width), jnp.float32)] * 3
     scratch = [
         pltpu.VMEM(keys, bf),
         pltpu.VMEM((width, 3 * width), bf),
         pltpu.VMEM((width, LANES), bf),
         pltpu.VMEM((LANES, width), bf),
-        pltpu.VMEM(mod_part.shape, jnp.float32),
-        pltpu.VMEM((3,) + mod_part.shape, jnp.float32),
+        pltpu.VMEM(table, jnp.float32),
+        pltpu.VMEM((3,) + table, jnp.float32),
         s((8,)),
         s((3,)),
         s((3,)),
@@ -952,7 +962,7 @@
             head(i, h)
             return 0
 
-        lax.fori_loop(0, HEADS, body, 0, unroll=2)
+        lax.fori_loop(0, HEADS, body, 0, unroll=4)
         to_core(i)
         steps += [functools.partial(to_core, i)] + exchange
     exchange[0]()
@@ -1154,11 +1164,10 @@
     sigmoid = jax.nn.sigmoid(cond_rows)
     silu_rows = (cond_rows * sigmoid).astype(bf)
     silu_slope = sigmoid * (1.0 + cond_rows * (1.0 - sigmoid))
-    mod_part = jnp.dot(silu_rows, w_ada, preferred_element_type=jnp.float32)
     bias_part = lax.dynamic_update_slice_in_dim(
         jnp.zeros((ada_cols,), jnp.float32), b_ada.astype(jnp.float32), grp * bias_cols, axis=0
     )
-    mod_part = mod_part + bias_part[None, :]
+    mod_parts = (silu_rows.astype(jnp.float32), w_ada, bias_part[None, :])
     live_mask = (jnp.arange(images, dtype=jnp.int32) < live_count[0]).astype(jnp.float32)
 
     gains = jnp.stack([jnp.tile(q_gain, HEADS), jnp.tile(k_gain, HEADS)])
@@ -1172,9 +1181,10 @@
         cuts += [half_cuts(2, 0, 0, w_down.shape[0], 4, 1)]
     else:
         qp_all, gu_all, down_all = (lax.all_gather(w, "grp", axis=0, tiled=True) for w in (w_qp, w_gu, w_down))
-        mod_part = lax.psum(mod_part, "grp")
+        mod_part = jnp.dot(silu_rows, w_ada, preferred_element_type=jnp.float32) + bias_part[None, :]
+        mod_parts = (lax.psum(mod_part, "grp"),)
         shards, cuts = [qp_all], []
-    outs = forward(x, mod_part, *common, shards, cuts)
+    outs = forward(x, mod_parts, *common, shards, cuts)
     normed_one, query, nq, nk, rq, rk, attended, inv, mod = outs[:9]
     tables, kv_all, rest = outs[9:12], outs[12], outs[13:]
     if fits:
@@ -1192,7 +1202,7 @@
         jnp.swapaxes(inv, 1, 2),
         kv_all,
         [d_w_gu.reshape(2, -1, w_gate.shape[0], ff)] if fits else [],
-        [half_cuts(0, 1, None, 2 * ff, 4, 1)] if fits else [],
+        [half_cuts(0, 1, None, 2 * ff, 6, 1)] if fits else [],
         (2, 2, 1, 2),
     )
     d_qkv, d_x, sums = qkv_backward(

time: 537 us -> 534 us (level); the launches traced: 532 us -> 524 us
  Pallas kernels: 502 us -> 494 us
    pallas_call x1, Pallas kernels: 135 us -> 129 us  [attention_backward(): pl.pallas_call(functools.partial(attention_back_kernel, n, cuts, lags), o...]
where the time goes in v10:
time: 534 us; the launch traced here: 524 us
  Pallas kernels  494 us (93%)
  other arithmetic  13.6 us (3%)
  local copies, waits for them, and re-layouts  10 us (2%)
    pallas_call x1, Pallas kernels, forward(): pl.pallas_call(kernel, out_shape=outs + [jax.ShapeDtypeStruct(keys, bf)]...  184 us
    pallas_call x1, Pallas kernels, attention_backward(): pl.pallas_call(functools.partial(attention_back_kernel, n, cuts, lags), o...  129 us
    pallas_call x1, Pallas kernels, scatter(): pl.pallas_call(functools.partial(scatter_kernel, n, cuts, lags), out_shap...  97 us
    pallas_call x1, Pallas kernels, mlp_block(): pl.pallas_call(mlp_kernel, grid=(steps,), in_specs=[whole(x.shape)] * 3 +...  51.5 us
    pallas_call x1, Pallas kernels, qkv_backward(): pl.pallas_call(qkv_back_kernel, grid=(images,), in_specs=[row(width), pl....  21.1 us
    pallas_call x1, Pallas kernels, weight_grads(): pl.pallas_call(weight_kernel, grid=(4,), in_specs=[whole, whole, pl.Block...  11.7 us

profile of v10, /device:TPU:0, one launch (start us, length us, event | category | flops | bytes accessed | tf_op | source)
XLA Modules:
  0.0 523.9 jit_solution(2197384062748964109)
XLA Ops:
  0.6 1.4 add_multiply_fusion
  2.1 0.7 reshape.120
  2.8 0.2 dynamic_update_slice.4.refs_3_
  2.9 0.0 copy-start.7
  3.0 0.7 tile.4
  3.6 0.1 stack_tile.6
  3.7 0.7 tile.5
  4.4 0.1 stack_tile.7
  4.5 0.6 pad_maximum_fusion.2.refs_5_.gains_ref
  5.1 2.9 pad_maximum_fusion.refs_8_
  8.0 0.0 copy-done.7
  8.0 0.0 copy-done.2
  8.0 0.0 copy-done.4
  8.0 0.0 copy-start.9
  8.0 1.2 pad_maximum_fusion.1.refs_7_
  9.1 0.0 copy-done.9
  9.2 0.6 pad_convert_fusion.refs_4_
  10.4 0.5 broadcast_in_dim.31.refs_6_
  10.9 183.7 %forward.1 = (bf16[2,256,1152]{2,1,0:T(8,128)(2,1)}, bf16[2,256,1152]{2,1,0:T(8,128)(2,1)}, f32[2,256,1152]{2,1,0:T(8,128)}, f32[2,256,1152]{2,1,0:T(8,128)}, f3...) custom-call(bf16[2,256,1152]{2,1,0:T(8,128)(2,1)} %bitcast.41, ...), custom_call_target="tpu_custom_call" | custom-call | tf_op jit(solution)/shard_map/forward/pallas_call | solution.py:860
  195.3 0.6 broadcast_in_dim.32.live_ref
  195.9 51.5 %mlp_block.1 = (bf16[2,256,1152]{2,1,0:T(8,128)(2,1)}, f32[2,256,1152]{2,1,0:T(8,128)}, bf16[2,256,1152]{2,1,0:T(8,128)(2,1)}, bf16[2,256,1152]{2,1,0:T(8,128)(2...) custom-call(bf16[2,256,1152]{2,1,0:T(8,128)(2,1)} %bitcast.42, ...), custom_call_target="tpu_custom_call" | custom-call | tf_op jit(solution)/shard_map/mlp_block/pallas_call | solution.py:1088
  247.4 0.0 copy-done.5
  247.5 0.8 copy.32
  248.3 129.3 %attention_backward.1 = (f32[2,256,1152]{2,1,0:T(8,128)}, bf16[2,2,256,1152]{3,2,1,0:T(8,128)(2,1)}, bf16[2,144,3072]{2,1,0:T(8,128)(2,1)}) custom-call(bf16[2,256,1152]{2,1,0:T(8,128)(2,1)} %get-tuple-element.52.q_ref, bf16[2,256,1152]{2,1,0:T(8,128)(2,1)} %get-tuple-element.53.do_ref, f32[2,128,256]{2,1,0:T(8,128)} %bitcast.51, ...), custom_call_target="tpu_custom_call" | custom-call | tf_op jit(solution)/shard_map/attention_backward/pallas_call | solution.py:983
  377.6 0.0 copy-done.6
  377.6 0.7 reshape.107.mod_ref
  378.2 21.1 %qkv_backward.1 = (bf16[2,256,3456]{2,1,0:T(8,128)(2,1)}, f32[2,256,1152]{2,1,0:T(8,128)}, f32[2,4,1152]{2,1,0:T(4,128)}) custom-call(bf16[2,256,1152]{2,1,0:T(8,128)(2,1)} %bitcast.43, f32[2,6,1152]{2,1,0:T(8,128)} %reshape.107.mod_ref, f32[2,256,1152]{2,1,0:T(8,128)} %get-tuple-element.51.mid_ref, f32[2,256,1152]{2,1,0:T(8,128)} %get-tuple-element.57.dq_ref, ...), custom_call_target="tpu_custom_call" | custom-call | tf_op jit(solution)/shard_map/qkv_backward/pallas_call | solution.py:450
  399.3 11.7 %weight_grads.1 = bf16[1152,4608]{1,0:T(8,128)(2,1)} custom-call(bf16[512,1152]{1,0:T(8,128)(2,1)} %bitcast.49, bf16[512,1152]{1,0:T(8,128)(2,1)} %bitcast.46, bf16[512,3456]{1,0:T(8,128)(2,1)} %bitcast.47, bf16[512,1152]{1,0:T(8,128)(2,1)} %bitcast.50), custom_call_target="tpu_custom_call" | custom-call | tf_op jit(solution)/shard_map/weight_grads/pallas_call | solution.py:492
  411.0 0.1 broadcast_in_dim.33
  411.1 0.1 reshape.116
  411.1 0.1 copy.33
  411.2 0.6 pad.12.refs_4_
  411.8 97.0 %gradient_scatter.1 = (bf16[384,1152]{1,0:T(8,128)(2,1)}, bf16[144,4608]{1,0:T(8,128)(2,1)}, bf16[8,16,1280]{2,1,0:T(8,128)(2,1)}, f32[8,8,256]{2,1,0:T(8,128)}) custom-call(bf16[8,384,1152]{2,1,0:T(8,128)(2,1)} %bitcast.45, bf16[8,144,4608]{2,1,0:T(8,128)(2,1)} %bitcast.37, f32[2,4,1152]{2,1,0:T(4,128)} %get-tuple-element.71.refs_2_, ...), custom_call_target="tpu_custom_call" | custom-call | tf_op jit(solution)/shard_map/gradient_scatter/pallas_call | solution.py:617
  508.8 1.0 slice.32
  509.8 0.3 reshape.119
  510.1 0.8 slice.31
  510.9 3.7 fusion
  514.6 1.4 slice_convert_fusion
  516.0 0.0 copy-done.3
  516.0 1.3 convert_element_type.66
  517.3 0.9 slice_convert_fusion.1
  518.2 0.1 convert_reduce_fusion
  518.3 0.7 dynamic_slice.7
  519.0 0.7 reshape.117
  519.7 1.0 convert_reduce_fusion.1
  520.7 0.1 reduce_sum.27
  520.8 0.5 slice_bitcast_fusion.1
  521.3 2.2 bitcast_convert_fusion
  (18 shorter events, 0.1 us)
Async XLA Ops:
  2.9 5.0 copy-start.7
  5.1 2.9 copy-start.2
  5.1 2.9 copy-start.4
  8.0 1.2 copy-start.9
  195.9 51.5 %copy-start.5 = (f32[2,256,128]{2,1,0:T(8,128)S(1)}, f32[2,256,128]{2,1,0:T(8,128)}, u32[]{:S(2)}) copy-start(f32[2,256,128]{2,1,0:T(8,128)} %get-tuple-element.54) | copy-start | bytes 786436
  248.3 129.3 %copy-start.6 = (f32[2,6912]{1,0:T(2,128)S(1)}, f32[2,6912]{1,0:T(2,128)}, u32[]{:S(2)}) copy-start(f32[2,6912]{1,0:T(2,128)} %get-tuple-element.46.mod_ref) | copy-start | bytes 165892
  510.9 3.7 copy-start.1
  514.6 1.5 copy-start.3
  516.0 3.0 copy-start.8
  516.0 5.3 %copy-start = (bf16[2,144,3072]{2,1,0:T(8,128)(2,1)S(1)}, bf16[2,144,3072]{2,1,0:T(8,128)(2,1)}, u32[]{:S(2)}) copy-start(bf16[2,144,3072]{2,1,0:T(8,128)(2,1)} %get-tuple-element.76) | copy-start | bytes 5308420

commit v11 on v9

--- a/solution.py
+++ b/solution.py
@@ -415,9 +415,11 @@
 def qkv_back_kernel(
     x_ref, mod_ref, mid_ref, dq_ref, dk_ref, dv_ref, nq_ref, nk_ref, rq_ref, rk_ref, w_ref,
     gains_ref, cos_ref, next_ref, prev_ref,
-    dqkv_ref, dx_ref, sums_ref,
+    dqkv_ref, dx_ref, sums_ref, w_buf, w_sem,
 ):
     width = x_ref.shape[-1]
+    load = pltpu.make_async_copy(w_ref.at[:, pl.ds(0, 3 * width)], w_buf, w_sem)
+    pl.when(pl.program_id(0) == 0)(load.start)
     tables = (cos_ref[...], next_ref[...], prev_ref[...])
     pick, spread = head_pick(width), head_spread(width)
     ins = ((dq_ref, nq_ref, rq_ref), (dk_ref, nk_ref, rk_ref))
@@ -430,7 +432,8 @@
         grad = (inner - unit * pick_dot(mean, spread)) * pick_dot(r_ref[0], spread)
         dqkv_ref[0, :, part * width : (part + 1) * width] = grad.astype(jnp.bfloat16)
     dqkv_ref[0, :, 2 * width : 3 * width] = dv_ref[0]
-    d_normed = dot_t(dqkv_ref[0], w_ref[...])
+    pl.when(pl.program_id(0) == 0)(load.wait)
+    d_normed = dot_t(dqkv_ref[0], w_buf[...])
     x = x_ref[0].astype(jnp.float32)
     root = lax.rsqrt(jnp.mean(x * x, axis=-1, keepdims=True) + EPS)
     unit = x * root
@@ -452,7 +455,7 @@
         + [pl.BlockSpec((None, 1, length, width), lambda i, s=s: (s, i, 0, 0)) for s in (0, 1)]
         + [row(width)] * 2
         + [row(LANES)] * 2
-        + [pl.BlockSpec((width, 3 * width), lambda i: (0, 0)), whole(gains)]
+        + [pl.BlockSpec(memory_space=pl.ANY), whole(gains)]
         + [whole(t) for t in tables],
         out_shape=[
             jax.ShapeDtypeStruct((images, length, 3 * width), jnp.bfloat16),
@@ -460,6 +463,7 @@
             jax.ShapeDtypeStruct((images, 4, width), jnp.float32),
         ],
         out_specs=[row(3 * width), row(width), pl.BlockSpec((1, 4, width), lambda i: (i, 0, 0))],
+        scratch_shapes=[pltpu.VMEM((width, 3 * width), jnp.bfloat16), pltpu.SemaphoreType.DMA],
         compiler_params=pltpu.CompilerParams(vmem_limit_bytes=60 * 2**20),
         name="qkv_backward",
     )(x, mod, d_mid, dq, d_kv, d_kv, nq, nk, rq, rk, qp_all, gains, *tables)
@@ -952,7 +956,7 @@
             head(i, h)
             return 0
 
-        lax.fori_loop(0, HEADS, body, 0, unroll=2)
+        lax.fori_loop(0, HEADS, body, 0, unroll=4)
         to_core(i)
         steps += [functools.partial(to_core, i)] + exchange
     exchange[0]()
@@ -1192,7 +1196,7 @@
         jnp.swapaxes(inv, 1, 2),
         kv_all,
         [d_w_gu.reshape(2, -1, w_gate.shape[0], ff)] if fits else [],
-        [half_cuts(0, 1, None, 2 * ff, 4, 1)] if fits else [],
+        [half_cuts(0, 1, None, 2 * ff, 6, 1)] if fits else [],
         (2, 2, 1, 2),
     )
     d_qkv, d_x, sums = qkv_backward(

time: 537 us -> 534 us (level)
  Pallas kernels: 502 us -> 494 us
    pallas_call x1, Pallas kernels: 135 us -> 129 us  [attention_backward(): pl.pallas_call(functools.partial(attention_back_kernel, n, cuts, lags), o...]
where the time goes in v11:
time: 534 us; the launch traced here: 524 us
  Pallas kernels  494 us (93%)
  other arithmetic  12.9 us (2%)
  local copies, waits for them, and re-layouts  8.39 us (2%)
  matrix products  6.37 us (1%)
    pallas_call x1, Pallas kernels, forward(): pl.pallas_call(kernel, out_shape=outs + [jax.ShapeDtypeStruct(keys, bf)]...  183 us
    pallas_call x1, Pallas kernels, attention_backward(): pl.pallas_call(functools.partial(attention_back_kernel, n, cuts, lags), o...  129 us
    pallas_call x1, Pallas kernels, scatter(): pl.pallas_call(functools.partial(scatter_kernel, n, cuts, lags), out_shap...  97.9 us
    pallas_call x1, Pallas kernels, mlp_block(): pl.pallas_call(mlp_kernel, grid=(steps,), in_specs=[whole(x.shape)] * 3 +...  51.5 us
    pallas_call x1, Pallas kernels, qkv_backward(): pl.pallas_call(qkv_back_kernel, grid=(images,), in_specs=[row(width), pl....  21.1 us
    pallas_call x1, Pallas kernels, weight_grads(): pl.pallas_call(weight_kernel, grid=(4,), in_specs=[whole, whole, pl.Block...  11.7 us

profile of v11, /device:TPU:0, one launch (start us, length us, event | category | flops | bytes accessed | tf_op | source)
XLA Modules:
  0.0 524.0 jit_solution(8370579442852067355)
XLA Ops:
  0.6 0.0 copy-start.10
  0.7 0.0 copy-start.11
  0.7 0.0 copy-start.4
  0.7 0.0 copy-start.3
  0.7 0.9 convert_dynamic-update-slice_fusion
  1.6 2.7 convolution_add_fusion.refs_1_
  4.3 0.0 copy-done.10
  4.3 0.1 stack_tile.6
  4.4 0.0 copy-done.11
  4.4 0.1 stack_tile.7
  4.5 0.6 pad_maximum_fusion.2.refs_3_.gains_ref
  5.2 1.3 pad_maximum_fusion.refs_6_
  6.5 0.2 copy-done.2
  6.7 0.3 copy-done.6
  7.1 1.2 pad_maximum_fusion.1.refs_5_
  8.2 0.6 pad_convert_fusion.refs_2_
  9.5 0.5 broadcast_in_dim.9.refs_4_
  10.0 183.1 %forward.1 = (bf16[2,256,1152]{2,1,0:T(8,128)(2,1)}, bf16[2,256,1152]{2,1,0:T(8,128)(2,1)}, f32[2,256,1152]{2,1,0:T(8,128)}, f32[2,256,1152]{2,1,0:T(8,128)}, f3...) custom-call(bf16[2,256,1152]{2,1,0:T(8,128)(2,1)} %bitcast.42, ...), custom_call_target="tpu_custom_call" | custom-call | tf_op jit(solution)/shard_map/forward/pallas_call | solution.py:854
  193.8 0.6 broadcast_in_dim.10.live_ref
  194.4 51.5 %mlp_block.1 = (bf16[2,256,1152]{2,1,0:T(8,128)(2,1)}, f32[2,256,1152]{2,1,0:T(8,128)}, bf16[2,256,1152]{2,1,0:T(8,128)(2,1)}, bf16[2,256,1152]{2,1,0:T(8,128)(2...) custom-call(bf16[2,256,1152]{2,1,0:T(8,128)(2,1)} %bitcast.43, ...), custom_call_target="tpu_custom_call" | custom-call | tf_op jit(solution)/shard_map/mlp_block/pallas_call | solution.py:1082
  245.9 0.8 copy.32
  246.7 128.5 %attention_backward.1 = (f32[2,256,1152]{2,1,0:T(8,128)}, bf16[2,2,256,1152]{3,2,1,0:T(8,128)(2,1)}, bf16[2,144,3072]{2,1,0:T(8,128)(2,1)}) custom-call(bf16[2,256,1152]{2,1,0:T(8,128)(2,1)} %get-tuple-element.52.q_ref, bf16[2,256,1152]{2,1,0:T(8,128)(2,1)} %get-tuple-element.53.do_ref, f32[2,128,256]{2,1,0:T(8,128)} %bitcast.52, ...), custom_call_target="tpu_custom_call" | custom-call | tf_op jit(solution)/shard_map/attention_backward/pallas_call | solution.py:977
  375.3 0.0 copy-done.8
  375.3 0.7 reshape.109.mod_ref
  376.0 21.1 %qkv_backward.1 = (bf16[2,256,3456]{2,1,0:T(8,128)(2,1)}, f32[2,256,1152]{2,1,0:T(8,128)}, f32[2,4,1152]{2,1,0:T(4,128)}) custom-call(bf16[2,256,1152]{2,1,0:T(8,128)(2,1)} %bitcast.44, f32[2,6,1152]{2,1,0:T(8,128)} %reshape.109.mod_ref, f32[2,256,1152]{2,1,0:T(8,128)} %get-tuple-element.51.mid_ref, f32[2,256,1152]{2,1,0:T(8,128)} %get-tuple-element.57.dq_ref, ...), custom_call_target="tpu_custom_call" | custom-call | tf_op jit(solution)/shard_map/qkv_backward/pallas_call | solution.py:450
  397.0 11.7 %weight_grads.1 = bf16[1152,4608]{1,0:T(8,128)(2,1)} custom-call(bf16[512,1152]{1,0:T(8,128)(2,1)} %bitcast.50, bf16[512,1152]{1,0:T(8,128)(2,1)} %bitcast.47, bf16[512,3456]{1,0:T(8,128)(2,1)} %bitcast.48, bf16[512,1152]{1,0:T(8,128)(2,1)} %bitcast.51), custom_call_target="tpu_custom_call" | custom-call | tf_op jit(solution)/shard_map/weight_grads/pallas_call | solution.py:492
  408.7 1.4 add_multiply_fusion.refs_6_
  410.1 0.1 broadcast_in_dim.11
  410.2 0.1 reshape.118
  410.3 0.1 copy.33
  410.4 0.6 pad.12.refs_4_
  411.0 97.9 %gradient_scatter.1 = (bf16[384,1152]{1,0:T(8,128)(2,1)}, bf16[144,4608]{1,0:T(8,128)(2,1)}, bf16[8,16,1280]{2,1,0:T(8,128)(2,1)}, f32[8,8,256]{2,1,0:T(8,128)}) custom-call(bf16[8,384,1152]{2,1,0:T(8,128)(2,1)} %bitcast.46, bf16[8,144,4608]{2,1,0:T(8,128)(2,1)} %bitcast.38, f32[2,4,1152]{2,1,0:T(4,128)} %get-tuple-element.71.refs_2_, ...), custom_call_target="tpu_custom_call" | custom-call | tf_op jit(solution)/shard_map/gradient_scatter/pallas_call | solution.py:617
  508.9 1.0 slice.32
  509.9 0.3 reshape.121
  510.2 0.8 slice.31
  511.0 3.7 fusion
  514.7 1.4 slice_convert_fusion
  516.1 0.0 copy-done.5
  516.1 1.3 convert_element_type.65
  517.4 0.9 slice_convert_fusion.1
  518.3 0.1 convert_reduce_fusion
  518.4 0.7 dynamic_slice.7
  519.1 0.7 reshape.119
  519.8 1.0 convert_reduce_fusion.1
  520.8 0.1 reduce_sum.27
  520.9 0.5 slice_bitcast_fusion.1
  521.4 0.0 copy-done
  521.4 2.2 bitcast_convert_fusion
  (24 shorter events, 0.1 us)
Async XLA Ops:
  0.6 3.7 copy-start.10
  0.7 3.8 copy-start.11
  0.7 4.5 copy-start.4
  0.7 4.5 copy-start.3
  5.2 1.6 copy-start.2
  5.2 1.9 copy-start.6
  7.0 1.2 copy-start.12
  194.4 51.5 %copy-start.7 = (f32[2,256,128]{2,1,0:T(8,128)S(1)}, f32[2,256,128]{2,1,0:T(8,128)}, u32[]{:S(2)}) copy-start(f32[2,256,128]{2,1,0:T(8,128)} %get-tuple-element.54) | copy-start | bytes 786436
  246.7 128.6 %copy-start.8 = (f32[2,6912]{1,0:T(2,128)S(1)}, f32[2,6912]{1,0:T(2,128)}, u32[]{:S(2)}) copy-start(f32[2,6912]{1,0:T(2,128)} %get-tuple-element.46.mod_ref) | copy-start | bytes 165892
  511.0 3.7 copy-start.1
  514.7 1.5 copy-start.5
  516.1 3.0 copy-start.9
  516.1 5.3 %copy-start = (bf16[2,144,3072]{2,1,0:T(8,128)(2,1)S(1)}, bf16[2,144,3072]{2,1,0:T(8,128)(2,1)}, u32[]{:S(2)}) copy-start(bf16[2,144,3072]{2,1,0:T(8,128)(2,1)} %get-tuple-element.76) | copy-start | bytes 5308420
